TPU v7x, 256 devices: a whole 4x4x8 slice. The times are simulated.
256 devices in a mesh: row: 32 (over y, z), col: 8 (over x, core).
Axes of the slice: x: 4, y: 4, z: 8, core: 2. Of those that a mesh axis runs over, the one named last changes fastest.
Arguments:
- points: float32 [16, 32768], P(None, ('col', 'row')), may hold values from -6 to 6
- right_sides: float32 [17, 32768], P(None, ('col', 'row')), may hold values from -40 to 40
Outputs:
- solution_field: float32 [17, 32768], P(None, ('col', 'row'))
- residual: float32 [17, 32768], P(None, ('col', 'row'))
All inputs are finite; a program needn't handle non-finite values.
Results may differ from a plain program's by a relative error of at most 0.0003.
Values sent between devices are 32-bit elements; how exact they have to be, the bound alone decides.
No kernel may reach another device: no remote copies, remote signals or barrier semaphores. Data moves between devices by JAX's collectives and lax.ppermute only.
A program may use at most 64 MiB of HBM per device.

v0:
```python
import jax
import jax.numpy as jnp
from jax import lax
from jax.sharding import PartitionSpec as P

ITERS = 2


NOISE = 0.1
SCALE = 0.125


def kernel_block(row_points, row_norms, col_points, col_norms):
    products = lax.dot_general(
        row_points,
        col_points,
        (((0,), (0,)), ((), ())),
        precision=lax.Precision.HIGHEST,
        preferred_element_type=jnp.float32,
    )
    return jnp.exp(-SCALE * (row_norms[:, None] + col_norms[None, :] - 2.0 * products))


def times_kernel(vectors, kernel):
    return lax.dot_general(
        vectors,
        kernel,
        (((1,), (1,)), ((), ())),
        precision=lax.Precision.HIGHEST,
        preferred_element_type=jnp.float32,
    )


def kernel_times(vectors, kernel):
    return lax.dot_general(
        vectors,
        kernel,
        (((1,), (0,)), ((), ())),
        precision=lax.Precision.HIGHEST,
        preferred_element_type=jnp.float32,
    )


def apply_operator(vectors, geometry):
    row_points, row_norms, col_points, col_norms = geometry
    row_count = vectors.shape[1]
    strip_count = row_points.shape[1] // row_count
    col_width = col_points.shape[1]
    col_vectors = lax.all_gather(vectors, "row", axis=1, tiled=True)
    block_col = lax.axis_index("col")
    block_row = lax.axis_index("row")
    row_vectors = lax.all_gather(vectors, "col", axis=1, tiled=True)
    position = jnp.arange(col_width) // row_count
    forward_mask = (position >= block_row).astype(jnp.float32)
    backward_mask = (position > block_row).astype(jnp.float32)
    col_part = jnp.zeros((vectors.shape[0], col_width), jnp.float32)
    pieces = []
    for strip_index in range(strip_count):
        low = strip_index * row_count
        strip_points = row_points[:, low : low + row_count]
        strip_norms = row_norms[low : low + row_count]
        strip_vectors = row_vectors[:, low : low + row_count]

        def skipped(col_sum):
            return (jnp.zeros((vectors.shape[0], row_count), jnp.float32), col_sum)

        def complete(col_sum):
            kernel = kernel_block(strip_points, strip_norms, col_points, col_norms)
            return (
                times_kernel(col_vectors, kernel),
                col_sum + kernel_times(strip_vectors, kernel),
            )

        def diagonal(col_sum):
            kernel = kernel_block(strip_points, strip_norms, col_points, col_norms)
            forward = times_kernel(col_vectors * forward_mask[None, :], kernel)
            return (forward, col_sum + kernel_times(strip_vectors, kernel) * backward_mask[None, :])

        active = strip_index < block_col
        branch_index = jnp.where(strip_index == block_col, 2, jnp.where(active, 1, 0))
        forward, col_part = lax.switch(branch_index, (skipped, complete, diagonal), col_part)
        pieces.append(forward)
    row_part = jnp.concatenate(pieces, axis=1)
    col_total = lax.psum_scatter(col_part, "row", scatter_dimension=1, tiled=True)
    row_total = lax.psum_scatter(row_part, "col", scatter_dimension=1, tiled=True)
    return row_total + col_total + NOISE * vectors


def per_device(points, right_sides):
    col_points = lax.all_gather(points, "row", axis=1, tiled=True)
    row_points = lax.all_gather(points, "col", axis=1, tiled=True)
    geometry = (
        row_points,
        jnp.sum(row_points * row_points, axis=0),
        col_points,
        jnp.sum(col_points * col_points, axis=0),
    )
    solution_field = jnp.zeros_like(right_sides)
    residual = right_sides
    direction = right_sides
    norm_now = lax.psum(jnp.sum(residual * residual, axis=1), ("row", "col"))
    for iteration in range(ITERS):
        mapped = apply_operator(direction, geometry)
        curve = lax.psum(jnp.sum(direction * mapped, axis=1), ("row", "col"))
        step_size = norm_now / curve
        solution_field = solution_field + step_size[:, None] * direction
        residual = residual - step_size[:, None] * mapped
        if iteration + 1 < ITERS:
            norm_next = lax.psum(jnp.sum(residual * residual, axis=1), ("row", "col"))
            direction = residual + (norm_next / norm_now)[:, None] * direction
            norm_now = norm_next
    return (solution_field, residual)


def solution(mesh):
    return jax.shard_map(
        per_device,
        mesh=mesh,
        in_specs=(P(None, ("col", "row")), P(None, ("col", "row"))),
        out_specs=(P(None, ("col", "row")), P(None, ("col", "row"))),
        check_vma=False,
    )
```

profile of v0, /device:TPU:1, one launch (start us, length us, event | category | flops | bytes accessed | tf_op | source)
XLA Modules:
  0.0 983.5 jit_solution(10047016186014600816)
XLA Ops:
  7.2 0.0 reduce-scatter.5.cloned.1.call-start
  7.2 37.5 %all_gather.19 = f32[16,4096]{1,0:T(8,128)S(1)} all-gather(f32[16,128]{1,0:T(8,128)} %param.50), channel_id=1, replica_groups=mesh['row'=32,'col'=8] {'row'}, dimensions={1}, use_global_device_ids=true | all-gather | bytes 270336 | tf_op jit(solution)/shard_map/all_gather | solution.py:90
  44.7 23.9 %all_gather.18 = f32[16,1024]{1,0:T(8,128)S(1)} all-gather(f32[16,128]{1,0:T(8,128)} %param.50), channel_id=1, replica_groups=mesh['row'=32,'col'=8] {'col'}, dimensions={1}, use_global_device_ids=true | all-gather | bytes 73728 | tf_op jit(solution)/shard_map/all_gather | solution.py:91
  68.7 33.0 %all_gather.20 = f32[17,4096]{1,0:T(8,128)S(1)} all-gather(f32[17,128]{1,0:T(8,128)} %param.51), channel_id=1, replica_groups=mesh['row'=32,'col'=8] {'row'}, dimensions={1}, use_global_device_ids=true | all-gather | bytes 287232 | tf_op jit(solution)/shard_map/all_gather | solution.py:49
  101.7 22.5 %all_gather.21 = f32[17,1024]{1,0:T(8,128)S(1)} all-gather(f32[17,128]{1,0:T(8,128)} %param.51), channel_id=1, replica_groups=mesh['row'=32,'col'=8] {'col'}, dimensions={1}, use_global_device_ids=true | all-gather | bytes 78336 | tf_op jit(solution)/shard_map/all_gather | solution.py:52
  124.3 5.1 conditional.16
  124.3 2.2 fusion.2
  126.5 1.2 convolution_bitcast_fusion
  127.7 1.7 convolution_bitcast_fusion.1
  129.5 6.7 conditional.17
  129.6 2.2 fusion.16
  131.8 1.2 fusion.18
  133.1 1.7 fusion.19
  136.2 13.1 %conditional.19 = (f32[17,128]{1,0:T(8,128)S(1)}, f32[17,4096]{1,0:T(8,128)S(1)}) conditional(s32[]{:T(128)} %clamp.35, f32[17,4096]{1,0:T(8,128)S(1)} %get-tuple-element.809, (f32[128]{0:T(128)S(1)}, f32[4096]{0:T(1024)S(1)}, f32[16,128]{1,0:T(8,128)S(1)}, f32[16,4096]{1,0:T(8,128)S(1)}, f32[17,4096]{1,0:T(8,128)S(1)}, ...), branch_computations={%region_13.14_spmd, %region_14.15_spmd, %region_15.16_spmd} | conditional | flops 316878848 | bytes 7464464 | solution.py:81
  149.3 12.8 %conditional.21 = (f32[17,128]{1,0:T(8,128)S(1)}, f32[17,4096]{1,0:T(8,128)S(1)}) conditional(s32[]{:T(128)} %clamp.37, f32[17,4096]{1,0:T(8,128)S(1)} %get-tuple-element.813, (f32[128]{0:T(128)S(1)}, f32[4096]{0:T(1024)S(1)}, f32[16,128]{1,0:T(8,128)S(1)}, f32[16,4096]{1,0:T(8,128)S(1)}, f32[17,4096]{1,0:T(8,128)S(1)}, ...), branch_computations={%region_19.20_spmd, %region_20.21_spmd, %region_21.22_spmd} | conditional | flops 316878848 | bytes 7464464 | solution.py:81
  162.3 14.8 %conditional.23 = (f32[17,128]{1,0:T(8,128)S(1)}, f32[17,4096]{1,0:T(8,128)S(1)}) conditional(s32[]{:T(128)} %clamp.39, f32[17,4096]{1,0:T(8,128)S(1)} %get-tuple-element.817, (f32[128]{0:T(128)S(1)}, f32[4096]{0:T(1024)S(1)}, f32[16,128]{1,0:T(8,128)S(1)}, f32[16,4096]{1,0:T(8,128)S(1)}, f32[17,4096]{1,0:T(8,128)S(1)}, ...), branch_computations={%region_25.26_spmd, %region_26.27_spmd, %region_27.28_spmd} | conditional | flops 316878848 | bytes 7464464 | solution.py:81
  177.2 0.7 copy-done.4
  177.9 0.0 reduce-scatter.7.cloned.1.call-start
  178.0 0.7 reduce-scatter.7.cloned.1.call-update
  178.6 0.0 reduce-scatter.9.cloned.1.call-start
  178.7 26.4 %reduce-scatter.5.cloned.1.call-done = f32[17,128]{1,0:T(8,128)} async-done(((f32[17,1024]{1,0:T(8,128)}), f32[17,128]{1,0:T(8,128)}) %reduce-scatter.5.cloned.1.call-update) | async-done | bytes 8720 | tf_op jit(solution)/shard_map/reduce_scatter | solution.py:85
  205.1 201.0 %reduce-scatter.7.cloned.1.call-done = f32[17,128]{1,0:T(8,128)} async-done(((f32[17,4096]{1,0:T(8,128)}), f32[17,128]{1,0:T(8,128)}) %reduce-scatter.7.cloned.1.call-update) | async-done | bytes 8720 | tf_op jit(solution)/shard_map/reduce_scatter | solution.py:84
  406.1 0.8 multiply_reduce_fusion.4
  406.9 79.8 %all-reduce = (f32[17]{0:T(128)S(1)}, f32[17]{0:T(128)S(1)}) all-reduce(f32[17]{0:T(128)S(1)} %get-tuple-element.837, f32[17]{0:T(128)S(1)} %get-tuple-element.836), channel_id=1, replica_groups=mesh['row'=32,'col'=8] {'row','col'}, use_global_device_ids=true, to_apply=%region_1.0 | all-reduce | flops 34 | bytes 272 | tf_op jit(solution)/shard_map/psum | solution.py:101
  486.7 0.9 multiply_reduce_fusion.3
  487.6 73.3 %psum.30 = f32[17]{0:T(128)S(1)} all-reduce(f32[17]{0:T(128)S(1)} %get-tuple-element.840), channel_id=1, replica_groups=mesh['row'=32,'col'=8] {'row','col'}, use_global_device_ids=true, to_apply=%region_33.34 | all-reduce | flops 17 | bytes 136 | tf_op jit(solution)/shard_map/psum | solution.py:109
  561.0 0.1 multiply_add_fusion.2
  561.0 33.3 %all_gather.22 = f32[17,4096]{1,0:T(8,128)S(1)} all-gather(f32[17,128]{1,0:T(8,128)S(1)} %multiply_add_fusion.2), channel_id=1, replica_groups=mesh['row'=32,'col'=8] {'row'}, dimensions={1}, use_global_device_ids=true | all-gather | bytes 287232 | tf_op jit(solution)/shard_map/all_gather | solution.py:49
  594.4 22.2 %all_gather.23 = f32[17,1024]{1,0:T(8,128)S(1)} all-gather(f32[17,128]{1,0:T(8,128)S(1)} %multiply_add_fusion.2), channel_id=1, replica_groups=mesh['row'=32,'col'=8] {'col'}, dimensions={1}, use_global_device_ids=true | all-gather | bytes 78336 | tf_op jit(solution)/shard_map/all_gather | solution.py:52
  616.6 5.1 conditional.24
  616.6 2.2 fusion.96
  618.8 1.2 convolution_bitcast_fusion.16
  620.0 1.7 convolution_bitcast_fusion.17
  621.8 6.9 conditional.25
  622.0 2.2 fusion.110
  624.2 1.2 fusion.112
  625.4 1.7 fusion.113
  628.7 12.8 %conditional.27 = (f32[17,128]{1,0:T(8,128)S(1)}, f32[17,4096]{1,0:T(8,128)S(1)}) conditional(s32[]{:T(128)} %clamp.35, f32[17,4096]{1,0:T(8,128)S(1)} %get-tuple-element.825, (f32[128]{0:T(128)S(1)}, f32[4096]{0:T(1024)S(1)}, f32[16,128]{1,0:T(8,128)S(1)}, f32[16,4096]{1,0:T(8,128)S(1)}, f32[17,4096]{1,0:T(8,128)S(1)}, ...), branch_computations={%region_43.44_spmd, %region_44.45_spmd, %region_45.46_spmd} | conditional | flops 316878848 | bytes 7464464 | solution.py:81
  641.6 13.1 %conditional.29 = (f32[17,128]{1,0:T(8,128)S(1)}, f32[17,4096]{1,0:T(8,128)S(1)}) conditional(s32[]{:T(128)} %clamp.37, f32[17,4096]{1,0:T(8,128)S(1)} %get-tuple-element.829, (f32[128]{0:T(128)S(1)}, f32[4096]{0:T(1024)S(1)}, f32[16,128]{1,0:T(8,128)S(1)}, f32[16,4096]{1,0:T(8,128)S(1)}, f32[17,4096]{1,0:T(8,128)S(1)}, ...), branch_computations={%region_49.50_spmd, %region_50.51_spmd, %region_51.52_spmd} | conditional | flops 316878848 | bytes 7464464 | solution.py:81
  654.7 7.9 conditional.31
  662.8 0.7 copy-done.3
  663.5 0.0 reduce-scatter.11.cloned.1.call-start
  663.5 0.5 reduce-scatter.11.cloned.1.call-update
  664.0 30.6 %reduce-scatter.9.cloned.1.call-done = f32[17,128]{1,0:T(8,128)} async-done(((f32[17,1024]{1,0:T(8,128)}), f32[17,128]{1,0:T(8,128)}) %reduce-scatter.9.cloned.1.call-update) | async-done | bytes 8720 | tf_op jit(solution)/shard_map/reduce_scatter | solution.py:85
  694.6 200.2 %reduce-scatter.11.cloned.1.call-done = f32[17,128]{1,0:T(8,128)} async-done(((f32[17,4096]{1,0:T(8,128)}), f32[17,128]{1,0:T(8,128)}) %reduce-scatter.11.cloned.1.call-update) | async-done | bytes 8720 | tf_op jit(solution)/shard_map/reduce_scatter | solution.py:84
  894.8 0.8 multiply_reduce_fusion.2
  895.6 79.8 %psum.31 = f32[17]{0:T(128)S(1)} all-reduce(f32[17]{0:T(128)S(1)} %multiply_reduce_fusion.2), channel_id=1, replica_groups=mesh['row'=32,'col'=8] {'row','col'}, use_global_device_ids=true, to_apply=%region_61.62 | all-reduce | flops 17 | bytes 136 | tf_op jit(solution)/shard_map/psum | solution.py:104
  975.4 1.4 multiply_subtract_fusion
  (54 shorter events, 0.4 us)
Async XLA Ops:
  7.2 197.9 %reduce-scatter.5.cloned.1.call-start = ((), (), s32[]{:S(2)}) async-start(), calls=%async_computation.4 | async-start | bytes 110592 | tf_op jit(solution)/shard_map/reduce_scatter | solution.py:85
  162.3 243.8 %copy-start.2 = (f32[17,128]{1,0:T(8,128)S(1)}, f32[17,128]{1,0:T(8,128)}, u32[]{:S(2)}) copy-start(f32[17,128]{1,0:T(8,128)} %param.51) | copy-start | bytes 26116
  177.2 0.8 copy-start
  177.2 0.7 copy-start.4
  177.9 228.2 %reduce-scatter.7.cloned.1.call-start = ((), (), s32[]{:S(2)}) async-start(), calls=%async_computation.5 | async-start | bytes 405504 | tf_op jit(solution)/shard_map/reduce_scatter | solution.py:84
  178.6 516.0 %reduce-scatter.9.cloned.1.call-start = ((), (), s32[]{:S(2)}) async-start(), calls=%async_computation.6 | async-start | bytes 110592 | tf_op jit(solution)/shard_map/reduce_scatter | solution.py:85
  662.7 0.9 copy-start.1
  662.7 0.7 copy-start.3
  663.5 231.3 %reduce-scatter.11.cloned.1.call-start = ((), (), s32[]{:S(2)}) async-start(), calls=%async_computation.7 | async-start | bytes 405504 | tf_op jit(solution)/shard_map/reduce_scatter | solution.py:84
Sparse Core Ops, SparseCore 0:
  178.0 26.9 reduce-scatter.4
  209.3 196.6 reduce-scatter.6
  663.6 30.9 reduce-scatter.8
  698.3 196.4 reduce-scatter.10
where the time goes:
time: 993 us; the launch traced here: 984 us
  waiting for transfers between devices  459 us (46%)
  blocking collectives  405 us (41%)
  loops' own time  78 us (8%)
  matrix products  20.5 us (2%)
  between operations  14.4 us (1%)
    reduce_scatter x2, waiting for transfers between devices, apply_operator(): lax.psum_scatter(col_part, 'row', scatter_dimension=1, tiled=True)  401 us
    psum x1, blocking collectives, per_device(): norm_now = lax.psum(jnp.sum(residual * residual, axis=1), ('row', 'col'))  79.8 us
    psum x1, blocking collectives, per_device(): curve = lax.psum(jnp.sum(direction * mapped, axis=1), ('row', 'col'))  79.8 us
    another operation x16, loops' own time, apply_operator(): lax.switch(branch_index, (skipped, complete, diagonal), col_part)  78 us
    psum x1, blocking collectives, per_device(): norm_next = lax.psum(jnp.sum(residual * residual, axis=1), ('row', 'col'))  73.3 us
    all_gather x2, blocking collectives, apply_operator(): col_vectors = lax.all_gather(vectors, 'row', axis=1, tiled=True)  66.4 us
    reduce_scatter x2, waiting for transfers between devices, apply_operator(): lax.psum_scatter(row_part, 'col', scatter_dimension=1, tiled=True)  56.9 us
    all_gather x2, blocking collectives, apply_operator(): row_vectors = lax.all_gather(vectors, 'col', axis=1, tiled=True)  44.7 us
  transfers between devices with their start and end apart: 4, of which 4 were waited for; matrix products, arithmetic and copies ran while one was open for 0% of the time, Pallas kernels for 0%

commit v1 on v0

v1 whole, which is shorter than its diff:
```python
import functools
import math

import jax
import jax.numpy as jnp
import numpy as np
from jax import lax
from jax.experimental import pallas as pl
from jax.experimental.pallas import tpu as pltpu
from jax.sharding import PartitionSpec as P

AXES = ("row", "col")
NOISE = 0.1
SCALE = 0.125
COEF = SCALE * math.log2(math.e)
F32 = jnp.float32
BF16 = jnp.bfloat16

DIMS = (("y", 4), ("w", 4), ("p", 2), ("x", 4), ("c", 2))
NAMES = [n for n, _ in DIMS]
IDS = np.arange(256).reshape([s for _, s in DIMS])


def send_by(**shift):
    target = IDS
    for name, amount in shift.items():
        target = np.roll(target, -amount, axis=NAMES.index(name))
    return list(zip(IDS.reshape(-1).tolist(), target.reshape(-1).tolist()))


def groups_over(*names):
    rest = [n for n in NAMES if n not in names]
    order = [NAMES.index(n) for n in rest + list(names)]
    size = int(np.prod([dict(DIMS)[n] for n in names]))
    return IDS.transpose(order).reshape(-1, size).tolist()


def split3(value):
    first = value.astype(BF16).astype(F32)
    rest = value - first
    second = rest.astype(BF16).astype(F32)
    return first, second, (rest - second).astype(BF16).astype(F32)


def norm_rows(points, norm_first):
    norm = -COEF * jnp.sum(points * points, axis=0, keepdims=True)
    parts = split3(norm)
    index = lax.broadcasted_iota(jnp.int32, points.shape, 0)
    base = 0 if norm_first else 3
    ones = 3 - base
    rows = jnp.where((index >= ones) & (index < ones + 3), 1.0, 0.0)
    for k in range(3):
        rows = jnp.where(index == base + k, parts[k], rows)
    return rows


def left_rows(points):
    a, b, c = split3(points * (2.0 * COEF))
    return jnp.concatenate(
        [a, a, b, b, a, c, norm_rows(points, True), jnp.zeros_like(a)], axis=0
    )


def right_rows(points):
    a, b, c = split3(points)
    return jnp.concatenate(
        [a, b, a, b, c, a, norm_rows(points, False), jnp.zeros_like(a)], axis=0
    )


def pad_rows(value, rows):
    return jnp.concatenate(
        [value, jnp.zeros((rows - value.shape[0], value.shape[1]), value.dtype)], axis=0
    )


def first_kernel(
    own_ref, by_c_ref, by_p_ref, x1_ref, x2_ref, x3_ref, col_ref,
    high_ref, low_ref, keep_ref, send_ref, left_ref, total_ref,
):
    step = pl.program_id(0)

    @pl.when(step == 0)
    def _():
        blocks = [
            jnp.concatenate([own_ref[...], by_c_ref[...], by_p_ref[...]], axis=1),
            x1_ref[...], x2_ref[...], x3_ref[...],
        ]
        for dx in range(4):
            rows = left_rows(blocks[dx]).T.astype(BF16)
            for dp in range(2):
                for dc in range(2):
                    low = (dp * 2 + dc) * 128
                    at = (dc * 8 + dp * 4 + dx) * 128
                    left_ref[at : at + 128, :] = rows[low : low + 128, :]
        total_ref[...] = jnp.zeros_like(total_ref)

    block = jnp.concatenate([col_ref[0], col_ref[1]], axis=1)
    right = right_rows(block[:16]).astype(BF16)
    parts = split3(block[16:])
    vectors = pad_rows(
        jnp.concatenate([pad_rows(part, 32) for part in parts], axis=0), 128
    ).T.astype(BF16)
    for chunk in range(8):
        at = pl.ds(chunk * 256, 256)
        kernel = jnp.exp2(jnp.dot(left_ref[at, :], right, preferred_element_type=F32))
        high = kernel.astype(BF16)
        low = (kernel - high.astype(F32)).astype(BF16)
        high_ref[at, :] = high
        low_ref[at, :] = low
        total_ref[at, :] += jnp.dot(
            high, vectors, preferred_element_type=F32
        ) + jnp.dot(low, vectors, preferred_element_type=F32)

    @pl.when(step == pl.num_programs(0) - 1)
    def _():
        for half, out_ref in enumerate((keep_ref, send_ref)):
            total = total_ref[half * 1024 : (half + 1) * 1024, :].T
            out_ref[...] = total[0:17] + total[32:49] + total[64:81]


def second_kernel(own_ref, by_p_ref, by_c_ref, high_ref, low_ref, out_ref, left_ref):
    @pl.when(pl.program_id(0) == 0)
    def _():
        vectors = jnp.concatenate([own_ref[...], by_p_ref[...], by_c_ref[...]], axis=1)
        left_ref[...] = jnp.concatenate(
            [pad_rows(part, 32) for part in split3(vectors)], axis=0
        ).astype(BF16)

    left = left_ref[...]
    total = jnp.dot(left, high_ref[...], preferred_element_type=F32) + jnp.dot(
        left, low_ref[...], preferred_element_type=F32
    )
    total = total[0:17] + total[32:49] + total[64:81]
    out_ref[0] = total[:, :128]
    out_ref[1] = total[:, 128:]


def dots_kernel(parts_ref, sides_ref, image_ref, out_first_ref, out_second_ref, dots_ref):
    sides = sides_ref[...]
    first = image_ref[:, :128] - sides
    second = jnp.sum(parts_ref[...], axis=0) - image_ref[:, :128] - first
    out_first_ref[...] = first
    out_second_ref[...] = second
    rows = jnp.concatenate(
        [pad_rows(t, 32) for t in (sides * sides, sides * first, first * first, first * second)],
        axis=0,
    )
    dots_ref[...] = jnp.sum(rows.T, axis=0, keepdims=True)


def last_kernel(dots_ref, sides_ref, first_ref, second_ref, solution_ref, residual_ref):
    dots = jnp.sum(dots_ref[...], axis=0)
    table = jnp.broadcast_to(dots, (128, 128)).T
    g0, g1, g2, g3 = (table[32 * k : 32 * k + 17] for k in range(4))
    diagonal = 1.0 + NOISE
    sides, first, second = sides_ref[...], first_ref[...], second_ref[...]
    step = g0 / (g1 + diagonal * g0)
    ratio = g1 / g0
    residual = step * (ratio * sides - first)
    norm = step * step * (g2 - ratio * g1)
    turn = norm / g0
    weight = step * ratio + turn
    direction = residual + turn * sides
    curve = (
        weight * weight * g1
        - 2.0 * weight * step * g2
        + step * step * g3
        + diagonal * (norm + turn * turn * g0)
    )
    step_next = norm / curve
    mapped = weight * first - step * second + diagonal * direction
    solution_ref[...] = step * sides + step_next * direction
    residual_ref[...] = residual - step_next * mapped


def whole(*shape):
    return pl.BlockSpec(shape, lambda i: (0,) * len(shape))


def per_device(points, right_sides):
    permute = functools.partial(lax.ppermute, axis_name=AXES)
    swap_c = send_by(c=1)
    swap_p = send_by(p=1)
    from_x = [send_by(x=-k) for k in (1, 2, 3)]
    col_groups = groups_over("y", "w")
    exchange = functools.partial(
        lax.all_to_all, axis_name=AXES, split_axis=0, concat_axis=0, tiled=True
    )

    by_c = permute(points, perm=swap_c)
    pair = jnp.concatenate([points, by_c], axis=1)
    by_p = permute(pair, perm=swap_p)
    four = jnp.concatenate([pair, by_p], axis=1)
    by_x = [permute(four, perm=p) for p in from_x]
    mine = jnp.concatenate([points, right_sides], axis=0)
    columns = exchange(
        jnp.broadcast_to(mine[None], (16, 33, 128)), axis_index_groups=col_groups
    )

    high, low, keep, send = pl.pallas_call(
        first_kernel,
        grid=(8,),
        in_specs=[
            whole(16, 128), whole(16, 128), whole(16, 256),
            whole(16, 512), whole(16, 512), whole(16, 512),
            pl.BlockSpec((2, 33, 128), lambda i: (i, 0, 0)),
        ],
        out_specs=[
            pl.BlockSpec((2048, 256), lambda i: (0, i)),
            pl.BlockSpec((2048, 256), lambda i: (0, i)),
            whole(17, 1024), whole(17, 1024),
        ],
        out_shape=[
            jax.ShapeDtypeStruct((2048, 2048), BF16),
            jax.ShapeDtypeStruct((2048, 2048), BF16),
            jax.ShapeDtypeStruct((17, 1024), F32),
            jax.ShapeDtypeStruct((17, 1024), F32),
        ],
        scratch_shapes=[pltpu.VMEM((2048, 128), BF16), pltpu.VMEM((2048, 128), F32)],
        compiler_params=pltpu.CompilerParams(vmem_limit_bytes=32 * 1024 * 1024),
        name="tile",
    )(points, by_c, by_p, *by_x, columns)

    half = keep + permute(send, perm=swap_c)
    quarter = half[:, :512] + permute(half[:, 512:], perm=swap_p)
    image = quarter
    for k, p in zip((1, 2, 3), from_x):
        image = image + jnp.roll(permute(quarter, perm=p), k * 128, axis=1)
    image_p = permute(image, perm=swap_p)
    image_c = permute(jnp.concatenate([image, image_p], axis=1), perm=swap_c)

    parts = pl.pallas_call(
        second_kernel,
        grid=(8,),
        in_specs=[
            whole(17, 512), whole(17, 512), whole(17, 1024),
            pl.BlockSpec((2048, 256), lambda i: (0, i)),
            pl.BlockSpec((2048, 256), lambda i: (0, i)),
        ],
        out_specs=pl.BlockSpec((2, 17, 128), lambda i: (i, 0, 0)),
        out_shape=jax.ShapeDtypeStruct((16, 17, 128), F32),
        scratch_shapes=[pltpu.VMEM((96, 2048), BF16)],
        compiler_params=pltpu.CompilerParams(vmem_limit_bytes=32 * 1024 * 1024),
        name="transposed",
    )(image, image_p, image_c, high, low)

    pieces = exchange(parts, axis_index_groups=col_groups)
    vector = jax.ShapeDtypeStruct((17, 128), F32)
    first, second, dots = pl.pallas_call(
        dots_kernel,
        out_shape=[vector, vector, jax.ShapeDtypeStruct((1, 128), F32)],
        name="dots",
    )(pieces, right_sides, image)
    all_dots = exchange(jnp.broadcast_to(dots[None], (256, 1, 128)))
    return pl.pallas_call(last_kernel, out_shape=[vector, vector], name="finish")(
        all_dots, right_sides, first, second
    )


def solution(mesh):
    spec = P(None, ("col", "row"))
    return jax.shard_map(
        lambda p, r: tuple(per_device(p, r)),
        mesh=mesh,
        in_specs=(spec, spec),
        out_specs=(spec, spec),
        check_vma=False,
    )
```

time: 993 us -> 121 us (0.12)
  waiting for transfers between devices: 459 us -> 17.7 us
  blocking collectives: 405 us -> 40.8 us
  loops' own time: 78 us -> 0 us
  starting transfers between devices: 0.16 us -> 29.6 us
  Pallas kernels: 0 us -> 27.9 us
  matrix products: 20.5 us -> 0 us
  between operations: 14.4 us -> 0.73 us
    reduce_scatter x4 -> x0, waiting for transfers between devices: 458 us -> none  [the longest x2 401 us: apply_operator(): lax.psum_scatter(col_part, 'row', scatter_dimension=1, tiled=True)]
    psum x3 -> x0, blocking collectives: 233 us -> none  [the longest x1 79.8 us: per_device(): norm_now = lax.psum(jnp.sum(residual * residual, axis=1), ('row', 'col'))]
    all_gather x6 -> x0, blocking collectives: 173 us -> none  [the longest x2 66.4 us: apply_operator(): col_vectors = lax.all_gather(vectors, 'row', axis=1, tiled=True)]
    another operation x16 -> x0, loops' own time: 78 us -> none  [apply_operator(): lax.switch(branch_index, (skipped, complete, diagonal), col_part)]
    all_to_all x0 -> x2, blocking collectives: none -> 40.8 us  [the longest x1 20.7 us: per_device(): all_dots = exchange(jnp.broadcast_to(dots[None], (256, 1, 128)))]
    pallas_call x0 -> x4, Pallas kernels: none -> 27.9 us  [the longest x1 18.2 us: per_device(): pl.pallas_call(first_kernel, grid=(8,), in_specs=[whole(16, 128), whole(1...]
    dot_general x12 -> x0, matrix products: 20.5 us -> none  [the longest x4 8.67 us: kernel_block(): lax.dot_general(row_points, col_points, (((0,), (0,)), ((), ())), precisi...]
    ppermute x0 -> x12, starting transfers between devices: none -> 17.8 us  [the longest x3 4.81 us: per_device(): by_x = [permute(four, perm=p) for p in from_x]]
  transfers between devices with their start and end apart: 4 -> 13, of which waited for: 4 -> 11; matrix products, arithmetic and copies ran while one was open for 0% -> 1% of each run, Pallas kernels for 0% -> 0%
where the time goes in v1:
time: 121 us
  blocking collectives  40.8 us (34%)
  starting transfers between devices  29.6 us (24%)
  Pallas kernels  27.9 us (23%)
  waiting for transfers between devices  17.7 us (15%)
  local copies, waits for them, and re-layouts  2.91 us (2%)
  other arithmetic  1.47 us (1%)
    all_to_all x1, blocking collectives, per_device(): all_dots = exchange(jnp.broadcast_to(dots[None], (256, 1, 128)))  20.7 us
    all_to_all x1, blocking collectives, per_device(): pieces = exchange(parts, axis_index_groups=col_groups)  20.1 us
    pallas_call x1, Pallas kernels, per_device(): pl.pallas_call(first_kernel, grid=(8,), in_specs=[whole(16, 128), whole(1...  18.2 us
    all_to_all x1, starting transfers between devices, per_device(): exchange(jnp.broadcast_to(mine[None], (16, 33, 128)), axis_index_groups=c...  11.7 us
    pallas_call x1, Pallas kernels, per_device(): pl.pallas_call(second_kernel, grid=(8,), in_specs=[whole(17, 512), whole(...  6.24 us
    ppermute x3, starting transfers between devices, per_device(): by_x = [permute(four, perm=p) for p in from_x]  4.81 us
    ppermute x1, starting transfers between devices, per_device(): image_c = permute(jnp.concatenate([image, image_p], axis=1), perm=swap_c)  4.05 us
    ppermute x3, waiting for transfers between devices, per_device(): image = image + jnp.roll(permute(quarter, perm=p), k * 128, axis=1)  3.93 us
  transfers between devices with their start and end apart: 13, of which 11 were waited for; matrix products, arithmetic and copies ran while one was open for 1% of the time, Pallas kernels for 0%

profile of v1, /device:TPU:1, one launch (start us, length us, event | category | flops | bytes accessed | tf_op | source)
XLA Modules:
  0.0 121.0 jit_solution(18381268844645140915)
XLA Ops:
  0.6 0.7 pad_maximum_fusion.1
  1.4 0.7 broadcast_in_dim.6
  2.1 11.7 %all-to-all-start = ((f32[16,33,128]{2,1,0:T(8,128)}), f32[16,33,128]{2,1,0:T(8,128)S(1)}, u32[]{:S(2)}, u32[]{:S(2)}) async-start(f32[16,33,128]{2,1,0:T(8,128)} %broadcast_in_dim.6), calls=%async_computation | async-start | bytes 655360 | tf_op jit(solution)/shard_map/all_to_all | solution.py:197
  13.9 1.0 collective-permute-start
  14.9 0.7 constant_dynamic-update-slice_fusion.2
  15.6 0.3 collective-permute-done.by_c_ref
  15.9 0.7 pad_maximum_fusion.2
  16.6 0.7 collective-permute-start.1
  17.4 3.7 %collective-permute-done.1.by_p_ref = f32[16,256]{1,0:T(8,128)S(1)} collective-permute-done((f32[16,256]{1,0:T(8,128)S(1)}, f32[16,256]{1,0:T(8,128)S(1)}, u32[]{:S(2)}, u32[]{:S(2)}) %collective-permute-start.1) | collective-permute-done | bytes 16416 | tf_op jit(solution)/shard_map/ppermute | solution.py:193
  21.0 1.2 %collective-permute-start.4 = (f32[16,512]{1,0:T(8,128)S(1)}, f32[16,512]{1,0:T(8,128)S(1)}, u32[]{:S(2)}, u32[]{:S(2)}) collective-permute-start(f32[16,512]{1,0:T(8,128)S(1)} %constant_dynamic-update-slice_fusion), channel_id=1, source_target_pairs={{0,2},{1,3},{2,4},{3,5},{4,6},{5,7},{6,0},{7,1},{8,10},{9,11},{10,... | collective-permute-start | bytes 98312 | tf_op jit(solution)/shard_map/ppermute | solution.py:195
  22.3 2.5 %collective-permute-start.3 = (f32[16,512]{1,0:T(8,128)S(1)}, f32[16,512]{1,0:T(8,128)S(1)}, u32[]{:S(2)}, u32[]{:S(2)}) collective-permute-start(f32[16,512]{1,0:T(8,128)S(1)} %constant_dynamic-update-slice_fusion), channel_id=1, source_target_pairs={{0,4},{1,5},{2,6},{3,7},{4,0},{5,1},{6,2},{7,3},{8,12},{9,13},{10,... | collective-permute-start | bytes 98312 | tf_op jit(solution)/shard_map/ppermute | solution.py:195
  24.7 1.2 collective-permute-start.2
  25.9 0.0 collective-permute-done.4.x3_ref
  25.9 0.7 collective-permute-done.3.x2_ref
  26.6 1.2 collective-permute-done.2.x1_ref
  27.8 0.1 all-to-all-done.col_ref
  27.9 0.0 copy-start.1
  27.9 0.7 copy-done.1
  28.6 18.2 %tile.1 = (bf16[2048,2048]{1,0:T(8,128)(2,1)S(1)}, bf16[2048,2048]{1,0:T(8,128)(2,1)S(1)}, f32[17,1024]{1,0:T(8,128)S(1)}, f32[17,1024]{1,0:T(8,128)S(1)}) custom-call(f32[16,128]{1,0:T(8,128)S(1)} %copy-done.1, f32[16,128]{1,0:T(8,128)S(1)} %collective-permute-done.by_c_ref, f32[16,256]{1,0:T(8,128)S(1)} %collective-permute-done.1.by_p_ref, ...), custom_call_target="tpu_custom_call" | custom-call | tf_op jit(solution)/shard_map/tile/pallas_call | solution.py:201
  46.7 3.4 %collective-permute-start.5 = (f32[17,1024]{1,0:T(8,128)S(1)}, f32[17,1024]{1,0:T(8,128)S(1)}, u32[]{:S(2)}, u32[]{:S(2)}) collective-permute-start(f32[17,1024]{1,0:T(8,128)S(1)} %get-tuple-element.10), channel_id=1, source_target_pairs={{0,1},{1,0},{2,3},{3,2},{4,5},{5,4},{6,7},{7,6},{8,9},{9,8},{10,11... | collective-permute-start | bytes 208904 | tf_op jit(solution)/shard_map/ppermute | solution.py:225
  50.1 0.9 collective-permute-done.5
  51.0 0.1 collective-permute-start.6
  51.1 2.9 %collective-permute-done.6 = f32[17,512]{1,0:T(8,128)S(1)} collective-permute-done((f32[17,512]{1,0:T(8,128)S(1)}, f32[17,512]{1,0:T(8,128)S(1)}, u32[]{:S(2)}, u32[]{:S(2)}) %collective-permute-start.6) | collective-permute-done | bytes 34848 | tf_op jit(solution)/shard_map/ppermute | solution.py:226
  54.1 0.1 collective-permute-start.9
  54.2 2.7 %collective-permute-start.7 = (f32[17,512]{1,0:T(8,128)S(1)}, f32[17,512]{1,0:T(8,128)S(1)}, u32[]{:S(2)}, u32[]{:S(2)}) collective-permute-start(f32[17,512]{1,0:T(8,128)S(1)} %slice_add_fusion), channel_id=1, source_target_pairs={{0,6},{1,7},{2,0},{3,1},{4,2},{5,3},{6,4},{7,5},{8,14},{9,15},{10,... | collective-permute-start | bytes 104456 | tf_op jit(solution)/shard_map/ppermute | solution.py:229
  56.8 0.9 collective-permute-start.8
  57.7 0.6 collective-permute-done.9
  58.3 0.0 collective-permute-done.7
  58.4 3.3 %collective-permute-done.8 = f32[17,512]{1,0:T(8,128)S(1)} collective-permute-done((f32[17,512]{1,0:T(8,128)S(1)}, f32[17,512]{1,0:T(8,128)S(1)}, u32[]{:S(2)}, u32[]{:S(2)}) %collective-permute-start.8) | collective-permute-done | bytes 34848 | tf_op jit(solution)/shard_map/ppermute | solution.py:229
  61.7 0.0 copy-start
  61.7 0.1 collective-permute-start.10
  61.8 2.9 %collective-permute-done.10.by_p_ref = f32[17,512]{1,0:T(8,128)S(1)} collective-permute-done((f32[17,512]{1,0:T(8,128)S(1)}, f32[17,512]{1,0:T(8,128)S(1)}, u32[]{:S(2)}, u32[]{:S(2)}) %collective-permute-start.10) | collective-permute-done | bytes 34848 | tf_op jit(solution)/shard_map/ppermute | solution.py:230
  64.8 4.1 %collective-permute-start.11 = (f32[17,1024]{1,0:T(8,128)S(1)}, f32[17,1024]{1,0:T(8,128)S(1)}, u32[]{:S(2)}, u32[]{:S(2)}) collective-permute-start(f32[17,1024]{1,0:T(8,128)S(1)} %pad_maximum_fusion), channel_id=1, source_target_pairs={{0,1},{1,0},{2,3},{3,2},{4,5},{5,4},{6,7},{7,6},{8,9},{9,8},{10,11... | collective-permute-start | bytes 208904 | tf_op jit(solution)/shard_map/ppermute | solution.py:231
  68.8 0.9 collective-permute-done.11.by_c_ref
  69.8 6.2 %transposed.1 = f32[16,17,128]{2,1,0:T(8,128)S(1)} custom-call(f32[17,512]{1,0:T(8,128)S(1)} %fusion.1.own_ref.image_ref, f32[17,512]{1,0:T(8,128)S(1)} %collective-permute-done.10.by_p_ref, f32[17,1024]{1,0:T(8,128)S(1)} %collective-permute-done.11.by_c_ref, bf16[2048,2048]{1,0:T(8,128)(2,1)S(1)} %get-tuple-element.11.high_ref, ...), custom_call_target="tpu_custom_call" | custom-call | tf_op jit(solution)/shard_map/transposed/pallas_call | solution.py:233
  76.0 0.0 copy-done
  76.0 20.1 %all_to_all.15.parts_ref = f32[16,17,128]{2,1,0:T(8,128)} all-to-all(f32[16,17,128]{2,1,0:T(8,128)S(1)} %transposed.1), channel_id=1, replica_groups={{0,16,32,48,64,80,96,112,128,144,160,176,192,208,224,240},{1,17,33,49,6..., dimensions={0} | all-to-all | bytes 278528 | tf_op jit(solution)/shard_map/all_to_all | solution.py:248
  96.1 1.6 %dots.1 = (f32[17,128]{1,0:T(8,128)}, f32[17,128]{1,0:T(8,128)}, f32[1,128]{1,0:T(1,128)}) custom-call(f32[16,17,128]{2,1,0:T(8,128)} %all_to_all.15.parts_ref, f32[17,128]{1,0:T(8,128)} %sides_ref.3, f32[17,512]{1,0:T(8,128)} %copy-done), custom_call_target="tpu_custom_call" | custom-call | tf_op jit(solution)/shard_map/dots/pallas_call | solution.py:250
  97.7 0.7 broadcast_in_dim.16
  98.4 20.7 %all_to_all.16.dots_ref = f32[256,1,128]{2,1,0:T(1,128)} all-to-all(f32[256,1,128]{2,1,0:T(1,128)S(1)} %broadcast_in_dim.16), channel_id=1, replica_groups=mesh['row'=32,'col'=8] {'row','col'}, dimensions={0} | all-to-all | bytes 262144 | tf_op jit(solution)/shard_map/all_to_all | solution.py:255
  119.1 1.9 %finish.1 = (f32[17,128]{1,0:T(8,128)}, f32[17,128]{1,0:T(8,128)}) custom-call(f32[256,1,128]{2,1,0:T(1,128)} %all_to_all.16.dots_ref, f32[17,128]{1,0:T(8,128)} %sides_ref.3, f32[17,128]{1,0:T(8,128)} %get-tuple-element.14.first_ref, f32[17,128]{1,0:T(8,128)} %get-tuple-element.15.second_ref), custom_call_target="tpu_custom_call" | custom-call | tf_op jit(solution)/shard_map/finish/pallas_call | solution.py:256
  (12 shorter events, 0.1 us)
Async XLA Ops:
  2.1 25.8 %all-to-all-start = ((f32[16,33,128]{2,1,0:T(8,128)}), f32[16,33,128]{2,1,0:T(8,128)S(1)}, u32[]{:S(2)}, u32[]{:S(2)}) async-start(f32[16,33,128]{2,1,0:T(8,128)} %broadcast_in_dim.6), calls=%async_computation | async-start | bytes 655360 | tf_op jit(solution)/shard_map/all_to_all | solution.py:197
  13.9 2.1 %collective-permute-start = (f32[16,128]{1,0:T(8,128)}, f32[16,128]{1,0:T(8,128)S(1)}, u32[]{:S(2)}, u32[]{:S(2)}) collective-permute-start(f32[16,128]{1,0:T(8,128)} %own_ref.1), channel_id=1, source_target_pairs={{0,1},{1,0},{2,3},{3,2},{4,5},{5,4},{6,7},{7,6},{8,9},{9,8},{10,11... | collective-permute-start | bytes 24584 | tf_op jit(solution)/shard_map/ppermute | solution.py:191
  16.6 4.4 %collective-permute-start.1 = (f32[16,256]{1,0:T(8,128)S(1)}, f32[16,256]{1,0:T(8,128)S(1)}, u32[]{:S(2)}, u32[]{:S(2)}) collective-permute-start(f32[16,256]{1,0:T(8,128)S(1)} %pad_maximum_fusion.2), channel_id=1, source_target_pairs={{0,8},{1,9},{2,10},{3,11},{4,12},{5,13},{6,14},{7,15},{8,0},{9,1},... | collective-permute-start | bytes 49160 | tf_op jit(solution)/shard_map/ppermute | solution.py:193
  21.0 4.8 %collective-permute-start.4 = (f32[16,512]{1,0:T(8,128)S(1)}, f32[16,512]{1,0:T(8,128)S(1)}, u32[]{:S(2)}, u32[]{:S(2)}) collective-permute-start(f32[16,512]{1,0:T(8,128)S(1)} %constant_dynamic-update-slice_fusion), channel_id=1, source_target_pairs={{0,2},{1,3},{2,4},{3,5},{4,6},{5,7},{6,0},{7,1},{8,10},{9,11},{10,... | collective-permute-start | bytes 98312 | tf_op jit(solution)/shard_map/ppermute | solution.py:195
  22.3 4.3 %collective-permute-start.3 = (f32[16,512]{1,0:T(8,128)S(1)}, f32[16,512]{1,0:T(8,128)S(1)}, u32[]{:S(2)}, u32[]{:S(2)}) collective-permute-start(f32[16,512]{1,0:T(8,128)S(1)} %constant_dynamic-update-slice_fusion), channel_id=1, source_target_pairs={{0,4},{1,5},{2,6},{3,7},{4,0},{5,1},{6,2},{7,3},{8,12},{9,13},{10,... | collective-permute-start | bytes 98312 | tf_op jit(solution)/shard_map/ppermute | solution.py:195
  24.7 3.1 %collective-permute-start.2 = (f32[16,512]{1,0:T(8,128)S(1)}, f32[16,512]{1,0:T(8,128)S(1)}, u32[]{:S(2)}, u32[]{:S(2)}) collective-permute-start(f32[16,512]{1,0:T(8,128)S(1)} %constant_dynamic-update-slice_fusion), channel_id=1, source_target_pairs={{0,6},{1,7},{2,0},{3,1},{4,2},{5,3},{6,4},{7,5},{8,14},{9,15},{10,... | collective-permute-start | bytes 98312 | tf_op jit(solution)/shard_map/ppermute | solution.py:195
  27.9 0.7 copy-start.1
  46.7 4.3 %collective-permute-start.5 = (f32[17,1024]{1,0:T(8,128)S(1)}, f32[17,1024]{1,0:T(8,128)S(1)}, u32[]{:S(2)}, u32[]{:S(2)}) collective-permute-start(f32[17,1024]{1,0:T(8,128)S(1)} %get-tuple-element.10), channel_id=1, source_target_pairs={{0,1},{1,0},{2,3},{3,2},{4,5},{5,4},{6,7},{7,6},{8,9},{9,8},{10,11... | collective-permute-start | bytes 208904 | tf_op jit(solution)/shard_map/ppermute | solution.py:225
  51.0 3.0 %collective-permute-start.6 = (f32[17,512]{1,0:T(8,128)S(1)}, f32[17,512]{1,0:T(8,128)S(1)}, u32[]{:S(2)}, u32[]{:S(2)}) collective-permute-start(f32[17,512]{1,0:T(8,128)S(1)} %slice.39), channel_id=1, source_target_pairs={{0,8},{1,9},{2,10},{3,11},{4,12},{5,13},{6,14},{7,15},{8,0},{9,1},... | collective-permute-start | bytes 104456 | tf_op jit(solution)/shard_map/ppermute | solution.py:226
  54.1 4.2 %collective-permute-start.9 = (f32[17,512]{1,0:T(8,128)S(1)}, f32[17,512]{1,0:T(8,128)S(1)}, u32[]{:S(2)}, u32[]{:S(2)}) collective-permute-start(f32[17,512]{1,0:T(8,128)S(1)} %slice_add_fusion), channel_id=1, source_target_pairs={{0,2},{1,3},{2,4},{3,5},{4,6},{5,7},{6,0},{7,1},{8,10},{9,11},{10,... | collective-permute-start | bytes 104456 | tf_op jit(solution)/shard_map/ppermute | solution.py:229
  54.2 4.1 %collective-permute-start.7 = (f32[17,512]{1,0:T(8,128)S(1)}, f32[17,512]{1,0:T(8,128)S(1)}, u32[]{:S(2)}, u32[]{:S(2)}) collective-permute-start(f32[17,512]{1,0:T(8,128)S(1)} %slice_add_fusion), channel_id=1, source_target_pairs={{0,6},{1,7},{2,0},{3,1},{4,2},{5,3},{6,4},{7,5},{8,14},{9,15},{10,... | collective-permute-start | bytes 104456 | tf_op jit(solution)/shard_map/ppermute | solution.py:229
  56.8 4.8 %collective-permute-start.8 = (f32[17,512]{1,0:T(8,128)S(1)}, f32[17,512]{1,0:T(8,128)S(1)}, u32[]{:S(2)}, u32[]{:S(2)}) collective-permute-start(f32[17,512]{1,0:T(8,128)S(1)} %slice_add_fusion), channel_id=1, source_target_pairs={{0,4},{1,5},{2,6},{3,7},{4,0},{5,1},{6,2},{7,3},{8,12},{9,13},{10,... | collective-permute-start | bytes 104456 | tf_op jit(solution)/shard_map/ppermute | solution.py:229
  61.7 14.3 %copy-start = (f32[17,512]{1,0:T(8,128)}, f32[17,512]{1,0:T(8,128)S(1)}, u32[]{:S(2)}) copy-start(f32[17,512]{1,0:T(8,128)S(1)} %fusion.1.own_ref.image_ref) | copy-start | bytes 104452
  61.7 3.0 %collective-permute-start.10 = (f32[17,512]{1,0:T(8,128)S(1)}, f32[17,512]{1,0:T(8,128)S(1)}, u32[]{:S(2)}, u32[]{:S(2)}) collective-permute-start(f32[17,512]{1,0:T(8,128)S(1)} %fusion.1.own_ref.image_ref), channel_id=1, source_target_pairs={{0,8},{1,9},{2,10},{3,11},{4,12},{5,13},{6,14},{7,15},{8,0},{9,1},... | collective-permute-start | bytes 104456 | tf_op jit(solution)/shard_map/ppermute | solution.py:230
  64.8 5.0 %collective-permute-start.11 = (f32[17,1024]{1,0:T(8,128)S(1)}, f32[17,1024]{1,0:T(8,128)S(1)}, u32[]{:S(2)}, u32[]{:S(2)}) collective-permute-start(f32[17,1024]{1,0:T(8,128)S(1)} %pad_maximum_fusion), channel_id=1, source_target_pairs={{0,1},{1,0},{2,3},{3,2},{4,5},{5,4},{6,7},{7,6},{8,9},{9,8},{10,11... | collective-permute-start | bytes 208904 | tf_op jit(solution)/shard_map/ppermute | solution.py:231

commit v2 on v1

v2 whole, which is shorter than its diff:
```python
import functools
import math

import jax
import jax.numpy as jnp
import numpy as np
from jax import lax
from jax.experimental import pallas as pl
from jax.experimental.pallas import tpu as pltpu
from jax.sharding import PartitionSpec as P

AXES = ("row", "col")
NOISE = 0.1
SCALE = 0.125
COEF = SCALE * math.log2(math.e)
F32 = jnp.float32
BF16 = jnp.bfloat16

DIMS = (("y", 4), ("u", 2), ("v", 2), ("p", 2), ("x", 4), ("c", 2))
NAMES = [n for n, _ in DIMS]
IDS = np.arange(256).reshape([s for _, s in DIMS])
FAR = (("v",), ("u",), ("u", "v"))


def swap(*names):
    target = np.flip(IDS, [NAMES.index(n) for n in names])
    return list(zip(IDS.reshape(-1).tolist(), target.reshape(-1).tolist()))


def groups_over(*names):
    rest = [n for n in NAMES if n not in names]
    order = [NAMES.index(n) for n in rest + list(names)]
    size = int(np.prod([dict(DIMS)[n] for n in names]))
    return IDS.transpose(order).reshape(-1, size).tolist()


def split3(value):
    first = value.astype(BF16).astype(F32)
    rest = value - first
    second = rest.astype(BF16).astype(F32)
    return first, second, (rest - second).astype(BF16).astype(F32)


def norm_rows(points, norm_first):
    norm = -COEF * jnp.sum(points * points, axis=0, keepdims=True)
    parts = split3(norm)
    index = lax.broadcasted_iota(jnp.int32, points.shape, 0)
    base = 0 if norm_first else 3
    ones = 3 - base
    rows = jnp.where((index >= ones) & (index < ones + 3), 1.0, 0.0)
    for k in range(3):
        rows = jnp.where(index == base + k, parts[k], rows)
    return rows


def left_rows(points):
    a, b, c = split3(points * (2.0 * COEF))
    return jnp.concatenate(
        [a, a, b, b, a, c, norm_rows(points, True), jnp.zeros_like(a)], axis=0
    )


def right_rows(points):
    a, b, c = split3(points)
    return jnp.concatenate(
        [a, b, a, b, c, a, norm_rows(points, False), jnp.zeros_like(a)], axis=0
    )


def pad_rows(value, rows):
    return jnp.concatenate(
        [value, jnp.zeros((rows - value.shape[0], value.shape[1]), value.dtype)], axis=0
    )


def tile_rows(left_ref, right_ref, vectors_ref, high_ref, low_ref, total_ref):
    count, width = high_ref.shape
    for column in range(0, width, 512):
        across = slice(column, column + 512)
        right, vectors = right_ref[:, across], vectors_ref[across, :]
        for row in range(0, count, 512):
            down = slice(row, row + 512)
            kernel = jnp.exp2(jnp.dot(left_ref[down, :], right, preferred_element_type=F32))
            high = kernel.astype(BF16)
            low = (kernel - high.astype(F32)).astype(BF16)
            high_ref[down, across] = high
            low_ref[down, across] = low
            part = jnp.dot(high, vectors, preferred_element_type=F32) + jnp.dot(
                low, vectors, preferred_element_type=F32
            )
            total_ref[down, :] = part if column == 0 else total_ref[down, :] + part


def sum_parts(total):
    return total[0:17] + total[32:49] + total[64:81]


def first_kernel(
    own_ref, by_c_ref, by_p_ref, v_ref, u_ref, uv_ref, columns_ref,
    high_ref, low_ref, out_ref, right_ref, vectors_ref, near_ref, next_ref,
    left_ref, total_ref,
):
    blocks = [
        jnp.concatenate([own_ref[...], by_c_ref[...], by_p_ref[...]], axis=1),
        v_ref[...], u_ref[...], uv_ref[...],
    ]
    for far in range(4):
        rows = left_rows(blocks[far]).T.astype(BF16)
        at = far * 128
        near_ref[at : at + 128, :] = rows[0:128, :]
        next_ref[at : at + 128, :] = rows[256:384, :]
        left_ref[at : at + 128, :] = rows[128:256, :]
        left_ref[512 + at : 640 + at, :] = rows[384:512, :]
    for group in range(4):
        block = jnp.concatenate([columns_ref[group * 4 + k] for k in range(4)], axis=1)
        at = slice(group * 512, group * 512 + 512)
        right_ref[:, at] = right_rows(block[:16]).astype(BF16)
        parts = [pad_rows(part, 32) for part in split3(block[16:])]
        vectors = pad_rows(jnp.concatenate(parts, axis=0), 128)
        vectors_ref[at, :] = vectors.T.astype(BF16)
    tile_rows(left_ref, right_ref, vectors_ref, high_ref, low_ref, total_ref)
    out_ref[...] = sum_parts(total_ref[...].T)


def more_kernel(left_ref, right_ref, vectors_ref, high_ref, low_ref, out_ref, total_ref):
    tile_rows(left_ref, right_ref, vectors_ref, high_ref, low_ref, total_ref)
    out_ref[...] = sum_parts(total_ref[...].T)


def transposed_kernel(image_ref, high_ref, low_ref, *rest_refs):
    out_ref = rest_refs[-1]
    left = jnp.concatenate(
        [pad_rows(part, 32) for part in split3(image_ref[...])], axis=0
    ).astype(BF16)
    total = jnp.dot(left, high_ref[...], preferred_element_type=F32) + jnp.dot(
        left, low_ref[...], preferred_element_type=F32
    )
    total = sum_parts(total)
    for k in range(16):
        piece = total[:, k * 128 : (k + 1) * 128]
        out_ref[k] = piece if len(rest_refs) == 1 else rest_refs[0][k] + piece


def dots_kernel(parts_ref, sides_ref, image_ref, out_first_ref, out_second_ref, dots_ref):
    sides = sides_ref[...]
    image = image_ref[:, :128]
    first = image - sides
    second = jnp.sum(parts_ref[...], axis=0) - image - first
    out_first_ref[...] = first
    out_second_ref[...] = second
    rows = jnp.concatenate(
        [pad_rows(t, 32) for t in (sides * sides, sides * first, first * first, first * second)],
        axis=0,
    )
    dots = jnp.sum(rows.T, axis=0, keepdims=True)
    dots_ref[...] = jnp.broadcast_to(dots[None], dots_ref.shape)


def last_kernel(dots_ref, sides_ref, first_ref, second_ref, solution_ref, residual_ref):
    dots = jnp.sum(dots_ref[...], axis=0)
    table = jnp.broadcast_to(dots, (128, 128)).T
    g0, g1, g2, g3 = (table[32 * k : 32 * k + 17] for k in range(4))
    diagonal = 1.0 + NOISE
    sides, first, second = sides_ref[...], first_ref[...], second_ref[...]
    step = g0 / (g1 + diagonal * g0)
    ratio = g1 / g0
    residual = step * (ratio * sides - first)
    norm = step * step * (g2 - ratio * g1)
    turn = norm / g0
    weight = step * ratio + turn
    direction = residual + turn * sides
    curve = (
        weight * weight * g1
        - 2.0 * weight * step * g2
        + step * step * g3
        + diagonal * (norm + turn * turn * g0)
    )
    step_next = norm / curve
    mapped = weight * first - step * second + diagonal * direction
    solution_ref[...] = step * sides + step_next * direction
    residual_ref[...] = residual - step_next * mapped


VMEM = pl.BlockSpec(memory_space=pltpu.VMEM)


def call(kernel, name, out_shape, scratch=(), flops=0, transcendentals=0):
    return pl.pallas_call(
        kernel,
        out_shape=out_shape,
        scratch_shapes=scratch,
        compiler_params=pltpu.CompilerParams(vmem_limit_bytes=28 * 1024 * 1024),
        cost_estimate=pl.CostEstimate(
            flops=flops, bytes_accessed=0, transcendentals=transcendentals
        ),
        name=name,
    )


def per_device(points, right_sides):
    permute = functools.partial(lax.ppermute, axis_name=AXES)
    exchange = functools.partial(
        lax.all_to_all, axis_name=AXES, split_axis=0, concat_axis=0, tiled=True
    )
    column_groups = groups_over("y", "x")
    swap_c, swap_p = swap("c"), swap("p")
    swap_far = [swap(*names) for names in FAR]

    by_c = permute(points, perm=swap_c)
    pair = jnp.concatenate([points, by_c], axis=1)
    by_p = permute(pair, perm=swap_p)
    four = jnp.concatenate([pair, by_p], axis=1)
    by_far = [permute(four, perm=p) for p in swap_far]
    mine = jnp.concatenate([points, right_sides], axis=0)
    columns = exchange(
        jnp.broadcast_to(mine[None], (16, 33, 128)), axis_index_groups=column_groups
    )

    def shape(rows, width, dtype=F32):
        return jax.ShapeDtypeStruct((rows, width), dtype)

    def tile(rows):
        return pltpu.VMEM((rows, 2048), BF16)

    high_c, low_c, send_c, right, vectors, near, following = call(
        first_kernel,
        "first",
        [
            tile(1024), tile(1024), shape(17, 1024), shape(128, 2048, BF16),
            shape(2048, 128, BF16), shape(512, 128, BF16), shape(512, 128, BF16),
        ],
        scratch=[pltpu.VMEM((1024, 128), BF16), pltpu.VMEM((1024, 128), F32)],
        flops=1024 * 2048 * 128 * 6,
        transcendentals=1024 * 2048,
    )(points, by_c, by_p, *by_far, columns)
    more = functools.partial(
        call, more_kernel,
        out_shape=[tile(512), tile(512), shape(17, 512)],
        scratch=[pltpu.VMEM((512, 128), F32)],
        flops=512 * 2048 * 128 * 6,
        transcendentals=512 * 2048,
    )
    from_c = permute(send_c, perm=swap_c)
    high_p, low_p, send_p = more(name="second")(following, right, vectors)
    from_p = permute(send_p + from_c[:, 512:], perm=swap_p)
    high, low, keep = more(name="third")(near, right, vectors)
    share = keep + from_c[:, :512] + from_p
    image = share
    for distance, p in enumerate(swap_far, 1):
        other = permute(share, perm=p)
        image = image + jnp.concatenate(
            [other[:, (k ^ distance) * 128 : (k ^ distance) * 128 + 128] for k in range(4)],
            axis=1,
        )

    def transposed(name, rows):
        return call(
            transposed_kernel, name, jax.ShapeDtypeStruct((16, 17, 128), F32),
            flops=rows * 2048 * 128 * 4,
        )

    image_p = permute(image, perm=swap_p)
    parts = transposed("near", 512)(image, high, low)
    image_c = permute(jnp.concatenate([image, image_p], axis=1), perm=swap_c)
    parts = transposed("next", 512)(image_p, high_p, low_p, parts)
    parts = transposed("other", 1024)(image_c, high_c, low_c, parts)
    pieces = exchange(parts, axis_index_groups=column_groups)

    vector = shape(17, 128)
    first, second, dots = call(
        dots_kernel, "dots", [vector, vector, jax.ShapeDtypeStruct((256, 1, 128), F32)]
    )(pieces, right_sides, image)
    all_dots = exchange(dots)
    return call(last_kernel, "finish", [vector, vector])(
        all_dots, right_sides, first, second
    )


def solution(mesh):
    spec = P(None, ("col", "row"))
    return jax.shard_map(
        lambda p, r: tuple(per_device(p, r)),
        mesh=mesh,
        in_specs=(spec, spec),
        out_specs=(spec, spec),
        check_vma=False,
    )
```

time: 121 us -> 95.5 us (0.79)
  Pallas kernels: 27.9 us -> 13.4 us
  blocking collectives: 40.8 us -> 34.6 us
  waiting for transfers between devices: 17.7 us -> 12.2 us
    pallas_call x4 -> x8, Pallas kernels: 27.9 us -> 13.4 us  [the longest x1 3.92 us: per_device(): call(first_kernel, 'first', [tile(1024), tile(1024), shape(17, 1024), sha...]
    all_to_all x1, starting transfers between devices: 11.7 us -> 5.02 us  [per_device(): exchange(jnp.broadcast_to(mine[None], (16, 33, 128)), axis_index_groups=c...]
    all_to_all x2, blocking collectives: 40.8 us -> 34.6 us  [the longest x1 20 us: per_device(): all_dots = exchange(dots)]
    ppermute x8, starting transfers between devices: 11.9 us -> 16.8 us  [the longest x3 7.65 us: per_device(): by_far = [permute(four, perm=p) for p in swap_far]]
    ppermute x1, starting transfers between devices: 1.04 us -> 3.33 us  [per_device(): by_c = permute(points, perm=swap_c)]
    ppermute x1, waiting for transfers between devices: 3.67 us -> 1.42 us  [per_device(): by_p = permute(pair, perm=swap_p)]
    ppermute x1, starting transfers between devices: 4.05 us -> 2.16 us  [per_device(): image_c = permute(jnp.concatenate([image, image_p], axis=1), perm=swap_c)]
    ppermute x1, starting transfers between devices: 0.09 us -> 1.53 us  [per_device(): image_p = permute(image, perm=swap_p)]
  transfers between devices with their start and end apart: 13 -> 13, of which waited for: 11 -> 6; matrix products, arithmetic and copies ran while one was open for 1% -> 3% of each run, Pallas kernels for 0% -> 7%
where the time goes in v2:
time: 95.5 us; the launch traced here: 95 us
  blocking collectives  34.6 us (36%)
  starting transfers between devices  30.4 us (32%)
  Pallas kernels  13.4 us (14%)
  waiting for transfers between devices  12.2 us (13%)
  local copies, waits for them, and re-layouts  2.16 us (2%)
  other arithmetic  1.47 us (2%)
    all_to_all x1, blocking collectives, per_device(): all_dots = exchange(dots)  20 us
    all_to_all x1, blocking collectives, per_device(): pieces = exchange(parts, axis_index_groups=column_groups)  14.5 us
    ppermute x3, starting transfers between devices, per_device(): by_far = [permute(four, perm=p) for p in swap_far]  7.65 us
    ppermute x3, starting transfers between devices, per_device(): other = permute(share, perm=p)  5.74 us
    all_to_all x1, starting transfers between devices, per_device(): exchange(jnp.broadcast_to(mine[None], (16, 33, 128)), axis_index_groups=c...  5.02 us
    ppermute x3, waiting for transfers between devices, per_device(): by_far = [permute(four, perm=p) for p in swap_far]  5.01 us
    ppermute x3, waiting for transfers between devices, per_device(): other = permute(share, perm=p)  4.3 us
    pallas_call x1, Pallas kernels, per_device(): call(first_kernel, 'first', [tile(1024), tile(1024), shape(17, 1024), sha...  3.92 us
  transfers between devices with their start and end apart: 13, of which 6 were waited for; matrix products, arithmetic and copies ran while one was open for 3% of the time, Pallas kernels for 7%

profile of v2, /device:TPU:1, one launch (start us, length us, event | category | flops | bytes accessed | tf_op | source)
XLA Modules:
  0.0 95.0 jit_solution(16826488864386546004)
XLA Ops:
  0.6 3.3 %collective-permute-start = (f32[16,128]{1,0:T(8,128)}, f32[16,128]{1,0:T(8,128)S(1)}, u32[]{:S(2)}, u32[]{:S(2)}) collective-permute-start(f32[16,128]{1,0:T(8,128)} %own_ref.1), channel_id=1, source_target_pairs={{0,1},{1,0},{2,3},{3,2},{4,5},{5,4},{6,7},{7,6},{8,9},{9,8},{10,11... | collective-permute-start | bytes 24584 | tf_op jit(solution)/shard_map/ppermute | solution.py:209
  4.0 0.7 pad_maximum_fusion.1
  4.7 0.7 broadcast_in_dim.2
  5.4 5.0 %all-to-all-start = ((f32[16,33,128]{2,1,0:T(8,128)}), f32[16,33,128]{2,1,0:T(8,128)S(1)}, u32[]{:S(2)}, u32[]{:S(2)}) async-start(f32[16,33,128]{2,1,0:T(8,128)} %broadcast_in_dim.2), calls=%async_computation | async-start | bytes 655360 | tf_op jit(solution)/shard_map/all_to_all | solution.py:215
  10.4 0.7 constant_dynamic-update-slice_fusion.2
  11.1 0.0 collective-permute-done.by_c_ref
  11.2 0.7 pad_maximum_fusion.2
  11.9 1.6 %collective-permute-start.1 = (f32[16,256]{1,0:T(8,128)S(1)}, f32[16,256]{1,0:T(8,128)S(1)}, u32[]{:S(2)}, u32[]{:S(2)}) collective-permute-start(f32[16,256]{1,0:T(8,128)S(1)} %pad_maximum_fusion.2), channel_id=1, source_target_pairs={{0,8},{1,9},{2,10},{3,11},{4,12},{5,13},{6,14},{7,15},{8,0},{9,1},... | collective-permute-start | bytes 49160 | tf_op jit(solution)/shard_map/ppermute | solution.py:211
  13.5 1.4 %collective-permute-done.1.by_p_ref = f32[16,256]{1,0:T(8,128)S(1)} collective-permute-done((f32[16,256]{1,0:T(8,128)S(1)}, f32[16,256]{1,0:T(8,128)S(1)}, u32[]{:S(2)}, u32[]{:S(2)}) %collective-permute-start.1) | collective-permute-done | bytes 16416 | tf_op jit(solution)/shard_map/ppermute | solution.py:211
  14.9 5.6 %collective-permute-start.4 = (f32[16,512]{1,0:T(8,128)S(1)}, f32[16,512]{1,0:T(8,128)S(1)}, u32[]{:S(2)}, u32[]{:S(2)}) collective-permute-start(f32[16,512]{1,0:T(8,128)S(1)} %constant_dynamic-update-slice_fusion), channel_id=1, source_target_pairs={{0,48},{1,49},{2,50},{3,51},{4,52},{5,53},{6,54},{7,55},{8,56},{9,... | collective-permute-start | bytes 98312 | tf_op jit(solution)/shard_map/ppermute | solution.py:213
  20.5 0.9 collective-permute-start.3
  21.4 1.2 %collective-permute-start.2 = (f32[16,512]{1,0:T(8,128)S(1)}, f32[16,512]{1,0:T(8,128)S(1)}, u32[]{:S(2)}, u32[]{:S(2)}) collective-permute-start(f32[16,512]{1,0:T(8,128)S(1)} %constant_dynamic-update-slice_fusion), channel_id=1, source_target_pairs={{0,16},{1,17},{2,18},{3,19},{4,20},{5,21},{6,22},{7,23},{8,24},{9,... | collective-permute-start | bytes 98312 | tf_op jit(solution)/shard_map/ppermute | solution.py:213
  22.6 0.0 collective-permute-done.4.uv_ref
  22.6 5.0 %collective-permute-done.3.u_ref = f32[16,512]{1,0:T(8,128)S(1)} collective-permute-done((f32[16,512]{1,0:T(8,128)S(1)}, f32[16,512]{1,0:T(8,128)S(1)}, u32[]{:S(2)}, u32[]{:S(2)}) %collective-permute-start.3) | collective-permute-done | bytes 32800 | tf_op jit(solution)/shard_map/ppermute | solution.py:213
  27.6 0.0 collective-permute-done.2.v_ref
  27.6 0.0 all-to-all-done.columns_ref
  27.6 0.0 copy-start.1
  27.6 0.7 copy-done.1
  28.3 3.9 %first.1 = (bf16[1024,2048]{1,0:T(8,128)(2,1)S(1)}, bf16[1024,2048]{1,0:T(8,128)(2,1)S(1)}, f32[17,1024]{1,0:T(8,128)S(1)}, bf16[128,2048]{1,0:T(8,128)(2,1)S(1)...) custom-call(f32[16,128]{1,0:T(8,128)S(1)} %copy-done.1, ...), custom_call_target="tpu_custom_call" | custom-call | flops 1610612736 | tf_op jit(solution)/shard_map/first/pallas_call | solution.py:225
  32.2 2.5 %collective-permute-start.5 = (f32[17,1024]{1,0:T(8,128)S(1)}, f32[17,1024]{1,0:T(8,128)S(1)}, u32[]{:S(2)}, u32[]{:S(2)}) collective-permute-start(f32[17,1024]{1,0:T(8,128)S(1)} %get-tuple-element.22), channel_id=1, source_target_pairs={{0,1},{1,0},{2,3},{3,2},{4,5},{5,4},{6,7},{7,6},{8,9},{9,8},{10,11... | collective-permute-start | bytes 208904 | tf_op jit(solution)/shard_map/ppermute | solution.py:243
  34.7 2.6 %second.1 = (bf16[512,2048]{1,0:T(8,128)(2,1)S(1)}, bf16[512,2048]{1,0:T(8,128)(2,1)S(1)}, f32[17,512]{1,0:T(8,128)S(1)}) custom-call(bf16[512,128]{1,0:T(8,128)(2,1)S(1)} %get-tuple-element.23.left_ref, bf16[128,2048]{1,0:T(8,128)(2,1)S(1)} %get-tuple-element.19.right_ref, bf16[2048,128]{1,0:T(8,128)(2,1)S(1)} %get-tuple-element.20.vectors_ref), custom_call_target="tpu_custom_call" | custom-call | flops 805306368 | tf_op jit(solution)/shard_map/second/pallas_call | solution.py:244
  37.4 0.0 collective-permute-done.5
  37.4 0.8 collective-permute-start.6
  38.3 2.6 %third.1 = (bf16[512,2048]{1,0:T(8,128)(2,1)S(1)}, bf16[512,2048]{1,0:T(8,128)(2,1)S(1)}, f32[17,512]{1,0:T(8,128)S(1)}) custom-call(bf16[512,128]{1,0:T(8,128)(2,1)S(1)} %get-tuple-element.18.left_ref, bf16[128,2048]{1,0:T(8,128)(2,1)S(1)} %get-tuple-element.19.right_ref, bf16[2048,128]{1,0:T(8,128)(2,1)S(1)} %get-tuple-element.20.vectors_ref), custom_call_target="tpu_custom_call" | custom-call | flops 805306368 | tf_op jit(solution)/shard_map/third/pallas_call | solution.py:246
  40.9 0.0 collective-permute-done.6
  40.9 2.7 %collective-permute-start.8 = (f32[17,512]{1,0:T(8,128)S(1)}, f32[17,512]{1,0:T(8,128)S(1)}, u32[]{:S(2)}, u32[]{:S(2)}) collective-permute-start(f32[17,512]{1,0:T(8,128)S(1)} %fusion), channel_id=1, source_target_pairs={{0,32},{1,33},{2,34},{3,35},{4,36},{5,37},{6,38},{7,39},{8,40},{9,... | collective-permute-start | bytes 104456 | tf_op jit(solution)/shard_map/ppermute | solution.py:250
  43.7 2.2 %collective-permute-start.9 = (f32[17,512]{1,0:T(8,128)S(1)}, f32[17,512]{1,0:T(8,128)S(1)}, u32[]{:S(2)}, u32[]{:S(2)}) collective-permute-start(f32[17,512]{1,0:T(8,128)S(1)} %fusion), channel_id=1, source_target_pairs={{0,48},{1,49},{2,50},{3,51},{4,52},{5,53},{6,54},{7,55},{8,56},{9,... | collective-permute-start | bytes 104456 | tf_op jit(solution)/shard_map/ppermute | solution.py:250
  45.8 0.9 collective-permute-start.7
  46.7 1.2 %collective-permute-done.8 = f32[17,512]{1,0:T(8,128)S(1)} collective-permute-done((f32[17,512]{1,0:T(8,128)S(1)}, f32[17,512]{1,0:T(8,128)S(1)}, u32[]{:S(2)}, u32[]{:S(2)}) %collective-permute-start.8) | collective-permute-done | bytes 34848 | tf_op jit(solution)/shard_map/ppermute | solution.py:250
  47.9 1.6 %collective-permute-done.9 = f32[17,512]{1,0:T(8,128)S(1)} collective-permute-done((f32[17,512]{1,0:T(8,128)S(1)}, f32[17,512]{1,0:T(8,128)S(1)}, u32[]{:S(2)}, u32[]{:S(2)}) %collective-permute-start.9) | collective-permute-done | bytes 34848 | tf_op jit(solution)/shard_map/ppermute | solution.py:250
  49.6 1.4 %collective-permute-done.7 = f32[17,512]{1,0:T(8,128)S(1)} collective-permute-done((f32[17,512]{1,0:T(8,128)S(1)}, f32[17,512]{1,0:T(8,128)S(1)}, u32[]{:S(2)}, u32[]{:S(2)}) %collective-permute-start.7) | collective-permute-done | bytes 34848 | tf_op jit(solution)/shard_map/ppermute | solution.py:250
  51.0 1.5 %collective-permute-start.10 = (f32[17,512]{1,0:T(8,128)S(1)}, f32[17,512]{1,0:T(8,128)S(1)}, u32[]{:S(2)}, u32[]{:S(2)}) collective-permute-start(f32[17,512]{1,0:T(8,128)S(1)} %fusion.2.image_ref), channel_id=1, source_target_pairs={{0,8},{1,9},{2,10},{3,11},{4,12},{5,13},{6,14},{7,15},{8,0},{9,1},... | collective-permute-start | bytes 104456 | tf_op jit(solution)/shard_map/ppermute | solution.py:262
  52.6 1.5 %collective-permute-done.10.image_ref = f32[17,512]{1,0:T(8,128)S(1)} collective-permute-done((f32[17,512]{1,0:T(8,128)S(1)}, f32[17,512]{1,0:T(8,128)S(1)}, u32[]{:S(2)}, u32[]{:S(2)}) %collective-permute-start.10) | collective-permute-done | bytes 34848 | tf_op jit(solution)/shard_map/ppermute | solution.py:262
  54.1 2.2 %collective-permute-start.11 = (f32[17,1024]{1,0:T(8,128)S(1)}, f32[17,1024]{1,0:T(8,128)S(1)}, u32[]{:S(2)}, u32[]{:S(2)}) collective-permute-start(f32[17,1024]{1,0:T(8,128)S(1)} %pad_maximum_fusion), channel_id=1, source_target_pairs={{0,1},{1,0},{2,3},{3,2},{4,5},{5,4},{6,7},{7,6},{8,9},{9,8},{10,11... | collective-permute-start | bytes 208904 | tf_op jit(solution)/shard_map/ppermute | solution.py:264
  56.2 0.8 near.1.rest_refs_0_
  57.0 0.8 next.1.rest_refs_0_
  57.8 0.0 collective-permute-done.11.image_ref
  57.8 0.0 copy-start
  57.9 1.4 %other.1 = f32[16,17,128]{2,1,0:T(8,128)S(1)} custom-call(f32[17,1024]{1,0:T(8,128)S(1)} %collective-permute-done.11.image_ref, bf16[1024,2048]{1,0:T(8,128)(2,1)S(1)} %get-tuple-element.25.high_ref, bf16[1024,2048]{1,0:T(8,128)(2,1)S(1)} %get-tuple-element.26.low_ref, f32[16,17,128]{2,1,0:T(8,128)S(1)} %next.1.rest_refs_0_), custom_call_target="tpu_custom_call" | custom-call | flops 1073741824 | tf_op jit(solution)/shard_map/other/pallas_call | solution.py:266
  59.3 14.5 %all_to_all.15.parts_ref = f32[16,17,128]{2,1,0:T(8,128)S(1)} all-to-all(f32[16,17,128]{2,1,0:T(8,128)S(1)} %other.1), channel_id=1, replica_groups={{0,2,4,6,64,66,68,70,128,130,132,134,192,194,196,198},{1,3,5,7,65,67,69..., dimensions={0} | all-to-all | bytes 278528 | tf_op jit(solution)/shard_map/all_to_all | solution.py:267
  73.8 0.0 copy-done
  73.8 0.2 dots.1
  74.0 20.0 %all_to_all.16.dots_ref = f32[256,1,128]{2,1,0:T(1,128)S(1)} all-to-all(f32[256,1,128]{2,1,0:T(1,128)S(1)} %get-tuple-element.31), channel_id=1, replica_groups=mesh['row'=32,'col'=8] {'row','col'}, dimensions={0} | all-to-all | bytes 262144 | tf_op jit(solution)/shard_map/all_to_all | solution.py:273
  94.1 1.0 %finish.1 = (f32[17,128]{1,0:T(8,128)}, f32[17,128]{1,0:T(8,128)}) custom-call(f32[256,1,128]{2,1,0:T(1,128)S(1)} %all_to_all.16.dots_ref, f32[17,128]{1,0:T(8,128)S(1)} %copy-done, f32[17,128]{1,0:T(8,128)S(1)} %get-tuple-element.32.first_ref, f32[17,128]{1,0:T(8,128)S(1)} %get-tuple-element.33.second_ref), custom_call_target="tpu_custom_call" | custom-call | tf_op jit(solution)/shard_map/finish/pallas_call | solution.py:274
  (9 shorter events, 0.1 us)
Async XLA Ops:
  0.6 10.5 %collective-permute-start = (f32[16,128]{1,0:T(8,128)}, f32[16,128]{1,0:T(8,128)S(1)}, u32[]{:S(2)}, u32[]{:S(2)}) collective-permute-start(f32[16,128]{1,0:T(8,128)} %own_ref.1), channel_id=1, source_target_pairs={{0,1},{1,0},{2,3},{3,2},{4,5},{5,4},{6,7},{7,6},{8,9},{9,8},{10,11... | collective-permute-start | bytes 24584 | tf_op jit(solution)/shard_map/ppermute | solution.py:209
  5.4 22.2 %all-to-all-start = ((f32[16,33,128]{2,1,0:T(8,128)}), f32[16,33,128]{2,1,0:T(8,128)S(1)}, u32[]{:S(2)}, u32[]{:S(2)}) async-start(f32[16,33,128]{2,1,0:T(8,128)} %broadcast_in_dim.2), calls=%async_computation | async-start | bytes 655360 | tf_op jit(solution)/shard_map/all_to_all | solution.py:215
  11.9 3.1 %collective-permute-start.1 = (f32[16,256]{1,0:T(8,128)S(1)}, f32[16,256]{1,0:T(8,128)S(1)}, u32[]{:S(2)}, u32[]{:S(2)}) collective-permute-start(f32[16,256]{1,0:T(8,128)S(1)} %pad_maximum_fusion.2), channel_id=1, source_target_pairs={{0,8},{1,9},{2,10},{3,11},{4,12},{5,13},{6,14},{7,15},{8,0},{9,1},... | collective-permute-start | bytes 49160 | tf_op jit(solution)/shard_map/ppermute | solution.py:211
  14.9 7.7 %collective-permute-start.4 = (f32[16,512]{1,0:T(8,128)S(1)}, f32[16,512]{1,0:T(8,128)S(1)}, u32[]{:S(2)}, u32[]{:S(2)}) collective-permute-start(f32[16,512]{1,0:T(8,128)S(1)} %constant_dynamic-update-slice_fusion), channel_id=1, source_target_pairs={{0,48},{1,49},{2,50},{3,51},{4,52},{5,53},{6,54},{7,55},{8,56},{9,... | collective-permute-start | bytes 98312 | tf_op jit(solution)/shard_map/ppermute | solution.py:213
  20.5 7.1 %collective-permute-start.3 = (f32[16,512]{1,0:T(8,128)S(1)}, f32[16,512]{1,0:T(8,128)S(1)}, u32[]{:S(2)}, u32[]{:S(2)}) collective-permute-start(f32[16,512]{1,0:T(8,128)S(1)} %constant_dynamic-update-slice_fusion), channel_id=1, source_target_pairs={{0,32},{1,33},{2,34},{3,35},{4,36},{5,37},{6,38},{7,39},{8,40},{9,... | collective-permute-start | bytes 98312 | tf_op jit(solution)/shard_map/ppermute | solution.py:213
  21.4 6.2 %collective-permute-start.2 = (f32[16,512]{1,0:T(8,128)S(1)}, f32[16,512]{1,0:T(8,128)S(1)}, u32[]{:S(2)}, u32[]{:S(2)}) collective-permute-start(f32[16,512]{1,0:T(8,128)S(1)} %constant_dynamic-update-slice_fusion), channel_id=1, source_target_pairs={{0,16},{1,17},{2,18},{3,19},{4,20},{5,21},{6,22},{7,23},{8,24},{9,... | collective-permute-start | bytes 98312 | tf_op jit(solution)/shard_map/ppermute | solution.py:213
  27.6 0.7 copy-start.1
  32.2 5.2 %collective-permute-start.5 = (f32[17,1024]{1,0:T(8,128)S(1)}, f32[17,1024]{1,0:T(8,128)S(1)}, u32[]{:S(2)}, u32[]{:S(2)}) collective-permute-start(f32[17,1024]{1,0:T(8,128)S(1)} %get-tuple-element.22), channel_id=1, source_target_pairs={{0,1},{1,0},{2,3},{3,2},{4,5},{5,4},{6,7},{7,6},{8,9},{9,8},{10,11... | collective-permute-start | bytes 208904 | tf_op jit(solution)/shard_map/ppermute | solution.py:243
  37.4 3.5 %collective-permute-start.6 = (f32[17,512]{1,0:T(8,128)S(1)}, f32[17,512]{1,0:T(8,128)S(1)}, u32[]{:S(2)}, u32[]{:S(2)}) collective-permute-start(f32[17,512]{1,0:T(8,128)S(1)} %slice_add_fusion), channel_id=1, source_target_pairs={{0,8},{1,9},{2,10},{3,11},{4,12},{5,13},{6,14},{7,15},{8,0},{9,1},... | collective-permute-start | bytes 104456 | tf_op jit(solution)/shard_map/ppermute | solution.py:245
  40.9 7.0 %collective-permute-start.8 = (f32[17,512]{1,0:T(8,128)S(1)}, f32[17,512]{1,0:T(8,128)S(1)}, u32[]{:S(2)}, u32[]{:S(2)}) collective-permute-start(f32[17,512]{1,0:T(8,128)S(1)} %fusion), channel_id=1, source_target_pairs={{0,32},{1,33},{2,34},{3,35},{4,36},{5,37},{6,38},{7,39},{8,40},{9,... | collective-permute-start | bytes 104456 | tf_op jit(solution)/shard_map/ppermute | solution.py:250
  43.7 5.9 %collective-permute-start.9 = (f32[17,512]{1,0:T(8,128)S(1)}, f32[17,512]{1,0:T(8,128)S(1)}, u32[]{:S(2)}, u32[]{:S(2)}) collective-permute-start(f32[17,512]{1,0:T(8,128)S(1)} %fusion), channel_id=1, source_target_pairs={{0,48},{1,49},{2,50},{3,51},{4,52},{5,53},{6,54},{7,55},{8,56},{9,... | collective-permute-start | bytes 104456 | tf_op jit(solution)/shard_map/ppermute | solution.py:250
  45.8 5.2 %collective-permute-start.7 = (f32[17,512]{1,0:T(8,128)S(1)}, f32[17,512]{1,0:T(8,128)S(1)}, u32[]{:S(2)}, u32[]{:S(2)}) collective-permute-start(f32[17,512]{1,0:T(8,128)S(1)} %fusion), channel_id=1, source_target_pairs={{0,16},{1,17},{2,18},{3,19},{4,20},{5,21},{6,22},{7,23},{8,24},{9,... | collective-permute-start | bytes 104456 | tf_op jit(solution)/shard_map/ppermute | solution.py:250
  51.0 3.0 %collective-permute-start.10 = (f32[17,512]{1,0:T(8,128)S(1)}, f32[17,512]{1,0:T(8,128)S(1)}, u32[]{:S(2)}, u32[]{:S(2)}) collective-permute-start(f32[17,512]{1,0:T(8,128)S(1)} %fusion.2.image_ref), channel_id=1, source_target_pairs={{0,8},{1,9},{2,10},{3,11},{4,12},{5,13},{6,14},{7,15},{8,0},{9,1},... | collective-permute-start | bytes 104456 | tf_op jit(solution)/shard_map/ppermute | solution.py:262
  54.1 3.8 %collective-permute-start.11 = (f32[17,1024]{1,0:T(8,128)S(1)}, f32[17,1024]{1,0:T(8,128)S(1)}, u32[]{:S(2)}, u32[]{:S(2)}) collective-permute-start(f32[17,1024]{1,0:T(8,128)S(1)} %pad_maximum_fusion), channel_id=1, source_target_pairs={{0,1},{1,0},{2,3},{3,2},{4,5},{5,4},{6,7},{7,6},{8,9},{9,8},{10,11... | collective-permute-start | bytes 208904 | tf_op jit(solution)/shard_map/ppermute | solution.py:264
  57.8 16.0 %copy-start = (f32[17,128]{1,0:T(8,128)S(1)}, f32[17,128]{1,0:T(8,128)}, u32[]{:S(2)}) copy-start(f32[17,128]{1,0:T(8,128)} %sides_ref.3) | copy-start | bytes 26116

commit v3 on v2

v3 whole, which is shorter than its diff:
```python
import functools
import math

import jax
import jax.numpy as jnp
import numpy as np
from jax import lax
from jax.experimental import pallas as pl
from jax.experimental.pallas import tpu as pltpu
from jax.sharding import PartitionSpec as P

AXES = ("row", "col")
NOISE = 0.1
SCALE = 0.125
COEF = SCALE * math.log2(math.e)
F32 = jnp.float32
BF16 = jnp.bfloat16

DIMS = (("y", 4), ("u", 2), ("v", 2), ("p", 2), ("x", 4), ("c", 2))
NAMES = [n for n, _ in DIMS]
IDS = np.arange(256).reshape([s for _, s in DIMS])


def swap(*names):
    target = np.flip(IDS, [NAMES.index(n) for n in names])
    return list(zip(IDS.reshape(-1).tolist(), target.reshape(-1).tolist()))


def groups_over(*names):
    rest = [n for n in NAMES if n not in names]
    order = [NAMES.index(n) for n in rest + list(names)]
    size = int(np.prod([dict(DIMS)[n] for n in names]))
    return IDS.transpose(order).reshape(-1, size).tolist()


def split3(value):
    first = value.astype(BF16).astype(F32)
    rest = value - first
    second = rest.astype(BF16).astype(F32)
    return first, second, (rest - second).astype(BF16).astype(F32)


def norm_rows(points, norm_first):
    norm = -COEF * jnp.sum(points * points, axis=0, keepdims=True)
    parts = split3(norm)
    index = lax.broadcasted_iota(jnp.int32, points.shape, 0)
    base = 0 if norm_first else 3
    ones = 3 - base
    rows = jnp.where((index >= ones) & (index < ones + 3), 1.0, 0.0)
    for k in range(3):
        rows = jnp.where(index == base + k, parts[k], rows)
    return rows


def left_rows(points):
    a, b, c = split3(points * (2.0 * COEF))
    return jnp.concatenate(
        [a, a, b, b, a, c, norm_rows(points, True), jnp.zeros_like(a)], axis=0
    )


def right_rows(points):
    a, b, c = split3(points)
    return jnp.concatenate(
        [a, b, a, b, c, a, norm_rows(points, False), jnp.zeros_like(a)], axis=0
    )


def pad_rows(value, rows):
    return jnp.concatenate(
        [value, jnp.zeros((rows - value.shape[0], value.shape[1]), value.dtype)], axis=0
    )


def tile_rows(left_ref, right_ref, vectors_ref, high_ref, low_ref):
    contract = (((1,), (1,)), ((), ()))
    total = None
    for column in range(0, 2048, 1024):
        across = slice(column, column + 1024)
        kernel = jnp.exp2(
            jnp.dot(left_ref[...], right_ref[:, across], preferred_element_type=F32)
        )
        high = kernel.astype(BF16)
        low = (kernel - high.astype(F32)).astype(BF16)
        high_ref[:, across] = high
        low_ref[:, across] = low
        for part in (high, low):
            product = lax.dot_general(
                vectors_ref[:, across], part, contract, preferred_element_type=F32
            )
            total = product if total is None else total + product
    return sum_parts(total)


def sum_parts(total):
    return total[0:17] + total[32:49] + total[64:81]


def spread_kernel(points_hbm, sides_hbm, points_ref, sides_ref, copies_ref, done):
    copies = [
        pltpu.make_async_copy(points_hbm, points_ref, done.at[0]),
        pltpu.make_async_copy(sides_hbm, sides_ref, done.at[1]),
    ]
    for copy in copies:
        copy.start()
    for copy in copies:
        copy.wait()
    both = jnp.concatenate([points_ref[...], sides_ref[...]], axis=0)
    copies_ref[...] = jnp.broadcast_to(both[None], copies_ref.shape)


def make_left(points_ref, left_ref):
    left_ref[...] = left_rows(points_ref[...]).T.astype(BF16)


def make_right(columns_ref, right_ref, vectors_ref):
    for group in range(4):
        block = jnp.concatenate([columns_ref[group * 4 + k] for k in range(4)], axis=1)
        at = slice(group * 512, group * 512 + 512)
        right_ref[:, at] = right_rows(block[:16]).astype(BF16)
        parts = [pad_rows(part, 32) for part in split3(block[16:])]
        vectors_ref[:, at] = jnp.concatenate(parts, axis=0).astype(BF16)


def near_own_kernel(
    points_ref, columns_ref, high_ref, low_ref, out_ref, left_ref, right_ref, vectors_ref
):
    make_left(points_ref, left_ref)
    make_right(columns_ref, right_ref, vectors_ref)
    out_ref[...] = tile_rows(left_ref, right_ref, vectors_ref, high_ref, low_ref)


def next_own_kernel(
    points_ref, right_ref, vectors_ref, high_ref, low_ref, out_ref, left_ref
):
    make_left(points_ref, left_ref)
    out_ref[...] = tile_rows(left_ref, right_ref, vectors_ref, high_ref, low_ref)


def next_other_kernel(
    left_ref, columns_ref, before_ref, high_ref, low_ref, out_ref, right_ref, vectors_ref
):
    make_right(columns_ref, right_ref, vectors_ref)
    out_ref[...] = before_ref[...] + tile_rows(
        left_ref, right_ref, vectors_ref, high_ref, low_ref
    )


def near_other_kernel(
    left_ref, right_ref, vectors_ref, before_ref, high_ref, low_ref, out_ref
):
    out_ref[...] = before_ref[...] + tile_rows(
        left_ref, right_ref, vectors_ref, high_ref, low_ref
    )


def vector_parts(image_ref):
    return jnp.concatenate(
        [pad_rows(part, 32) for part in split3(image_ref[...])], axis=0
    ).astype(BF16)


def transposed_product(left, high_ref, low_ref):
    return sum_parts(
        jnp.dot(left, high_ref[...], preferred_element_type=F32)
        + jnp.dot(left, low_ref[...], preferred_element_type=F32)
    )


def near_transposed_kernel(
    image_ref, other_high_ref, other_low_ref, own_high_ref, own_low_ref, other_ref, own_ref
):
    left = vector_parts(image_ref)
    for high_ref, low_ref, out_ref in (
        (other_high_ref, other_low_ref, other_ref), (own_high_ref, own_low_ref, own_ref)
    ):
        total = transposed_product(left, high_ref, low_ref)
        for k in range(16):
            out_ref[k] = total[:, k * 128 : (k + 1) * 128]


def next_transposed_kernel(image_ref, high_ref, low_ref, before_ref, out_ref):
    total = transposed_product(vector_parts(image_ref), high_ref, low_ref)
    for k in range(16):
        out_ref[k] = before_ref[k] + total[:, k * 128 : (k + 1) * 128]


def dots_kernel(parts_ref, sides_ref, image_ref, out_first_ref, out_second_ref, dots_ref):
    sides = sides_ref[...]
    image = image_ref[:, :128]
    first = image - sides
    second = jnp.sum(parts_ref[...], axis=0) - image - first
    out_first_ref[...] = first
    out_second_ref[...] = second
    rows = jnp.concatenate(
        [pad_rows(t, 32) for t in (sides * sides, sides * first, first * first, first * second)],
        axis=0,
    )
    dots = jnp.sum(rows.T, axis=0, keepdims=True)
    dots_ref[...] = jnp.broadcast_to(dots[None], dots_ref.shape)


def last_kernel(dots_ref, sides_ref, first_ref, second_ref, solution_ref, residual_ref):
    dots = jnp.sum(dots_ref[...], axis=0)
    table = jnp.broadcast_to(dots, (128, 128)).T
    g0, g1, g2, g3 = (table[32 * k : 32 * k + 17] for k in range(4))
    diagonal = 1.0 + NOISE
    sides, first, second = sides_ref[...], first_ref[...], second_ref[...]
    step = g0 / (g1 + diagonal * g0)
    ratio = g1 / g0
    residual = step * (ratio * sides - first)
    norm = step * step * (g2 - ratio * g1)
    turn = norm / g0
    weight = step * ratio + turn
    direction = residual + turn * sides
    curve = (
        weight * weight * g1
        - 2.0 * weight * step * g2
        + step * step * g3
        + diagonal * (norm + turn * turn * g0)
    )
    step_next = norm / curve
    mapped = weight * first - step * second + diagonal * direction
    solution_ref[...] = step * sides + step_next * direction
    residual_ref[...] = residual - step_next * mapped


VMEM = pl.BlockSpec(memory_space=pltpu.VMEM)


def call(kernel, name, out_shape, scratch=(), flops=0, transcendentals=0):
    return pl.pallas_call(
        kernel,
        out_shape=out_shape,
        scratch_shapes=scratch,
        compiler_params=pltpu.CompilerParams(vmem_limit_bytes=28 * 1024 * 1024),
        cost_estimate=pl.CostEstimate(
            flops=flops, bytes_accessed=0, transcendentals=transcendentals
        ),
        name=name,
    )


def per_device(points, right_sides):
    permute = functools.partial(lax.ppermute, axis_name=AXES)
    exchange = functools.partial(
        lax.all_to_all, axis_name=AXES, split_axis=0, concat_axis=0, tiled=True
    )
    column_groups = groups_over("y", "x")
    swap_c, swap_p, swap_v, swap_uv = swap("c"), swap("p"), swap("v"), swap("u", "v")

    def shape(*dims, dtype=F32):
        return jax.ShapeDtypeStruct(dims, dtype)

    tiles = [pltpu.VMEM((512, 2048), BF16), pltpu.VMEM((512, 2048), BF16)]
    left_shape = shape(512, 128, dtype=BF16)
    right_shapes = [shape(128, 2048, dtype=BF16), shape(96, 2048, dtype=BF16)]
    make = functools.partial(
        call,
        flops=512 * 2048 * 128 * 6,
        transcendentals=512 * 2048,
    )

    by_v = permute(points, perm=swap_v)
    points, sides, copies = pl.pallas_call(
        spread_kernel,
        in_specs=[pl.BlockSpec(memory_space=pl.ANY)] * 2,
        out_shape=[
            pltpu.VMEM((16, 128), F32), pltpu.VMEM((17, 128), F32),
            pltpu.VMEM((16, 33, 128), F32),
        ],
        scratch_shapes=[pltpu.SemaphoreType.DMA((2,))],
        name="spread",
    )(points, right_sides)
    copies, by_v = lax.optimization_barrier((copies, by_v))
    pair = jnp.concatenate([points, by_v], axis=1)
    near_points = jnp.concatenate([pair, permute(pair, perm=swap_uv)], axis=1)
    own = exchange(copies, axis_index_groups=column_groups)

    next_points = permute(near_points, perm=swap_p)
    other = permute(own, perm=swap_c)
    *near_own, near_sum, near_left, right, vectors = make(
        near_own_kernel, "near_own",
        [*tiles, shape(17, 512), left_shape, *right_shapes],
    )(near_points, own)
    *next_own, next_sum, next_left = make(
        next_own_kernel, "next_own", [*tiles, shape(17, 512), left_shape]
    )(next_points, right, vectors)
    *next_other, next_sum, right, vectors = make(
        next_other_kernel, "next_other", [*tiles, shape(17, 512), *right_shapes]
    )(next_left, other, next_sum)
    from_p = permute(next_sum, perm=swap_p)
    *near_other, near_sum = make(
        near_other_kernel, "near_other", [*tiles, shape(17, 512)]
    )(near_left, right, vectors, near_sum)

    def turned(value, distance):
        return jnp.concatenate(
            [value[:, (k ^ distance) * 128 : (k ^ distance) * 128 + 128] for k in range(4)],
            axis=1,
        )

    total = near_sum + from_p
    total = total + turned(permute(total, perm=swap_v), 1)
    image = total + turned(permute(total, perm=swap_uv), 2)

    by_owner = shape(16, 17, 128)
    next_image = permute(image, perm=swap_p)
    other_part, own_part = call(
        near_transposed_kernel, "near_transposed", [by_owner, by_owner],
        flops=1024 * 2048 * 512,
    )(image, *near_other, *near_own)
    product = functools.partial(
        call, next_transposed_kernel, out_shape=by_owner, flops=512 * 2048 * 512
    )
    other_part = product(name="other_transposed")(next_image, *next_other, other_part)
    from_c = permute(other_part, perm=swap_c)
    own_part = product(name="own_transposed")(next_image, *next_own, own_part)
    pieces = exchange(own_part + from_c, axis_index_groups=column_groups)

    vector = shape(17, 128)
    first, second, dots = call(dots_kernel, "dots", [vector, vector, shape(256, 1, 128)])(
        pieces, sides, image
    )
    all_dots = exchange(dots)
    return call(last_kernel, "finish", [vector, vector])(
        all_dots, sides, first, second
    )


def solution(mesh):
    spec = P(None, ("col", "row"))
    return jax.shard_map(
        lambda p, r: tuple(per_device(p, r)),
        mesh=mesh,
        in_specs=(spec, spec),
        out_specs=(spec, spec),
        check_vma=False,
    )
```

time: 95.5 us -> 90.2 us (0.945)
  waiting for transfers between devices: 12.2 us -> 8.81 us
  starting transfers between devices: 30.4 us -> 33.2 us
  local copies, waits for them, and re-layouts: 2.16 us -> 0.01 us
  other arithmetic: 1.47 us -> 0.06 us
  blocking collectives: 34.6 us -> 33.3 us
    ppermute x12 -> x9, waiting for transfers between devices: 12.2 us -> 6.07 us  [the longest x1 2.01 us: per_device(): total = total + turned(permute(total, perm=swap_v), 1)]
    all_to_all x1, blocking collectives: 14.5 us -> 10.7 us  [per_device(): pieces = exchange(own_part + from_c, axis_index_groups=column_groups)]
    all_to_all x1, waiting for transfers between devices: 0.01 us -> 2.74 us  [per_device(): own = exchange(copies, axis_index_groups=column_groups)]
    all_to_all x1, blocking collectives: 20 us -> 22.6 us  [per_device(): all_dots = exchange(dots)]
    all_to_all x1, starting transfers between devices: 5.02 us -> 6.77 us  [per_device(): own = exchange(copies, axis_index_groups=column_groups)]
    concatenate x3 -> x1, other arithmetic: 1.43 us -> 0.01 us  [per_device(): pair = jnp.concatenate([points, by_v], axis=1)]
    unnamed x6 -> x2, local copies, waits for them, and re-layouts: 1.4 us -> 0.01 us
    ppermute x12 -> x9, starting transfers between devices: 25.4 us -> 26.4 us  [the longest x1 5.2 us: per_device(): near_points = jnp.concatenate([pair, permute(pair, perm=swap_uv)], axis=1)]
  transfers between devices with their start and end apart: 13 -> 10, of which waited for: 6 -> 6; matrix products, arithmetic and copies ran while one was open for 3% -> 0% of each run, Pallas kernels for 7% -> 11%
where the time goes in v3:
time: 90.2 us; the launch traced here: 89.9 us
  blocking collectives  33.3 us (37%)
  starting transfers between devices  33.2 us (37%)
  Pallas kernels  13.8 us (15%)
  waiting for transfers between devices  8.81 us (10%)
    all_to_all x1, blocking collectives, per_device(): all_dots = exchange(dots)  22.6 us
    all_to_all x1, blocking collectives, per_device(): pieces = exchange(own_part + from_c, axis_index_groups=column_groups)  10.7 us
    all_to_all x1, starting transfers between devices, per_device(): own = exchange(copies, axis_index_groups=column_groups)  6.77 us
    ppermute x1, starting transfers between devices, per_device(): near_points = jnp.concatenate([pair, permute(pair, perm=swap_uv)], axis=1)  5.2 us
    ppermute x1, starting transfers between devices, per_device(): from_c = permute(other_part, perm=swap_c)  4.96 us
    ppermute x1, starting transfers between devices, per_device(): image = total + turned(permute(total, perm=swap_uv), 2)  4.12 us
    ppermute x1, starting transfers between devices, per_device(): by_v = permute(points, perm=swap_v)  3.91 us
    all_to_all x1, waiting for transfers between devices, per_device(): own = exchange(copies, axis_index_groups=column_groups)  2.74 us
  transfers between devices with their start and end apart: 10, of which 6 were waited for; matrix products, arithmetic and copies ran while one was open for 0% of the time, Pallas kernels for 11%

profile of v3, /device:TPU:1, one launch (start us, length us, event | category | flops | bytes accessed | tf_op | source)
XLA Modules:
  0.0 89.9 jit_solution(11421354092736832987)
XLA Ops:
  0.6 3.9 %collective-permute-start = (f32[16,128]{1,0:T(8,128)}, f32[16,128]{1,0:T(8,128)S(1)}, u32[]{:S(2)}, u32[]{:S(2)}) collective-permute-start(f32[16,128]{1,0:T(8,128)} %points_hbm.1), channel_id=1, source_target_pairs={{0,16},{1,17},{2,18},{3,19},{4,20},{5,21},{6,22},{7,23},{8,24},{9,... | collective-permute-start | bytes 24584 | tf_op jit(solution)/shard_map/ppermute | solution.py:264
  4.5 1.5 %spread.1 = (f32[16,128]{1,0:T(8,128)S(1)}, f32[17,128]{1,0:T(8,128)S(1)}, f32[16,33,128]{2,1,0:T(8,128)}) custom-call(f32[16,128]{1,0:T(8,128)} %points_hbm.1, f32[17,128]{1,0:T(8,128)} %sides_hbm.1), custom_call_target="tpu_custom_call" | custom-call | tf_op jit(solution)/shard_map/spread/pallas_call | solution.py:265
  6.0 0.0 collective-permute-done
  6.0 6.8 %all-to-all-start = ((f32[16,33,128]{2,1,0:T(8,128)}), f32[16,33,128]{2,1,0:T(8,128)S(1)}, u32[]{:S(2)}, u32[]{:S(2)}) async-start(f32[16,33,128]{2,1,0:T(8,128)} %get-tuple-element.33), calls=%async_computation | async-start | bytes 655360 | tf_op jit(solution)/shard_map/all_to_all | solution.py:278
  12.8 5.2 %collective-permute-start.1 = (f32[16,256]{1,0:T(8,128)S(1)}, f32[16,256]{1,0:T(8,128)S(1)}, u32[]{:S(2)}, u32[]{:S(2)}) collective-permute-start(f32[16,256]{1,0:T(8,128)S(1)} %pad_maximum_fusion), channel_id=1, source_target_pairs={{0,48},{1,49},{2,50},{3,51},{4,52},{5,53},{6,54},{7,55},{8,56},{9,... | collective-permute-start | bytes 49160 | tf_op jit(solution)/shard_map/ppermute | solution.py:277
  18.0 2.7 %all-to-all-done.columns_ref = f32[16,33,128]{2,1,0:T(8,128)S(1)} async-done(((f32[16,33,128]{2,1,0:T(8,128)}), f32[16,33,128]{2,1,0:T(8,128)S(1)}, u32[]{:S(2)}, u32[]{:S(2)}) %all-to-all-start) | async-done | bytes 270368 | tf_op jit(solution)/shard_map/all_to_all | solution.py:278
  20.8 2.6 %collective-permute-start.3 = (f32[16,33,128]{2,1,0:T(8,128)S(1)}, f32[16,33,128]{2,1,0:T(8,128)S(1)}, u32[]{:S(2)}, u32[]{:S(2)}) collective-permute-start(f32[16,33,128]{2,1,0:T(8,128)S(1)} %all-to-all-done.columns_ref), channel_id=1, source_target_pairs={{0,1},{1,0},{2,3},{3,2},{4,5},{5,4},{6,7},{7,6},{8,9},{9,8},{10,11... | collective-permute-start | bytes 811016 | tf_op jit(solution)/shard_map/ppermute | solution.py:281
  23.4 0.0 collective-permute-done.1
  23.4 1.7 %collective-permute-start.2 = (f32[16,512]{1,0:T(8,128)S(1)}, f32[16,512]{1,0:T(8,128)S(1)}, u32[]{:S(2)}, u32[]{:S(2)}) collective-permute-start(f32[16,512]{1,0:T(8,128)S(1)} %constant_dynamic-update-slice_fusion.points_ref), channel_id=1, source_target_pairs={{0,8},{1,9},{2,10},{3,11},{4,12},{5,13},{6,14},{7,15},{8,0},{9,1},... | collective-permute-start | bytes 98312 | tf_op jit(solution)/shard_map/ppermute | solution.py:280
  25.1 2.1 %near_own.1 = (bf16[512,2048]{1,0:T(8,128)(2,1)S(1)}, bf16[512,2048]{1,0:T(8,128)(2,1)S(1)}, f32[17,512]{1,0:T(8,128)S(1)}, bf16[512,128]{1,0:T(8,128)(2,1)S(1)}...) custom-call(f32[16,512]{1,0:T(8,128)S(1)} %constant_dynamic-update-slice_fusion.points_ref, ...), custom_call_target="tpu_custom_call" | custom-call | flops 805306368 | tf_op jit(solution)/shard_map/near_own/pallas_call | solution.py:282
  27.2 0.0 collective-permute-done.2.points_ref
  27.2 2.0 %next_own.1 = (bf16[512,2048]{1,0:T(8,128)(2,1)S(1)}, bf16[512,2048]{1,0:T(8,128)(2,1)S(1)}, f32[17,512]{1,0:T(8,128)S(1)}, bf16[512,128]{1,0:T(8,128)(2,1)S(1)}) custom-call(f32[16,512]{1,0:T(8,128)S(1)} %collective-permute-done.2.points_ref, bf16[128,2048]{1,0:T(8,128)(2,1)S(1)} %get-tuple-element.35.right_ref, ...), custom_call_target="tpu_custom_call" | custom-call | flops 805306368 | tf_op jit(solution)/shard_map/next_own/pallas_call | solution.py:286
  29.3 0.0 collective-permute-done.3.columns_ref
  29.3 2.1 %next_other.1 = (bf16[512,2048]{1,0:T(8,128)(2,1)S(1)}, bf16[512,2048]{1,0:T(8,128)(2,1)S(1)}, f32[17,512]{1,0:T(8,128)S(1)}, bf16[128,2048]{1,0:T(8,128)(2,1)S(1)}, bf16[96,2048]{1,0:T(8,128)(2,1)S(1)}) custom-call(bf16[512,128]{1,0:T(8,128)(2,1)S(1)} %get-tuple-element.37.left_ref, f32[16,33,128]{2,1,0:T(8,128)S(1)} %collective-permute-done.3.columns_ref, ...), custom_call_target="tpu_custom_call" | custom-call | flops 805306368 | tf_op jit(solution)/shard_map/next_other/pallas_call | solution.py:289
  31.4 0.8 collective-permute-start.4
  32.1 2.0 %near_other.1 = (bf16[512,2048]{1,0:T(8,128)(2,1)S(1)}, bf16[512,2048]{1,0:T(8,128)(2,1)S(1)}, f32[17,512]{1,0:T(8,128)S(1)}) custom-call(bf16[512,128]{1,0:T(8,128)(2,1)S(1)} %get-tuple-element.34.left_ref, bf16[128,2048]{1,0:T(8,128)(2,1)S(1)} %get-tuple-element.39.right_ref, bf16[96,2048]{1,0:T(8,128)(2,1)S(1)} %get-tuple-element.40.vectors_ref, ...), custom_call_target="tpu_custom_call" | custom-call | flops 805306368 | tf_op jit(solution)/shard_map/near_other/pallas_call | solution.py:293
  34.2 0.3 collective-permute-done.4
  34.4 2.7 %collective-permute-start.5 = (f32[17,512]{1,0:T(8,128)S(1)}, f32[17,512]{1,0:T(8,128)S(1)}, u32[]{:S(2)}, u32[]{:S(2)}) collective-permute-start(f32[17,512]{1,0:T(8,128)S(1)} %add.12), channel_id=1, source_target_pairs={{0,16},{1,17},{2,18},{3,19},{4,20},{5,21},{6,22},{7,23},{8,24},{9,... | collective-permute-start | bytes 104456 | tf_op jit(solution)/shard_map/ppermute | solution.py:304
  37.1 2.0 %collective-permute-done.5 = f32[17,512]{1,0:T(8,128)S(1)} collective-permute-done((f32[17,512]{1,0:T(8,128)S(1)}, f32[17,512]{1,0:T(8,128)S(1)}, u32[]{:S(2)}, u32[]{:S(2)}) %collective-permute-start.5) | collective-permute-done | bytes 34848 | tf_op jit(solution)/shard_map/ppermute | solution.py:304
  39.2 4.1 %collective-permute-start.6 = (f32[17,512]{1,0:T(8,128)S(1)}, f32[17,512]{1,0:T(8,128)S(1)}, u32[]{:S(2)}, u32[]{:S(2)}) collective-permute-start(f32[17,512]{1,0:T(8,128)S(1)} %maximum_add_fusion), channel_id=1, source_target_pairs={{0,48},{1,49},{2,50},{3,51},{4,52},{5,53},{6,54},{7,55},{8,56},{9,... | collective-permute-start | bytes 104456 | tf_op jit(solution)/shard_map/ppermute | solution.py:305
  43.3 2.0 %collective-permute-done.6 = f32[17,512]{1,0:T(8,128)S(1)} collective-permute-done((f32[17,512]{1,0:T(8,128)S(1)}, f32[17,512]{1,0:T(8,128)S(1)}, u32[]{:S(2)}, u32[]{:S(2)}) %collective-permute-start.6) | collective-permute-done | bytes 34848 | tf_op jit(solution)/shard_map/ppermute | solution.py:305
  45.3 0.4 collective-permute-start.7
  45.7 1.4 %near_transposed.1 = (f32[16,17,128]{2,1,0:T(8,128)S(1)}, f32[16,17,128]{2,1,0:T(8,128)S(1)}) custom-call(f32[17,512]{1,0:T(8,128)S(1)} %maximum_add_fusion.1.image_ref, bf16[512,2048]{1,0:T(8,128)(2,1)S(1)} %get-tuple-element.46.other_high_ref, bf16[512,2048]{1,0:T(8,128)(2,1)S(1)} %get-tuple-element.47.other_low_ref, ...), custom_call_target="tpu_custom_call" | custom-call | flops 1073741824 | tf_op jit(solution)/shard_map/near_transposed/pallas_call | solution.py:309
  47.2 1.5 %collective-permute-done.7.image_ref = f32[17,512]{1,0:T(8,128)S(1)} collective-permute-done((f32[17,512]{1,0:T(8,128)S(1)}, f32[17,512]{1,0:T(8,128)S(1)}, u32[]{:S(2)}, u32[]{:S(2)}) %collective-permute-start.7) | collective-permute-done | bytes 34848 | tf_op jit(solution)/shard_map/ppermute | solution.py:308
  48.6 0.8 other_transposed.1
  49.5 5.0 %collective-permute-start.8 = (f32[16,17,128]{2,1,0:T(8,128)S(1)}, f32[16,17,128]{2,1,0:T(8,128)S(1)}, u32[]{:S(2)}, u32[]{:S(2)}) collective-permute-start(f32[16,17,128]{2,1,0:T(8,128)S(1)} %other_transposed.1), channel_id=1, source_target_pairs={{0,1},{1,0},{2,3},{3,2},{4,5},{5,4},{6,7},{7,6},{8,9},{9,8},{10,11... | collective-permute-start | bytes 417800 | tf_op jit(solution)/shard_map/ppermute | solution.py:317
  54.4 0.8 own_transposed.1
  55.2 0.3 collective-permute-done.8
  55.5 10.7 %all_to_all.15.parts_ref = f32[16,17,128]{2,1,0:T(8,128)S(1)} all-to-all(f32[16,17,128]{2,1,0:T(8,128)S(1)} %add.15), channel_id=1, replica_groups={{0,2,4,6,64,66,68,70,128,130,132,134,192,194,196,198},{1,3,5,7,65,67,69..., dimensions={0} | all-to-all | bytes 278528 | tf_op jit(solution)/shard_map/all_to_all | solution.py:319
  66.2 0.2 dots.1
  66.4 22.6 %all_to_all.16.dots_ref = f32[256,1,128]{2,1,0:T(1,128)S(1)} all-to-all(f32[256,1,128]{2,1,0:T(1,128)S(1)} %get-tuple-element.55), channel_id=1, replica_groups=mesh['row'=32,'col'=8] {'row','col'}, dimensions={0} | all-to-all | bytes 262144 | tf_op jit(solution)/shard_map/all_to_all | solution.py:325
  88.9 1.0 %finish.1 = (f32[17,128]{1,0:T(8,128)}, f32[17,128]{1,0:T(8,128)}) custom-call(f32[256,1,128]{2,1,0:T(1,128)S(1)} %all_to_all.16.dots_ref, f32[17,128]{1,0:T(8,128)S(1)} %get-tuple-element.54.sides_ref, f32[17,128]{1,0:T(8,128)S(1)} %get-tuple-element.56.first_ref, f32[17,128]{1,0:T(8,128)S(1)} %get-tuple-element.57.second_ref), custom_call_target="tpu_custom_call" | custom-call | tf_op jit(solution)/shard_map/finish/pallas_call | solution.py:326
  (10 shorter events, 0.1 us)
Async XLA Ops:
  0.6 5.4 %collective-permute-start = (f32[16,128]{1,0:T(8,128)}, f32[16,128]{1,0:T(8,128)S(1)}, u32[]{:S(2)}, u32[]{:S(2)}) collective-permute-start(f32[16,128]{1,0:T(8,128)} %points_hbm.1), channel_id=1, source_target_pairs={{0,16},{1,17},{2,18},{3,19},{4,20},{5,21},{6,22},{7,23},{8,24},{9,... | collective-permute-start | bytes 24584 | tf_op jit(solution)/shard_map/ppermute | solution.py:264
  6.0 14.7 %all-to-all-start = ((f32[16,33,128]{2,1,0:T(8,128)}), f32[16,33,128]{2,1,0:T(8,128)S(1)}, u32[]{:S(2)}, u32[]{:S(2)}) async-start(f32[16,33,128]{2,1,0:T(8,128)} %get-tuple-element.33), calls=%async_computation | async-start | bytes 655360 | tf_op jit(solution)/shard_map/all_to_all | solution.py:278
  12.8 10.6 %collective-permute-start.1 = (f32[16,256]{1,0:T(8,128)S(1)}, f32[16,256]{1,0:T(8,128)S(1)}, u32[]{:S(2)}, u32[]{:S(2)}) collective-permute-start(f32[16,256]{1,0:T(8,128)S(1)} %pad_maximum_fusion), channel_id=1, source_target_pairs={{0,48},{1,49},{2,50},{3,51},{4,52},{5,53},{6,54},{7,55},{8,56},{9,... | collective-permute-start | bytes 49160 | tf_op jit(solution)/shard_map/ppermute | solution.py:277
  20.8 8.5 %collective-permute-start.3 = (f32[16,33,128]{2,1,0:T(8,128)S(1)}, f32[16,33,128]{2,1,0:T(8,128)S(1)}, u32[]{:S(2)}, u32[]{:S(2)}) collective-permute-start(f32[16,33,128]{2,1,0:T(8,128)S(1)} %all-to-all-done.columns_ref), channel_id=1, source_target_pairs={{0,1},{1,0},{2,3},{3,2},{4,5},{5,4},{6,7},{7,6},{8,9},{9,8},{10,11... | collective-permute-start | bytes 811016 | tf_op jit(solution)/shard_map/ppermute | solution.py:281
  23.4 3.8 %collective-permute-start.2 = (f32[16,512]{1,0:T(8,128)S(1)}, f32[16,512]{1,0:T(8,128)S(1)}, u32[]{:S(2)}, u32[]{:S(2)}) collective-permute-start(f32[16,512]{1,0:T(8,128)S(1)} %constant_dynamic-update-slice_fusion.points_ref), channel_id=1, source_target_pairs={{0,8},{1,9},{2,10},{3,11},{4,12},{5,13},{6,14},{7,15},{8,0},{9,1},... | collective-permute-start | bytes 98312 | tf_op jit(solution)/shard_map/ppermute | solution.py:280
  31.4 3.0 %collective-permute-start.4 = (f32[17,512]{1,0:T(8,128)S(1)}, f32[17,512]{1,0:T(8,128)S(1)}, u32[]{:S(2)}, u32[]{:S(2)}) collective-permute-start(f32[17,512]{1,0:T(8,128)S(1)} %get-tuple-element.43), channel_id=1, source_target_pairs={{0,8},{1,9},{2,10},{3,11},{4,12},{5,13},{6,14},{7,15},{8,0},{9,1},... | collective-permute-start | bytes 104456 | tf_op jit(solution)/shard_map/ppermute | solution.py:292
  34.4 4.7 %collective-permute-start.5 = (f32[17,512]{1,0:T(8,128)S(1)}, f32[17,512]{1,0:T(8,128)S(1)}, u32[]{:S(2)}, u32[]{:S(2)}) collective-permute-start(f32[17,512]{1,0:T(8,128)S(1)} %add.12), channel_id=1, source_target_pairs={{0,16},{1,17},{2,18},{3,19},{4,20},{5,21},{6,22},{7,23},{8,24},{9,... | collective-permute-start | bytes 104456 | tf_op jit(solution)/shard_map/ppermute | solution.py:304
  39.2 6.1 %collective-permute-start.6 = (f32[17,512]{1,0:T(8,128)S(1)}, f32[17,512]{1,0:T(8,128)S(1)}, u32[]{:S(2)}, u32[]{:S(2)}) collective-permute-start(f32[17,512]{1,0:T(8,128)S(1)} %maximum_add_fusion), channel_id=1, source_target_pairs={{0,48},{1,49},{2,50},{3,51},{4,52},{5,53},{6,54},{7,55},{8,56},{9,... | collective-permute-start | bytes 104456 | tf_op jit(solution)/shard_map/ppermute | solution.py:305
  45.3 3.3 %collective-permute-start.7 = (f32[17,512]{1,0:T(8,128)S(1)}, f32[17,512]{1,0:T(8,128)S(1)}, u32[]{:S(2)}, u32[]{:S(2)}) collective-permute-start(f32[17,512]{1,0:T(8,128)S(1)} %maximum_add_fusion.1.image_ref), channel_id=1, source_target_pairs={{0,8},{1,9},{2,10},{3,11},{4,12},{5,13},{6,14},{7,15},{8,0},{9,1},... | collective-permute-start | bytes 104456 | tf_op jit(solution)/shard_map/ppermute | solution.py:308
  49.5 6.0 %collective-permute-start.8 = (f32[16,17,128]{2,1,0:T(8,128)S(1)}, f32[16,17,128]{2,1,0:T(8,128)S(1)}, u32[]{:S(2)}, u32[]{:S(2)}) collective-permute-start(f32[16,17,128]{2,1,0:T(8,128)S(1)} %other_transposed.1), channel_id=1, source_target_pairs={{0,1},{1,0},{2,3},{3,2},{4,5},{5,4},{6,7},{7,6},{8,9},{9,8},{10,11... | collective-permute-start | bytes 417800 | tf_op jit(solution)/shard_map/ppermute | solution.py:317

commit v4 on v3

--- a/solution.py
+++ b/solution.py
@@ -73,22 +73,28 @@
 
 
 def tile_rows(left_ref, right_ref, vectors_ref, high_ref, low_ref):
-    contract = (((1,), (1,)), ((), ()))
-    total = None
-    for column in range(0, 2048, 1024):
-        across = slice(column, column + 1024)
-        kernel = jnp.exp2(
-            jnp.dot(left_ref[...], right_ref[:, across], preferred_element_type=F32)
-        )
-        high = kernel.astype(BF16)
-        low = (kernel - high.astype(F32)).astype(BF16)
-        high_ref[:, across] = high
-        low_ref[:, across] = low
-        for part in (high, low):
-            product = lax.dot_general(
-                vectors_ref[:, across], part, contract, preferred_element_type=F32
+    width = 256
+    total, waiting = 0.0, None
+    for column in range(0, 2048 + width, width):
+        made = None
+        if column < 2048:
+            across = slice(column, column + width)
+            kernel = jnp.exp2(
+                jnp.dot(left_ref[...], right_ref[:, across], preferred_element_type=F32)
             )
-            total = product if total is None else total + product
+            high = kernel.astype(BF16)
+            low = (kernel - high.astype(F32)).astype(BF16)
+            high_ref[:, across] = high
+            low_ref[:, across] = low
+            made = across, high, low
+        if waiting:
+            across, *parts = waiting
+            for part in parts:
+                total = total + lax.dot_general(
+                    vectors_ref[:, across], part, (((1,), (1,)), ((), ())),
+                    preferred_element_type=F32,
+                )
+        waiting = made
     return sum_parts(total)
 
 
@@ -196,8 +202,7 @@
         [pad_rows(t, 32) for t in (sides * sides, sides * first, first * first, first * second)],
         axis=0,
     )
-    dots = jnp.sum(rows.T, axis=0, keepdims=True)
-    dots_ref[...] = jnp.broadcast_to(dots[None], dots_ref.shape)
+    dots_ref[...] = jnp.sum(rows.T, axis=0, keepdims=True)
 
 
 def last_kernel(dots_ref, sides_ref, first_ref, second_ref, solution_ref, residual_ref):
@@ -272,12 +277,12 @@
         scratch_shapes=[pltpu.SemaphoreType.DMA((2,))],
         name="spread",
     )(points, right_sides)
-    copies, by_v = lax.optimization_barrier((copies, by_v))
     pair = jnp.concatenate([points, by_v], axis=1)
     near_points = jnp.concatenate([pair, permute(pair, perm=swap_uv)], axis=1)
     own = exchange(copies, axis_index_groups=column_groups)
-
     next_points = permute(near_points, perm=swap_p)
+    own, near_points = lax.optimization_barrier((own, near_points))
+
     other = permute(own, perm=swap_c)
     *near_own, near_sum, near_left, right, vectors = make(
         near_own_kernel, "near_own",
@@ -319,10 +324,14 @@
     pieces = exchange(own_part + from_c, axis_index_groups=column_groups)
 
     vector = shape(17, 128)
-    first, second, dots = call(dots_kernel, "dots", [vector, vector, shape(256, 1, 128)])(
+    first, second, dots = call(dots_kernel, "dots", [vector, vector, shape(1, 128)])(
         pieces, sides, image
     )
-    all_dots = exchange(dots)
+    dots = dots + permute(dots, perm=swap_c)
+    all_dots = exchange(
+        jnp.broadcast_to(dots[None], (128, 1, 128)),
+        axis_index_groups=groups_over("y", "u", "v", "p", "x"),
+    )
     return call(last_kernel, "finish", [vector, vector])(
         all_dots, sides, first, second
     )

time: 90.2 us -> 88.2 us (0.978)
  waiting for transfers between devices: 8.81 us -> 12.1 us
  blocking collectives: 33.3 us -> 30.8 us
  starting transfers between devices: 33.2 us -> 30.9 us
    all_to_all x1, blocking collectives: 22.6 us -> 19.9 us  [per_device(): exchange(jnp.broadcast_to(dots[None], (128, 1, 128)), axis_index_groups=g...]
    ppermute x1, starting transfers between devices: 2.73 us -> 0.09 us  [per_device(): total = total + turned(permute(total, perm=swap_v), 1)]
    ppermute x0 -> x1, starting transfers between devices: none -> 1.88 us  [per_device(): dots = dots + permute(dots, perm=swap_c)]
    ppermute x1, waiting for transfers between devices: 2.01 us -> 3.84 us  [per_device(): total = total + turned(permute(total, perm=swap_v), 1)]
    ppermute x1, waiting for transfers between devices: 0.01 us -> 1.13 us  [per_device(): near_points = jnp.concatenate([pair, permute(pair, perm=swap_uv)], axis=1)]
    ppermute x1, starting transfers between devices: 5.2 us -> 4.29 us  [per_device(): near_points = jnp.concatenate([pair, permute(pair, perm=swap_uv)], axis=1)]
  transfers between devices with their start and end apart: 10 -> 11, of which waited for: 6 -> 8; matrix products, arithmetic and copies ran while one was open for 0% -> 0% of each run, Pallas kernels for 11% -> 11%
where the time goes in v4:
time: 88.2 us; the launch traced here: 87.9 us
  starting transfers between devices  30.9 us (35%)
  blocking collectives  30.8 us (35%)
  Pallas kernels  13.2 us (15%)
  waiting for transfers between devices  12.1 us (14%)
    all_to_all x1, blocking collectives, per_device(): exchange(jnp.broadcast_to(dots[None], (128, 1, 128)), axis_index_groups=g...  19.9 us
    all_to_all x1, blocking collectives, per_device(): pieces = exchange(own_part + from_c, axis_index_groups=column_groups)  10.9 us
    all_to_all x1, starting transfers between devices, per_device(): own = exchange(copies, axis_index_groups=column_groups)  6.77 us
    ppermute x1, starting transfers between devices, per_device(): from_c = permute(other_part, perm=swap_c)  4.91 us
    ppermute x1, starting transfers between devices, per_device(): near_points = jnp.concatenate([pair, permute(pair, perm=swap_uv)], axis=1)  4.29 us
    ppermute x1, starting transfers between devices, per_device(): by_v = permute(points, perm=swap_v)  3.91 us
    ppermute x1, waiting for transfers between devices, per_device(): total = total + turned(permute(total, perm=swap_v), 1)  3.84 us
    ppermute x1, starting transfers between devices, per_device(): image = total + turned(permute(total, perm=swap_uv), 2)  3.49 us
  transfers between devices with their start and end apart: 11, of which 8 were waited for; matrix products, arithmetic and copies ran while one was open for 0% of the time, Pallas kernels for 11%

profile of v4, /device:TPU:1, one launch (start us, length us, event | category | flops | bytes accessed | tf_op | source)
XLA Modules:
  0.0 87.9 jit_solution(14622851460323339334)
XLA Ops:
  0.6 3.9 %collective-permute-start = (f32[16,128]{1,0:T(8,128)}, f32[16,128]{1,0:T(8,128)S(1)}, u32[]{:S(2)}, u32[]{:S(2)}) collective-permute-start(f32[16,128]{1,0:T(8,128)} %points_hbm.1), channel_id=1, source_target_pairs={{0,16},{1,17},{2,18},{3,19},{4,20},{5,21},{6,22},{7,23},{8,24},{9,... | collective-permute-start | bytes 24584 | tf_op jit(solution)/shard_map/ppermute | solution.py:269
  4.5 1.5 %spread.1 = (f32[16,128]{1,0:T(8,128)S(1)}, f32[17,128]{1,0:T(8,128)S(1)}, f32[16,33,128]{2,1,0:T(8,128)}) custom-call(f32[16,128]{1,0:T(8,128)} %points_hbm.1, f32[17,128]{1,0:T(8,128)} %sides_hbm.1), custom_call_target="tpu_custom_call" | custom-call | tf_op jit(solution)/shard_map/spread/pallas_call | solution.py:270
  6.0 6.8 %all-to-all-start = ((f32[16,33,128]{2,1,0:T(8,128)}), f32[16,33,128]{2,1,0:T(8,128)S(1)}, u32[]{:S(2)}, u32[]{:S(2)}) async-start(f32[16,33,128]{2,1,0:T(8,128)} %get-tuple-element.30), calls=%async_computation | async-start | bytes 655360 | tf_op jit(solution)/shard_map/all_to_all | solution.py:282
  12.8 0.0 collective-permute-done
  12.9 4.3 %collective-permute-start.1 = (f32[16,256]{1,0:T(8,128)S(1)}, f32[16,256]{1,0:T(8,128)S(1)}, u32[]{:S(2)}, u32[]{:S(2)}) collective-permute-start(f32[16,256]{1,0:T(8,128)S(1)} %pad_maximum_fusion), channel_id=1, source_target_pairs={{0,48},{1,49},{2,50},{3,51},{4,52},{5,53},{6,54},{7,55},{8,56},{9,... | collective-permute-start | bytes 49160 | tf_op jit(solution)/shard_map/ppermute | solution.py:281
  17.1 1.1 %collective-permute-done.1 = f32[16,256]{1,0:T(8,128)S(1)} collective-permute-done((f32[16,256]{1,0:T(8,128)S(1)}, f32[16,256]{1,0:T(8,128)S(1)}, u32[]{:S(2)}, u32[]{:S(2)}) %collective-permute-start.1) | collective-permute-done | bytes 16416 | tf_op jit(solution)/shard_map/ppermute | solution.py:281
  18.3 2.7 %all-to-all-done.columns_ref = f32[16,33,128]{2,1,0:T(8,128)S(1)} async-done(((f32[16,33,128]{2,1,0:T(8,128)}), f32[16,33,128]{2,1,0:T(8,128)S(1)}, u32[]{:S(2)}, u32[]{:S(2)}) %all-to-all-start) | async-done | bytes 270368 | tf_op jit(solution)/shard_map/all_to_all | solution.py:282
  20.9 2.2 %collective-permute-start.3 = (f32[16,33,128]{2,1,0:T(8,128)S(1)}, f32[16,33,128]{2,1,0:T(8,128)S(1)}, u32[]{:S(2)}, u32[]{:S(2)}) collective-permute-start(f32[16,33,128]{2,1,0:T(8,128)S(1)} %all-to-all-done.columns_ref), channel_id=1, source_target_pairs={{0,1},{1,0},{2,3},{3,2},{4,5},{5,4},{6,7},{7,6},{8,9},{9,8},{10,11... | collective-permute-start | bytes 811016 | tf_op jit(solution)/shard_map/ppermute | solution.py:286
  23.2 1.6 %collective-permute-start.2 = (f32[16,512]{1,0:T(8,128)S(1)}, f32[16,512]{1,0:T(8,128)S(1)}, u32[]{:S(2)}, u32[]{:S(2)}) collective-permute-start(f32[16,512]{1,0:T(8,128)S(1)} %constant_dynamic-update-slice_fusion.points_ref), channel_id=1, source_target_pairs={{0,8},{1,9},{2,10},{3,11},{4,12},{5,13},{6,14},{7,15},{8,0},{9,1},... | collective-permute-start | bytes 98312 | tf_op jit(solution)/shard_map/ppermute | solution.py:283
  24.8 1.9 %near_own.1 = (bf16[512,2048]{1,0:T(8,128)(2,1)S(1)}, bf16[512,2048]{1,0:T(8,128)(2,1)S(1)}, f32[17,512]{1,0:T(8,128)S(1)}, bf16[512,128]{1,0:T(8,128)(2,1)S(1)}...) custom-call(f32[16,512]{1,0:T(8,128)S(1)} %constant_dynamic-update-slice_fusion.points_ref, ...), custom_call_target="tpu_custom_call" | custom-call | flops 805306368 | tf_op jit(solution)/shard_map/near_own/pallas_call | solution.py:287
  26.7 0.0 collective-permute-done.2.points_ref
  26.8 2.0 %next_own.1 = (bf16[512,2048]{1,0:T(8,128)(2,1)S(1)}, bf16[512,2048]{1,0:T(8,128)(2,1)S(1)}, f32[17,512]{1,0:T(8,128)S(1)}, bf16[512,128]{1,0:T(8,128)(2,1)S(1)}) custom-call(f32[16,512]{1,0:T(8,128)S(1)} %collective-permute-done.2.points_ref, bf16[128,2048]{1,0:T(8,128)(2,1)S(1)} %get-tuple-element.35.right_ref, ...), custom_call_target="tpu_custom_call" | custom-call | flops 805306368 | tf_op jit(solution)/shard_map/next_own/pallas_call | solution.py:291
  28.7 0.0 collective-permute-done.3.columns_ref
  28.7 1.9 %next_other.1 = (bf16[512,2048]{1,0:T(8,128)(2,1)S(1)}, bf16[512,2048]{1,0:T(8,128)(2,1)S(1)}, f32[17,512]{1,0:T(8,128)S(1)}, bf16[128,2048]{1,0:T(8,128)(2,1)S(1)}, bf16[96,2048]{1,0:T(8,128)(2,1)S(1)}) custom-call(bf16[512,128]{1,0:T(8,128)(2,1)S(1)} %get-tuple-element.37.left_ref, f32[16,33,128]{2,1,0:T(8,128)S(1)} %collective-permute-done.3.columns_ref, ...), custom_call_target="tpu_custom_call" | custom-call | flops 805306368 | tf_op jit(solution)/shard_map/next_other/pallas_call | solution.py:294
  30.6 0.9 collective-permute-start.4
  31.5 1.9 %near_other.1 = (bf16[512,2048]{1,0:T(8,128)(2,1)S(1)}, bf16[512,2048]{1,0:T(8,128)(2,1)S(1)}, f32[17,512]{1,0:T(8,128)S(1)}) custom-call(bf16[512,128]{1,0:T(8,128)(2,1)S(1)} %get-tuple-element.34.left_ref, bf16[128,2048]{1,0:T(8,128)(2,1)S(1)} %get-tuple-element.39.right_ref, bf16[96,2048]{1,0:T(8,128)(2,1)S(1)} %get-tuple-element.40.vectors_ref, ...), custom_call_target="tpu_custom_call" | custom-call | flops 805306368 | tf_op jit(solution)/shard_map/near_other/pallas_call | solution.py:298
  33.4 0.3 collective-permute-done.4
  33.7 0.1 collective-permute-start.5
  33.8 3.8 %collective-permute-done.5 = f32[17,512]{1,0:T(8,128)S(1)} collective-permute-done((f32[17,512]{1,0:T(8,128)S(1)}, f32[17,512]{1,0:T(8,128)S(1)}, u32[]{:S(2)}, u32[]{:S(2)}) %collective-permute-start.5) | collective-permute-done | bytes 34848 | tf_op jit(solution)/shard_map/ppermute | solution.py:309
  37.6 3.5 %collective-permute-start.6 = (f32[17,512]{1,0:T(8,128)S(1)}, f32[17,512]{1,0:T(8,128)S(1)}, u32[]{:S(2)}, u32[]{:S(2)}) collective-permute-start(f32[17,512]{1,0:T(8,128)S(1)} %maximum_add_fusion), channel_id=1, source_target_pairs={{0,48},{1,49},{2,50},{3,51},{4,52},{5,53},{6,54},{7,55},{8,56},{9,... | collective-permute-start | bytes 104456 | tf_op jit(solution)/shard_map/ppermute | solution.py:310
  41.1 2.2 %collective-permute-done.6 = f32[17,512]{1,0:T(8,128)S(1)} collective-permute-done((f32[17,512]{1,0:T(8,128)S(1)}, f32[17,512]{1,0:T(8,128)S(1)}, u32[]{:S(2)}, u32[]{:S(2)}) %collective-permute-start.6) | collective-permute-done | bytes 34848 | tf_op jit(solution)/shard_map/ppermute | solution.py:310
  43.3 0.8 collective-permute-start.7
  44.2 1.4 %near_transposed.1 = (f32[16,17,128]{2,1,0:T(8,128)S(1)}, f32[16,17,128]{2,1,0:T(8,128)S(1)}) custom-call(f32[17,512]{1,0:T(8,128)S(1)} %maximum_add_fusion.1.image_ref, bf16[512,2048]{1,0:T(8,128)(2,1)S(1)} %get-tuple-element.46.other_high_ref, bf16[512,2048]{1,0:T(8,128)(2,1)S(1)} %get-tuple-element.47.other_low_ref, ...), custom_call_target="tpu_custom_call" | custom-call | flops 1073741824 | tf_op jit(solution)/shard_map/near_transposed/pallas_call | solution.py:314
  45.6 0.9 %collective-permute-done.7.image_ref = f32[17,512]{1,0:T(8,128)S(1)} collective-permute-done((f32[17,512]{1,0:T(8,128)S(1)}, f32[17,512]{1,0:T(8,128)S(1)}, u32[]{:S(2)}, u32[]{:S(2)}) %collective-permute-start.7) | collective-permute-done | bytes 34848 | tf_op jit(solution)/shard_map/ppermute | solution.py:313
  46.5 0.8 other_transposed.1
  47.3 4.9 %collective-permute-start.8 = (f32[16,17,128]{2,1,0:T(8,128)S(1)}, f32[16,17,128]{2,1,0:T(8,128)S(1)}, u32[]{:S(2)}, u32[]{:S(2)}) collective-permute-start(f32[16,17,128]{2,1,0:T(8,128)S(1)} %other_transposed.1), channel_id=1, source_target_pairs={{0,1},{1,0},{2,3},{3,2},{4,5},{5,4},{6,7},{7,6},{8,9},{9,8},{10,11... | collective-permute-start | bytes 417800 | tf_op jit(solution)/shard_map/ppermute | solution.py:322
  52.3 0.8 own_transposed.1
  53.1 0.3 collective-permute-done.8
  53.4 10.9 %all_to_all.15.parts_ref = f32[16,17,128]{2,1,0:T(8,128)S(1)} all-to-all(f32[16,17,128]{2,1,0:T(8,128)S(1)} %add.18), channel_id=1, replica_groups={{0,2,4,6,64,66,68,70,128,130,132,134,192,194,196,198},{1,3,5,7,65,67,69..., dimensions={0} | all-to-all | bytes 278528 | tf_op jit(solution)/shard_map/all_to_all | solution.py:324
  64.2 0.1 dots.1
  64.3 1.9 %collective-permute-start.9 = (f32[1,128]{1,0:T(1,128)S(1)}, f32[1,128]{1,0:T(1,128)S(1)}, u32[]{:S(2)}, u32[]{:S(2)}) collective-permute-start(f32[1,128]{1,0:T(1,128)S(1)} %get-tuple-element.55), channel_id=1, source_target_pairs={{0,1},{1,0},{2,3},{3,2},{4,5},{5,4},{6,7},{7,6},{8,9},{9,8},{10,11... | collective-permute-start | bytes 1544 | tf_op jit(solution)/shard_map/ppermute | solution.py:330
  66.2 0.8 collective-permute-done.9
  67.1 19.9 %all_to_all.16.dots_ref = f32[128,1,128]{2,1,0:T(1,128)S(1)} all-to-all(f32[128,1,128]{2,1,0:T(1,128)S(1)} %broadcast_in_dim.9), channel_id=1, replica_groups={{0,2,4,6,8,10,12,14,16,18,20,22,24,26,28,30,32,34,36,38,40,42,44,46,48,..., dimensions={0} | all-to-all | bytes 131072 | tf_op jit(solution)/shard_map/all_to_all | solution.py:331
  87.0 0.8 finish.1
  (12 shorter events, 0.1 us)
Async XLA Ops:
  0.6 12.2 %collective-permute-start = (f32[16,128]{1,0:T(8,128)}, f32[16,128]{1,0:T(8,128)S(1)}, u32[]{:S(2)}, u32[]{:S(2)}) collective-permute-start(f32[16,128]{1,0:T(8,128)} %points_hbm.1), channel_id=1, source_target_pairs={{0,16},{1,17},{2,18},{3,19},{4,20},{5,21},{6,22},{7,23},{8,24},{9,... | collective-permute-start | bytes 24584 | tf_op jit(solution)/shard_map/ppermute | solution.py:269
  6.0 14.9 %all-to-all-start = ((f32[16,33,128]{2,1,0:T(8,128)}), f32[16,33,128]{2,1,0:T(8,128)S(1)}, u32[]{:S(2)}, u32[]{:S(2)}) async-start(f32[16,33,128]{2,1,0:T(8,128)} %get-tuple-element.30), calls=%async_computation | async-start | bytes 655360 | tf_op jit(solution)/shard_map/all_to_all | solution.py:282
  12.9 5.4 %collective-permute-start.1 = (f32[16,256]{1,0:T(8,128)S(1)}, f32[16,256]{1,0:T(8,128)S(1)}, u32[]{:S(2)}, u32[]{:S(2)}) collective-permute-start(f32[16,256]{1,0:T(8,128)S(1)} %pad_maximum_fusion), channel_id=1, source_target_pairs={{0,48},{1,49},{2,50},{3,51},{4,52},{5,53},{6,54},{7,55},{8,56},{9,... | collective-permute-start | bytes 49160 | tf_op jit(solution)/shard_map/ppermute | solution.py:281
  20.9 7.8 %collective-permute-start.3 = (f32[16,33,128]{2,1,0:T(8,128)S(1)}, f32[16,33,128]{2,1,0:T(8,128)S(1)}, u32[]{:S(2)}, u32[]{:S(2)}) collective-permute-start(f32[16,33,128]{2,1,0:T(8,128)S(1)} %all-to-all-done.columns_ref), channel_id=1, source_target_pairs={{0,1},{1,0},{2,3},{3,2},{4,5},{5,4},{6,7},{7,6},{8,9},{9,8},{10,11... | collective-permute-start | bytes 811016 | tf_op jit(solution)/shard_map/ppermute | solution.py:286
  23.2 3.6 %collective-permute-start.2 = (f32[16,512]{1,0:T(8,128)S(1)}, f32[16,512]{1,0:T(8,128)S(1)}, u32[]{:S(2)}, u32[]{:S(2)}) collective-permute-start(f32[16,512]{1,0:T(8,128)S(1)} %constant_dynamic-update-slice_fusion.points_ref), channel_id=1, source_target_pairs={{0,8},{1,9},{2,10},{3,11},{4,12},{5,13},{6,14},{7,15},{8,0},{9,1},... | collective-permute-start | bytes 98312 | tf_op jit(solution)/shard_map/ppermute | solution.py:283
  30.6 3.0 %collective-permute-start.4 = (f32[17,512]{1,0:T(8,128)S(1)}, f32[17,512]{1,0:T(8,128)S(1)}, u32[]{:S(2)}, u32[]{:S(2)}) collective-permute-start(f32[17,512]{1,0:T(8,128)S(1)} %get-tuple-element.43), channel_id=1, source_target_pairs={{0,8},{1,9},{2,10},{3,11},{4,12},{5,13},{6,14},{7,15},{8,0},{9,1},... | collective-permute-start | bytes 104456 | tf_op jit(solution)/shard_map/ppermute | solution.py:297
  33.7 3.9 %collective-permute-start.5 = (f32[17,512]{1,0:T(8,128)S(1)}, f32[17,512]{1,0:T(8,128)S(1)}, u32[]{:S(2)}, u32[]{:S(2)}) collective-permute-start(f32[17,512]{1,0:T(8,128)S(1)} %add.15), channel_id=1, source_target_pairs={{0,16},{1,17},{2,18},{3,19},{4,20},{5,21},{6,22},{7,23},{8,24},{9,... | collective-permute-start | bytes 104456 | tf_op jit(solution)/shard_map/ppermute | solution.py:309
  37.6 5.7 %collective-permute-start.6 = (f32[17,512]{1,0:T(8,128)S(1)}, f32[17,512]{1,0:T(8,128)S(1)}, u32[]{:S(2)}, u32[]{:S(2)}) collective-permute-start(f32[17,512]{1,0:T(8,128)S(1)} %maximum_add_fusion), channel_id=1, source_target_pairs={{0,48},{1,49},{2,50},{3,51},{4,52},{5,53},{6,54},{7,55},{8,56},{9,... | collective-permute-start | bytes 104456 | tf_op jit(solution)/shard_map/ppermute | solution.py:310
  43.3 3.2 %collective-permute-start.7 = (f32[17,512]{1,0:T(8,128)S(1)}, f32[17,512]{1,0:T(8,128)S(1)}, u32[]{:S(2)}, u32[]{:S(2)}) collective-permute-start(f32[17,512]{1,0:T(8,128)S(1)} %maximum_add_fusion.1.image_ref), channel_id=1, source_target_pairs={{0,8},{1,9},{2,10},{3,11},{4,12},{5,13},{6,14},{7,15},{8,0},{9,1},... | collective-permute-start | bytes 104456 | tf_op jit(solution)/shard_map/ppermute | solution.py:313
  47.3 6.0 %collective-permute-start.8 = (f32[16,17,128]{2,1,0:T(8,128)S(1)}, f32[16,17,128]{2,1,0:T(8,128)S(1)}, u32[]{:S(2)}, u32[]{:S(2)}) collective-permute-start(f32[16,17,128]{2,1,0:T(8,128)S(1)} %other_transposed.1), channel_id=1, source_target_pairs={{0,1},{1,0},{2,3},{3,2},{4,5},{5,4},{6,7},{7,6},{8,9},{9,8},{10,11... | collective-permute-start | bytes 417800 | tf_op jit(solution)/shard_map/ppermute | solution.py:322
  64.3 2.7 %collective-permute-start.9 = (f32[1,128]{1,0:T(1,128)S(1)}, f32[1,128]{1,0:T(1,128)S(1)}, u32[]{:S(2)}, u32[]{:S(2)}) collective-permute-start(f32[1,128]{1,0:T(1,128)S(1)} %get-tuple-element.55), channel_id=1, source_target_pairs={{0,1},{1,0},{2,3},{3,2},{4,5},{5,4},{6,7},{7,6},{8,9},{9,8},{10,11... | collective-permute-start | bytes 1544 | tf_op jit(solution)/shard_map/ppermute | solution.py:330

commit v5 on v4

--- a/solution.py
+++ b/solution.py
@@ -111,8 +111,9 @@
         copy.start()
     for copy in copies:
         copy.wait()
-    both = jnp.concatenate([points_ref[...], sides_ref[...]], axis=0)
-    copies_ref[...] = jnp.broadcast_to(both[None], copies_ref.shape)
+    for k in range(16):
+        copies_ref[k, 0:16, :] = points_ref[...]
+        copies_ref[k, 16:33, :] = sides_ref[...]
 
 
 def make_left(points_ref, left_ref):
@@ -306,8 +307,9 @@
         )
 
     total = near_sum + from_p
-    total = total + turned(permute(total, perm=swap_v), 1)
-    image = total + turned(permute(total, perm=swap_uv), 2)
+    image = total
+    for distance, pairs in ((3, swap("u")), (2, swap_uv), (1, swap_v)):
+        image = image + turned(permute(total, perm=pairs), distance)
 
     by_owner = shape(16, 17, 128)
     next_image = permute(image, perm=swap_p)

time: 88.2 us -> 88.1 us (level)
  blocking collectives: 30.8 us -> 28.4 us
  starting transfers between devices: 30.9 us -> 32.9 us
    all_to_all x1, blocking collectives: 19.9 us -> 17.5 us  [per_device(): exchange(jnp.broadcast_to(dots[None], (128, 1, 128)), axis_index_groups=g...]
    ppermute x2 -> x3, starting transfers between devices: 3.58 us -> 5.74 us  [per_device(): image = image + turned(permute(total, perm=pairs), distance)]
    ppermute x2 -> x3, waiting for transfers between devices: 6.01 us -> 6.15 us  [per_device(): image = image + turned(permute(total, perm=pairs), distance)]
  transfers between devices with their start and end apart: 11 -> 12, of which waited for: 8 -> 8; matrix products, arithmetic and copies ran while one was open for 0% -> 0% of each run, Pallas kernels for 11% -> 11%
where the time goes in v5:
time: 88.1 us; the launch traced here: 87.7 us
  starting transfers between devices  32.9 us (37%)
  blocking collectives  28.4 us (32%)
  Pallas kernels  13.2 us (15%)
  waiting for transfers between devices  12.4 us (14%)
    all_to_all x1, blocking collectives, per_device(): exchange(jnp.broadcast_to(dots[None], (128, 1, 128)), axis_index_groups=g...  17.5 us
    all_to_all x1, blocking collectives, per_device(): pieces = exchange(own_part + from_c, axis_index_groups=column_groups)  10.9 us
    all_to_all x1, starting transfers between devices, per_device(): own = exchange(copies, axis_index_groups=column_groups)  6.77 us
    ppermute x3, waiting for transfers between devices, per_device(): image = image + turned(permute(total, perm=pairs), distance)  6.15 us
    ppermute x3, starting transfers between devices, per_device(): image = image + turned(permute(total, perm=pairs), distance)  5.74 us
    ppermute x1, starting transfers between devices, per_device(): from_c = permute(other_part, perm=swap_c)  4.94 us
    ppermute x1, starting transfers between devices, per_device(): near_points = jnp.concatenate([pair, permute(pair, perm=swap_uv)], axis=1)  4.29 us
    ppermute x1, starting transfers between devices, per_device(): by_v = permute(points, perm=swap_v)  3.91 us
  transfers between devices with their start and end apart: 12, of which 8 were waited for; matrix products, arithmetic and copies ran while one was open for 0% of the time, Pallas kernels for 11%

profile of v5, /device:TPU:1, one launch (start us, length us, event | category | flops | bytes accessed | tf_op | source)
XLA Modules:
  0.0 87.7 jit_solution(6890343587006495092)
XLA Ops:
  0.6 3.9 %collective-permute-start = (f32[16,128]{1,0:T(8,128)}, f32[16,128]{1,0:T(8,128)S(1)}, u32[]{:S(2)}, u32[]{:S(2)}) collective-permute-start(f32[16,128]{1,0:T(8,128)} %points_hbm.1), channel_id=1, source_target_pairs={{0,16},{1,17},{2,18},{3,19},{4,20},{5,21},{6,22},{7,23},{8,24},{9,... | collective-permute-start | bytes 24584 | tf_op jit(solution)/shard_map/ppermute | solution.py:270
  4.5 1.5 %spread.1 = (f32[16,128]{1,0:T(8,128)S(1)}, f32[17,128]{1,0:T(8,128)S(1)}, f32[16,33,128]{2,1,0:T(8,128)}) custom-call(f32[16,128]{1,0:T(8,128)} %points_hbm.1, f32[17,128]{1,0:T(8,128)} %sides_hbm.1), custom_call_target="tpu_custom_call" | custom-call | tf_op jit(solution)/shard_map/spread/pallas_call | solution.py:271
  6.0 6.8 %all-to-all-start = ((f32[16,33,128]{2,1,0:T(8,128)}), f32[16,33,128]{2,1,0:T(8,128)S(1)}, u32[]{:S(2)}, u32[]{:S(2)}) async-start(f32[16,33,128]{2,1,0:T(8,128)} %get-tuple-element.30), calls=%async_computation | async-start | bytes 655360 | tf_op jit(solution)/shard_map/all_to_all | solution.py:283
  12.8 0.0 collective-permute-done
  12.8 4.3 %collective-permute-start.1 = (f32[16,256]{1,0:T(8,128)S(1)}, f32[16,256]{1,0:T(8,128)S(1)}, u32[]{:S(2)}, u32[]{:S(2)}) collective-permute-start(f32[16,256]{1,0:T(8,128)S(1)} %pad_maximum_fusion), channel_id=1, source_target_pairs={{0,48},{1,49},{2,50},{3,51},{4,52},{5,53},{6,54},{7,55},{8,56},{9,... | collective-permute-start | bytes 49160 | tf_op jit(solution)/shard_map/ppermute | solution.py:282
  17.1 1.1 %collective-permute-done.1 = f32[16,256]{1,0:T(8,128)S(1)} collective-permute-done((f32[16,256]{1,0:T(8,128)S(1)}, f32[16,256]{1,0:T(8,128)S(1)}, u32[]{:S(2)}, u32[]{:S(2)}) %collective-permute-start.1) | collective-permute-done | bytes 16416 | tf_op jit(solution)/shard_map/ppermute | solution.py:282
  18.3 2.7 %all-to-all-done.columns_ref = f32[16,33,128]{2,1,0:T(8,128)S(1)} async-done(((f32[16,33,128]{2,1,0:T(8,128)}), f32[16,33,128]{2,1,0:T(8,128)S(1)}, u32[]{:S(2)}, u32[]{:S(2)}) %all-to-all-start) | async-done | bytes 270368 | tf_op jit(solution)/shard_map/all_to_all | solution.py:283
  20.9 2.2 %collective-permute-start.3 = (f32[16,33,128]{2,1,0:T(8,128)S(1)}, f32[16,33,128]{2,1,0:T(8,128)S(1)}, u32[]{:S(2)}, u32[]{:S(2)}) collective-permute-start(f32[16,33,128]{2,1,0:T(8,128)S(1)} %all-to-all-done.columns_ref), channel_id=1, source_target_pairs={{0,1},{1,0},{2,3},{3,2},{4,5},{5,4},{6,7},{7,6},{8,9},{9,8},{10,11... | collective-permute-start | bytes 811016 | tf_op jit(solution)/shard_map/ppermute | solution.py:287
  23.1 1.6 %collective-permute-start.2 = (f32[16,512]{1,0:T(8,128)S(1)}, f32[16,512]{1,0:T(8,128)S(1)}, u32[]{:S(2)}, u32[]{:S(2)}) collective-permute-start(f32[16,512]{1,0:T(8,128)S(1)} %constant_dynamic-update-slice_fusion.points_ref), channel_id=1, source_target_pairs={{0,8},{1,9},{2,10},{3,11},{4,12},{5,13},{6,14},{7,15},{8,0},{9,1},... | collective-permute-start | bytes 98312 | tf_op jit(solution)/shard_map/ppermute | solution.py:284
  24.8 1.9 %near_own.1 = (bf16[512,2048]{1,0:T(8,128)(2,1)S(1)}, bf16[512,2048]{1,0:T(8,128)(2,1)S(1)}, f32[17,512]{1,0:T(8,128)S(1)}, bf16[512,128]{1,0:T(8,128)(2,1)S(1)}...) custom-call(f32[16,512]{1,0:T(8,128)S(1)} %constant_dynamic-update-slice_fusion.points_ref, ...), custom_call_target="tpu_custom_call" | custom-call | flops 805306368 | tf_op jit(solution)/shard_map/near_own/pallas_call | solution.py:288
  26.7 0.0 collective-permute-done.2.points_ref
  26.7 2.0 %next_own.1 = (bf16[512,2048]{1,0:T(8,128)(2,1)S(1)}, bf16[512,2048]{1,0:T(8,128)(2,1)S(1)}, f32[17,512]{1,0:T(8,128)S(1)}, bf16[512,128]{1,0:T(8,128)(2,1)S(1)}) custom-call(f32[16,512]{1,0:T(8,128)S(1)} %collective-permute-done.2.points_ref, bf16[128,2048]{1,0:T(8,128)(2,1)S(1)} %get-tuple-element.35.right_ref, ...), custom_call_target="tpu_custom_call" | custom-call | flops 805306368 | tf_op jit(solution)/shard_map/next_own/pallas_call | solution.py:292
  28.7 0.0 collective-permute-done.3.columns_ref
  28.7 1.9 %next_other.1 = (bf16[512,2048]{1,0:T(8,128)(2,1)S(1)}, bf16[512,2048]{1,0:T(8,128)(2,1)S(1)}, f32[17,512]{1,0:T(8,128)S(1)}, bf16[128,2048]{1,0:T(8,128)(2,1)S(1)}, bf16[96,2048]{1,0:T(8,128)(2,1)S(1)}) custom-call(bf16[512,128]{1,0:T(8,128)(2,1)S(1)} %get-tuple-element.37.left_ref, f32[16,33,128]{2,1,0:T(8,128)S(1)} %collective-permute-done.3.columns_ref, ...), custom_call_target="tpu_custom_call" | custom-call | flops 805306368 | tf_op jit(solution)/shard_map/next_other/pallas_call | solution.py:295
  30.6 0.9 collective-permute-start.4
  31.5 1.9 %near_other.1 = (bf16[512,2048]{1,0:T(8,128)(2,1)S(1)}, bf16[512,2048]{1,0:T(8,128)(2,1)S(1)}, f32[17,512]{1,0:T(8,128)S(1)}) custom-call(bf16[512,128]{1,0:T(8,128)(2,1)S(1)} %get-tuple-element.34.left_ref, bf16[128,2048]{1,0:T(8,128)(2,1)S(1)} %get-tuple-element.39.right_ref, bf16[96,2048]{1,0:T(8,128)(2,1)S(1)} %get-tuple-element.40.vectors_ref, ...), custom_call_target="tpu_custom_call" | custom-call | flops 805306368 | tf_op jit(solution)/shard_map/near_other/pallas_call | solution.py:299
  33.4 0.3 collective-permute-done.4
  33.7 3.4 %collective-permute-start.6 = (f32[17,512]{1,0:T(8,128)S(1)}, f32[17,512]{1,0:T(8,128)S(1)}, u32[]{:S(2)}, u32[]{:S(2)}) collective-permute-start(f32[17,512]{1,0:T(8,128)S(1)} %add.18), channel_id=1, source_target_pairs={{0,48},{1,49},{2,50},{3,51},{4,52},{5,53},{6,54},{7,55},{8,56},{9,... | collective-permute-start | bytes 104456 | tf_op jit(solution)/shard_map/ppermute | solution.py:312
  37.1 1.2 %collective-permute-start.7 = (f32[17,512]{1,0:T(8,128)S(1)}, f32[17,512]{1,0:T(8,128)S(1)}, u32[]{:S(2)}, u32[]{:S(2)}) collective-permute-start(f32[17,512]{1,0:T(8,128)S(1)} %add.18), channel_id=1, source_target_pairs={{0,16},{1,17},{2,18},{3,19},{4,20},{5,21},{6,22},{7,23},{8,24},{9,... | collective-permute-start | bytes 104456 | tf_op jit(solution)/shard_map/ppermute | solution.py:312
  38.3 1.1 %collective-permute-start.5 = (f32[17,512]{1,0:T(8,128)S(1)}, f32[17,512]{1,0:T(8,128)S(1)}, u32[]{:S(2)}, u32[]{:S(2)}) collective-permute-start(f32[17,512]{1,0:T(8,128)S(1)} %add.18), channel_id=1, source_target_pairs={{0,32},{1,33},{2,34},{3,35},{4,36},{5,37},{6,38},{7,39},{8,40},{9,... | collective-permute-start | bytes 104456 | tf_op jit(solution)/shard_map/ppermute | solution.py:312
  39.4 0.0 collective-permute-done.6
  39.4 1.8 %collective-permute-done.7 = f32[17,512]{1,0:T(8,128)S(1)} collective-permute-done((f32[17,512]{1,0:T(8,128)S(1)}, f32[17,512]{1,0:T(8,128)S(1)}, u32[]{:S(2)}, u32[]{:S(2)}) %collective-permute-start.7) | collective-permute-done | bytes 34848 | tf_op jit(solution)/shard_map/ppermute | solution.py:312
  41.2 4.3 %collective-permute-done.5 = f32[17,512]{1,0:T(8,128)S(1)} collective-permute-done((f32[17,512]{1,0:T(8,128)S(1)}, f32[17,512]{1,0:T(8,128)S(1)}, u32[]{:S(2)}, u32[]{:S(2)}) %collective-permute-start.5) | collective-permute-done | bytes 34848 | tf_op jit(solution)/shard_map/ppermute | solution.py:312
  45.6 0.7 collective-permute-start.8
  46.3 1.4 %near_transposed.1 = (f32[16,17,128]{2,1,0:T(8,128)S(1)}, f32[16,17,128]{2,1,0:T(8,128)S(1)}) custom-call(f32[17,512]{1,0:T(8,128)S(1)} %fusion.1.image_ref, bf16[512,2048]{1,0:T(8,128)(2,1)S(1)} %get-tuple-element.46.other_high_ref, bf16[512,2048]{1,0:T(8,128)(2,1)S(1)} %get-tuple-element.47.other_low_ref, ...), custom_call_target="tpu_custom_call" | custom-call | flops 1073741824 | tf_op jit(solution)/shard_map/near_transposed/pallas_call | solution.py:316
  47.7 1.1 %collective-permute-done.8.image_ref = f32[17,512]{1,0:T(8,128)S(1)} collective-permute-done((f32[17,512]{1,0:T(8,128)S(1)}, f32[17,512]{1,0:T(8,128)S(1)}, u32[]{:S(2)}, u32[]{:S(2)}) %collective-permute-start.8) | collective-permute-done | bytes 34848 | tf_op jit(solution)/shard_map/ppermute | solution.py:315
  48.8 0.8 other_transposed.1
  49.6 4.9 %collective-permute-start.9 = (f32[16,17,128]{2,1,0:T(8,128)S(1)}, f32[16,17,128]{2,1,0:T(8,128)S(1)}, u32[]{:S(2)}, u32[]{:S(2)}) collective-permute-start(f32[16,17,128]{2,1,0:T(8,128)S(1)} %other_transposed.1), channel_id=1, source_target_pairs={{0,1},{1,0},{2,3},{3,2},{4,5},{5,4},{6,7},{7,6},{8,9},{9,8},{10,11... | collective-permute-start | bytes 417800 | tf_op jit(solution)/shard_map/ppermute | solution.py:324
  54.6 0.8 own_transposed.1
  55.4 0.3 collective-permute-done.9
  55.7 10.9 %all_to_all.15.parts_ref = f32[16,17,128]{2,1,0:T(8,128)S(1)} all-to-all(f32[16,17,128]{2,1,0:T(8,128)S(1)} %add.22), channel_id=1, replica_groups={{0,2,4,6,64,66,68,70,128,130,132,134,192,194,196,198},{1,3,5,7,65,67,69..., dimensions={0} | all-to-all | bytes 278528 | tf_op jit(solution)/shard_map/all_to_all | solution.py:326
  66.6 0.1 dots.1
  66.7 1.9 %collective-permute-start.10 = (f32[1,128]{1,0:T(1,128)S(1)}, f32[1,128]{1,0:T(1,128)S(1)}, u32[]{:S(2)}, u32[]{:S(2)}) collective-permute-start(f32[1,128]{1,0:T(1,128)S(1)} %get-tuple-element.55), channel_id=1, source_target_pairs={{0,1},{1,0},{2,3},{3,2},{4,5},{5,4},{6,7},{7,6},{8,9},{9,8},{10,11... | collective-permute-start | bytes 1544 | tf_op jit(solution)/shard_map/ppermute | solution.py:332
  68.6 0.8 collective-permute-done.10
  69.4 17.5 %all_to_all.16.dots_ref = f32[128,1,128]{2,1,0:T(1,128)S(1)} all-to-all(f32[128,1,128]{2,1,0:T(1,128)S(1)} %broadcast_in_dim.9), channel_id=1, replica_groups={{0,2,4,6,8,10,12,14,16,18,20,22,24,26,28,30,32,34,36,38,40,42,44,46,48,..., dimensions={0} | all-to-all | bytes 131072 | tf_op jit(solution)/shard_map/all_to_all | solution.py:333
  86.9 0.8 finish.1
  (12 shorter events, 0.1 us)
Async XLA Ops:
  0.6 12.2 %collective-permute-start = (f32[16,128]{1,0:T(8,128)}, f32[16,128]{1,0:T(8,128)S(1)}, u32[]{:S(2)}, u32[]{:S(2)}) collective-permute-start(f32[16,128]{1,0:T(8,128)} %points_hbm.1), channel_id=1, source_target_pairs={{0,16},{1,17},{2,18},{3,19},{4,20},{5,21},{6,22},{7,23},{8,24},{9,... | collective-permute-start | bytes 24584 | tf_op jit(solution)/shard_map/ppermute | solution.py:270
  6.0 14.9 %all-to-all-start = ((f32[16,33,128]{2,1,0:T(8,128)}), f32[16,33,128]{2,1,0:T(8,128)S(1)}, u32[]{:S(2)}, u32[]{:S(2)}) async-start(f32[16,33,128]{2,1,0:T(8,128)} %get-tuple-element.30), calls=%async_computation | async-start | bytes 655360 | tf_op jit(solution)/shard_map/all_to_all | solution.py:283
  12.8 5.4 %collective-permute-start.1 = (f32[16,256]{1,0:T(8,128)S(1)}, f32[16,256]{1,0:T(8,128)S(1)}, u32[]{:S(2)}, u32[]{:S(2)}) collective-permute-start(f32[16,256]{1,0:T(8,128)S(1)} %pad_maximum_fusion), channel_id=1, source_target_pairs={{0,48},{1,49},{2,50},{3,51},{4,52},{5,53},{6,54},{7,55},{8,56},{9,... | collective-permute-start | bytes 49160 | tf_op jit(solution)/shard_map/ppermute | solution.py:282
  20.9 7.8 %collective-permute-start.3 = (f32[16,33,128]{2,1,0:T(8,128)S(1)}, f32[16,33,128]{2,1,0:T(8,128)S(1)}, u32[]{:S(2)}, u32[]{:S(2)}) collective-permute-start(f32[16,33,128]{2,1,0:T(8,128)S(1)} %all-to-all-done.columns_ref), channel_id=1, source_target_pairs={{0,1},{1,0},{2,3},{3,2},{4,5},{5,4},{6,7},{7,6},{8,9},{9,8},{10,11... | collective-permute-start | bytes 811016 | tf_op jit(solution)/shard_map/ppermute | solution.py:287
  23.1 3.6 %collective-permute-start.2 = (f32[16,512]{1,0:T(8,128)S(1)}, f32[16,512]{1,0:T(8,128)S(1)}, u32[]{:S(2)}, u32[]{:S(2)}) collective-permute-start(f32[16,512]{1,0:T(8,128)S(1)} %constant_dynamic-update-slice_fusion.points_ref), channel_id=1, source_target_pairs={{0,8},{1,9},{2,10},{3,11},{4,12},{5,13},{6,14},{7,15},{8,0},{9,1},... | collective-permute-start | bytes 98312 | tf_op jit(solution)/shard_map/ppermute | solution.py:284
  30.6 3.0 %collective-permute-start.4 = (f32[17,512]{1,0:T(8,128)S(1)}, f32[17,512]{1,0:T(8,128)S(1)}, u32[]{:S(2)}, u32[]{:S(2)}) collective-permute-start(f32[17,512]{1,0:T(8,128)S(1)} %get-tuple-element.43), channel_id=1, source_target_pairs={{0,8},{1,9},{2,10},{3,11},{4,12},{5,13},{6,14},{7,15},{8,0},{9,1},... | collective-permute-start | bytes 104456 | tf_op jit(solution)/shard_map/ppermute | solution.py:298
  33.7 5.7 %collective-permute-start.6 = (f32[17,512]{1,0:T(8,128)S(1)}, f32[17,512]{1,0:T(8,128)S(1)}, u32[]{:S(2)}, u32[]{:S(2)}) collective-permute-start(f32[17,512]{1,0:T(8,128)S(1)} %add.18), channel_id=1, source_target_pairs={{0,48},{1,49},{2,50},{3,51},{4,52},{5,53},{6,54},{7,55},{8,56},{9,... | collective-permute-start | bytes 104456 | tf_op jit(solution)/shard_map/ppermute | solution.py:312
  37.1 4.1 %collective-permute-start.7 = (f32[17,512]{1,0:T(8,128)S(1)}, f32[17,512]{1,0:T(8,128)S(1)}, u32[]{:S(2)}, u32[]{:S(2)}) collective-permute-start(f32[17,512]{1,0:T(8,128)S(1)} %add.18), channel_id=1, source_target_pairs={{0,16},{1,17},{2,18},{3,19},{4,20},{5,21},{6,22},{7,23},{8,24},{9,... | collective-permute-start | bytes 104456 | tf_op jit(solution)/shard_map/ppermute | solution.py:312
  38.3 7.3 %collective-permute-start.5 = (f32[17,512]{1,0:T(8,128)S(1)}, f32[17,512]{1,0:T(8,128)S(1)}, u32[]{:S(2)}, u32[]{:S(2)}) collective-permute-start(f32[17,512]{1,0:T(8,128)S(1)} %add.18), channel_id=1, source_target_pairs={{0,32},{1,33},{2,34},{3,35},{4,36},{5,37},{6,38},{7,39},{8,40},{9,... | collective-permute-start | bytes 104456 | tf_op jit(solution)/shard_map/ppermute | solution.py:312
  45.6 3.2 %collective-permute-start.8 = (f32[17,512]{1,0:T(8,128)S(1)}, f32[17,512]{1,0:T(8,128)S(1)}, u32[]{:S(2)}, u32[]{:S(2)}) collective-permute-start(f32[17,512]{1,0:T(8,128)S(1)} %fusion.1.image_ref), channel_id=1, source_target_pairs={{0,8},{1,9},{2,10},{3,11},{4,12},{5,13},{6,14},{7,15},{8,0},{9,1},... | collective-permute-start | bytes 104456 | tf_op jit(solution)/shard_map/ppermute | solution.py:315
  49.6 6.0 %collective-permute-start.9 = (f32[16,17,128]{2,1,0:T(8,128)S(1)}, f32[16,17,128]{2,1,0:T(8,128)S(1)}, u32[]{:S(2)}, u32[]{:S(2)}) collective-permute-start(f32[16,17,128]{2,1,0:T(8,128)S(1)} %other_transposed.1), channel_id=1, source_target_pairs={{0,1},{1,0},{2,3},{3,2},{4,5},{5,4},{6,7},{7,6},{8,9},{9,8},{10,11... | collective-permute-start | bytes 417800 | tf_op jit(solution)/shard_map/ppermute | solution.py:324
  66.7 2.7 %collective-permute-start.10 = (f32[1,128]{1,0:T(1,128)S(1)}, f32[1,128]{1,0:T(1,128)S(1)}, u32[]{:S(2)}, u32[]{:S(2)}) collective-permute-start(f32[1,128]{1,0:T(1,128)S(1)} %get-tuple-element.55), channel_id=1, source_target_pairs={{0,1},{1,0},{2,3},{3,2},{4,5},{5,4},{6,7},{7,6},{8,9},{9,8},{10,11... | collective-permute-start | bytes 1544 | tf_op jit(solution)/shard_map/ppermute | solution.py:332

commit v6 on v5

--- a/solution.py
+++ b/solution.py
@@ -161,6 +161,21 @@
     )
 
 
+def stack_kernel(sum_ref, from_p_ref, out_ref):
+    total = sum_ref[...] + from_p_ref[...]
+    for k in range(4):
+        out_ref[17 * k : 17 * k + 17, :] = total[:, 128 * k : 128 * k + 128]
+
+
+def image_kernel(own_ref, one_ref, two_ref, three_ref, out_ref):
+    for k in range(4):
+        total = own_ref[17 * k : 17 * k + 17, :]
+        for distance, ref in ((1, one_ref), (2, two_ref), (3, three_ref)):
+            at = 17 * (k ^ distance)
+            total = total + ref[at : at + 17, :]
+        out_ref[:, 128 * k : 128 * k + 128] = total
+
+
 def vector_parts(image_ref):
     return jnp.concatenate(
         [pad_rows(part, 32) for part in split3(image_ref[...])], axis=0
@@ -300,16 +315,10 @@
         near_other_kernel, "near_other", [*tiles, shape(17, 512)]
     )(near_left, right, vectors, near_sum)
 
-    def turned(value, distance):
-        return jnp.concatenate(
-            [value[:, (k ^ distance) * 128 : (k ^ distance) * 128 + 128] for k in range(4)],
-            axis=1,
-        )
-
-    total = near_sum + from_p
-    image = total
-    for distance, pairs in ((3, swap("u")), (2, swap_uv), (1, swap_v)):
-        image = image + turned(permute(total, perm=pairs), distance)
+    total = call(stack_kernel, "stack", shape(68, 128))(near_sum, from_p)
+    image = call(image_kernel, "image", shape(17, 512))(
+        total, *(permute(total, perm=p) for p in (swap_v, swap_uv, swap("u")))
+    )
 
     by_owner = shape(16, 17, 128)
     next_image = permute(image, perm=swap_p)

time: 88.1 us -> 86.7 us (0.984)
  waiting for transfers between devices: 12.4 us -> 8.8 us
  blocking collectives: 28.4 us -> 29.6 us
  starting transfers between devices: 32.9 us -> 33.9 us
    ppermute x3, waiting for transfers between devices: 6.15 us -> 3.51 us  [per_device(): permute(total, perm=p)]
    all_to_all x1, blocking collectives: 17.5 us -> 18.7 us  [per_device(): exchange(jnp.broadcast_to(dots[None], (128, 1, 128)), axis_index_groups=g...]
    ppermute x1, starting transfers between devices: 0.67 us -> 1.76 us  [per_device(): next_image = permute(image, perm=swap_p)]
    ppermute x1, waiting for transfers between devices: 1.11 us -> 0.12 us  [per_device(): next_image = permute(image, perm=swap_p)]
where the time goes in v6:
time: 86.7 us; the launch traced here: 86.4 us
  starting transfers between devices  33.9 us (39%)
  blocking collectives  29.6 us (34%)
  Pallas kernels  13.2 us (15%)
  waiting for transfers between devices  8.8 us (10%)
    all_to_all x1, blocking collectives, per_device(): exchange(jnp.broadcast_to(dots[None], (128, 1, 128)), axis_index_groups=g...  18.7 us
    all_to_all x1, blocking collectives, per_device(): pieces = exchange(own_part + from_c, axis_index_groups=column_groups)  10.9 us
    all_to_all x1, starting transfers between devices, per_device(): own = exchange(copies, axis_index_groups=column_groups)  6.77 us
    ppermute x3, starting transfers between devices, per_device(): permute(total, perm=p)  5.74 us
    ppermute x1, starting transfers between devices, per_device(): from_c = permute(other_part, perm=swap_c)  4.86 us
    ppermute x1, starting transfers between devices, per_device(): near_points = jnp.concatenate([pair, permute(pair, perm=swap_uv)], axis=1)  4.29 us
    ppermute x1, starting transfers between devices, per_device(): by_v = permute(points, perm=swap_v)  3.91 us
    ppermute x3, waiting for transfers between devices, per_device(): permute(total, perm=p)  3.51 us
  transfers between devices with their start and end apart: 12, of which 8 were waited for; matrix products, arithmetic and copies ran while one was open for 0% of the time, Pallas kernels for 11%

profile of v6, /device:TPU:1, one launch (start us, length us, event | category | flops | bytes accessed | tf_op | source)
XLA Modules:
  0.0 86.4 jit_solution(13963285295181529926)
XLA Ops:
  0.6 3.9 %collective-permute-start = (f32[16,128]{1,0:T(8,128)}, f32[16,128]{1,0:T(8,128)S(1)}, u32[]{:S(2)}, u32[]{:S(2)}) collective-permute-start(f32[16,128]{1,0:T(8,128)} %points_hbm.1), channel_id=1, source_target_pairs={{0,16},{1,17},{2,18},{3,19},{4,20},{5,21},{6,22},{7,23},{8,24},{9,... | collective-permute-start | bytes 24584 | tf_op jit(solution)/shard_map/ppermute | solution.py:285
  4.5 1.5 %spread.1 = (f32[16,128]{1,0:T(8,128)S(1)}, f32[17,128]{1,0:T(8,128)S(1)}, f32[16,33,128]{2,1,0:T(8,128)}) custom-call(f32[16,128]{1,0:T(8,128)} %points_hbm.1, f32[17,128]{1,0:T(8,128)} %sides_hbm.1), custom_call_target="tpu_custom_call" | custom-call | tf_op jit(solution)/shard_map/spread/pallas_call | solution.py:286
  6.0 6.8 %all-to-all-start = ((f32[16,33,128]{2,1,0:T(8,128)}), f32[16,33,128]{2,1,0:T(8,128)S(1)}, u32[]{:S(2)}, u32[]{:S(2)}) async-start(f32[16,33,128]{2,1,0:T(8,128)} %get-tuple-element.30), calls=%async_computation | async-start | bytes 655360 | tf_op jit(solution)/shard_map/all_to_all | solution.py:298
  12.8 0.0 collective-permute-done
  12.8 4.3 %collective-permute-start.1 = (f32[16,256]{1,0:T(8,128)S(1)}, f32[16,256]{1,0:T(8,128)S(1)}, u32[]{:S(2)}, u32[]{:S(2)}) collective-permute-start(f32[16,256]{1,0:T(8,128)S(1)} %pad_maximum_fusion), channel_id=1, source_target_pairs={{0,48},{1,49},{2,50},{3,51},{4,52},{5,53},{6,54},{7,55},{8,56},{9,... | collective-permute-start | bytes 49160 | tf_op jit(solution)/shard_map/ppermute | solution.py:297
  17.1 1.1 %collective-permute-done.1 = f32[16,256]{1,0:T(8,128)S(1)} collective-permute-done((f32[16,256]{1,0:T(8,128)S(1)}, f32[16,256]{1,0:T(8,128)S(1)}, u32[]{:S(2)}, u32[]{:S(2)}) %collective-permute-start.1) | collective-permute-done | bytes 16416 | tf_op jit(solution)/shard_map/ppermute | solution.py:297
  18.3 2.7 %all-to-all-done.columns_ref = f32[16,33,128]{2,1,0:T(8,128)S(1)} async-done(((f32[16,33,128]{2,1,0:T(8,128)}), f32[16,33,128]{2,1,0:T(8,128)S(1)}, u32[]{:S(2)}, u32[]{:S(2)}) %all-to-all-start) | async-done | bytes 270368 | tf_op jit(solution)/shard_map/all_to_all | solution.py:298
  20.9 2.2 %collective-permute-start.3 = (f32[16,33,128]{2,1,0:T(8,128)S(1)}, f32[16,33,128]{2,1,0:T(8,128)S(1)}, u32[]{:S(2)}, u32[]{:S(2)}) collective-permute-start(f32[16,33,128]{2,1,0:T(8,128)S(1)} %all-to-all-done.columns_ref), channel_id=1, source_target_pairs={{0,1},{1,0},{2,3},{3,2},{4,5},{5,4},{6,7},{7,6},{8,9},{9,8},{10,11... | collective-permute-start | bytes 811016 | tf_op jit(solution)/shard_map/ppermute | solution.py:302
  23.2 1.6 %collective-permute-start.2 = (f32[16,512]{1,0:T(8,128)S(1)}, f32[16,512]{1,0:T(8,128)S(1)}, u32[]{:S(2)}, u32[]{:S(2)}) collective-permute-start(f32[16,512]{1,0:T(8,128)S(1)} %constant_dynamic-update-slice_fusion.points_ref), channel_id=1, source_target_pairs={{0,8},{1,9},{2,10},{3,11},{4,12},{5,13},{6,14},{7,15},{8,0},{9,1},... | collective-permute-start | bytes 98312 | tf_op jit(solution)/shard_map/ppermute | solution.py:299
  24.8 1.9 %near_own.1 = (bf16[512,2048]{1,0:T(8,128)(2,1)S(1)}, bf16[512,2048]{1,0:T(8,128)(2,1)S(1)}, f32[17,512]{1,0:T(8,128)S(1)}, bf16[512,128]{1,0:T(8,128)(2,1)S(1)}...) custom-call(f32[16,512]{1,0:T(8,128)S(1)} %constant_dynamic-update-slice_fusion.points_ref, ...), custom_call_target="tpu_custom_call" | custom-call | flops 805306368 | tf_op jit(solution)/shard_map/near_own/pallas_call | solution.py:303
  26.7 0.0 collective-permute-done.2.points_ref
  26.7 2.0 %next_own.1 = (bf16[512,2048]{1,0:T(8,128)(2,1)S(1)}, bf16[512,2048]{1,0:T(8,128)(2,1)S(1)}, f32[17,512]{1,0:T(8,128)S(1)}, bf16[512,128]{1,0:T(8,128)(2,1)S(1)}) custom-call(f32[16,512]{1,0:T(8,128)S(1)} %collective-permute-done.2.points_ref, bf16[128,2048]{1,0:T(8,128)(2,1)S(1)} %get-tuple-element.35.right_ref, ...), custom_call_target="tpu_custom_call" | custom-call | flops 805306368 | tf_op jit(solution)/shard_map/next_own/pallas_call | solution.py:307
  28.7 0.0 collective-permute-done.3.columns_ref
  28.7 1.9 %next_other.1 = (bf16[512,2048]{1,0:T(8,128)(2,1)S(1)}, bf16[512,2048]{1,0:T(8,128)(2,1)S(1)}, f32[17,512]{1,0:T(8,128)S(1)}, bf16[128,2048]{1,0:T(8,128)(2,1)S(1)}, bf16[96,2048]{1,0:T(8,128)(2,1)S(1)}) custom-call(bf16[512,128]{1,0:T(8,128)(2,1)S(1)} %get-tuple-element.37.left_ref, f32[16,33,128]{2,1,0:T(8,128)S(1)} %collective-permute-done.3.columns_ref, ...), custom_call_target="tpu_custom_call" | custom-call | flops 805306368 | tf_op jit(solution)/shard_map/next_other/pallas_call | solution.py:310
  30.6 0.9 collective-permute-start.4
  31.5 1.9 %near_other.1 = (bf16[512,2048]{1,0:T(8,128)(2,1)S(1)}, bf16[512,2048]{1,0:T(8,128)(2,1)S(1)}, f32[17,512]{1,0:T(8,128)S(1)}) custom-call(bf16[512,128]{1,0:T(8,128)(2,1)S(1)} %get-tuple-element.34.left_ref, bf16[128,2048]{1,0:T(8,128)(2,1)S(1)} %get-tuple-element.39.right_ref, bf16[96,2048]{1,0:T(8,128)(2,1)S(1)} %get-tuple-element.40.vectors_ref, ...), custom_call_target="tpu_custom_call" | custom-call | flops 805306368 | tf_op jit(solution)/shard_map/near_other/pallas_call | solution.py:314
  33.4 0.3 collective-permute-done.4.from_p_ref
  33.7 4.3 %collective-permute-start.7 = (f32[68,128]{1,0:T(8,128)S(1)}, f32[68,128]{1,0:T(8,128)S(1)}, u32[]{:S(2)}, u32[]{:S(2)}) collective-permute-start(f32[68,128]{1,0:T(8,128)S(1)} %stack.1.own_ref), channel_id=1, source_target_pairs={{0,32},{1,33},{2,34},{3,35},{4,36},{5,37},{6,38},{7,39},{8,40},{9,... | collective-permute-start | bytes 104456 | tf_op jit(solution)/shard_map/ppermute | solution.py:320
  38.0 0.0 collective-permute-start.6
  38.0 1.4 %collective-permute-start.5 = (f32[68,128]{1,0:T(8,128)S(1)}, f32[68,128]{1,0:T(8,128)S(1)}, u32[]{:S(2)}, u32[]{:S(2)}) collective-permute-start(f32[68,128]{1,0:T(8,128)S(1)} %stack.1.own_ref), channel_id=1, source_target_pairs={{0,16},{1,17},{2,18},{3,19},{4,20},{5,21},{6,22},{7,23},{8,24},{9,... | collective-permute-start | bytes 104456 | tf_op jit(solution)/shard_map/ppermute | solution.py:320
  39.4 1.1 %collective-permute-done.7.three_ref = f32[68,128]{1,0:T(8,128)S(1)} collective-permute-done((f32[68,128]{1,0:T(8,128)S(1)}, f32[68,128]{1,0:T(8,128)S(1)}, u32[]{:S(2)}, u32[]{:S(2)}) %collective-permute-start.7) | collective-permute-done | bytes 34848 | tf_op jit(solution)/shard_map/ppermute | solution.py:320
  40.5 2.4 %collective-permute-done.6.two_ref = f32[68,128]{1,0:T(8,128)S(1)} collective-permute-done((f32[68,128]{1,0:T(8,128)S(1)}, f32[68,128]{1,0:T(8,128)S(1)}, u32[]{:S(2)}, u32[]{:S(2)}) %collective-permute-start.6) | collective-permute-done | bytes 34848 | tf_op jit(solution)/shard_map/ppermute | solution.py:320
  42.9 0.0 collective-permute-done.5.one_ref
  43.0 1.8 %collective-permute-start.8 = (f32[17,512]{1,0:T(8,128)S(1)}, f32[17,512]{1,0:T(8,128)S(1)}, u32[]{:S(2)}, u32[]{:S(2)}) collective-permute-start(f32[17,512]{1,0:T(8,128)S(1)} %image.1.image_ref), channel_id=1, source_target_pairs={{0,8},{1,9},{2,10},{3,11},{4,12},{5,13},{6,14},{7,15},{8,0},{9,1},... | collective-permute-start | bytes 104456 | tf_op jit(solution)/shard_map/ppermute | solution.py:324
  44.7 1.4 %near_transposed.1 = (f32[16,17,128]{2,1,0:T(8,128)S(1)}, f32[16,17,128]{2,1,0:T(8,128)S(1)}) custom-call(f32[17,512]{1,0:T(8,128)S(1)} %image.1.image_ref, bf16[512,2048]{1,0:T(8,128)(2,1)S(1)} %get-tuple-element.46.other_high_ref, bf16[512,2048]{1,0:T(8,128)(2,1)S(1)} %get-tuple-element.47.other_low_ref, ...), custom_call_target="tpu_custom_call" | custom-call | flops 1073741824 | tf_op jit(solution)/shard_map/near_transposed/pallas_call | solution.py:325
  46.1 0.1 collective-permute-done.8.image_ref
  46.3 0.8 other_transposed.1
  47.1 4.9 %collective-permute-start.9 = (f32[16,17,128]{2,1,0:T(8,128)S(1)}, f32[16,17,128]{2,1,0:T(8,128)S(1)}, u32[]{:S(2)}, u32[]{:S(2)}) collective-permute-start(f32[16,17,128]{2,1,0:T(8,128)S(1)} %other_transposed.1), channel_id=1, source_target_pairs={{0,1},{1,0},{2,3},{3,2},{4,5},{5,4},{6,7},{7,6},{8,9},{9,8},{10,11... | collective-permute-start | bytes 417800 | tf_op jit(solution)/shard_map/ppermute | solution.py:333
  51.9 0.8 own_transposed.1
  52.7 0.3 collective-permute-done.9
  53.0 10.9 %all_to_all.15.parts_ref = f32[16,17,128]{2,1,0:T(8,128)S(1)} all-to-all(f32[16,17,128]{2,1,0:T(8,128)S(1)} %add.6), channel_id=1, replica_groups={{0,2,4,6,64,66,68,70,128,130,132,134,192,194,196,198},{1,3,5,7,65,67,69..., dimensions={0} | all-to-all | bytes 278528 | tf_op jit(solution)/shard_map/all_to_all | solution.py:335
  63.9 0.1 dots.1
  64.0 1.9 %collective-permute-start.10 = (f32[1,128]{1,0:T(1,128)S(1)}, f32[1,128]{1,0:T(1,128)S(1)}, u32[]{:S(2)}, u32[]{:S(2)}) collective-permute-start(f32[1,128]{1,0:T(1,128)S(1)} %get-tuple-element.55), channel_id=1, source_target_pairs={{0,1},{1,0},{2,3},{3,2},{4,5},{5,4},{6,7},{7,6},{8,9},{9,8},{10,11... | collective-permute-start | bytes 1544 | tf_op jit(solution)/shard_map/ppermute | solution.py:341
  65.9 0.8 collective-permute-done.10
  66.8 18.7 %all_to_all.16.dots_ref = f32[128,1,128]{2,1,0:T(1,128)S(1)} all-to-all(f32[128,1,128]{2,1,0:T(1,128)S(1)} %broadcast_in_dim.9), channel_id=1, replica_groups={{0,2,4,6,8,10,12,14,16,18,20,22,24,26,28,30,32,34,36,38,40,42,44,46,48,..., dimensions={0} | all-to-all | bytes 131072 | tf_op jit(solution)/shard_map/all_to_all | solution.py:342
  85.5 0.8 finish.1
  (9 shorter events, 0.1 us)
Async XLA Ops:
  0.6 12.2 %collective-permute-start = (f32[16,128]{1,0:T(8,128)}, f32[16,128]{1,0:T(8,128)S(1)}, u32[]{:S(2)}, u32[]{:S(2)}) collective-permute-start(f32[16,128]{1,0:T(8,128)} %points_hbm.1), channel_id=1, source_target_pairs={{0,16},{1,17},{2,18},{3,19},{4,20},{5,21},{6,22},{7,23},{8,24},{9,... | collective-permute-start | bytes 24584 | tf_op jit(solution)/shard_map/ppermute | solution.py:285
  6.0 14.9 %all-to-all-start = ((f32[16,33,128]{2,1,0:T(8,128)}), f32[16,33,128]{2,1,0:T(8,128)S(1)}, u32[]{:S(2)}, u32[]{:S(2)}) async-start(f32[16,33,128]{2,1,0:T(8,128)} %get-tuple-element.30), calls=%async_computation | async-start | bytes 655360 | tf_op jit(solution)/shard_map/all_to_all | solution.py:298
  12.8 5.4 %collective-permute-start.1 = (f32[16,256]{1,0:T(8,128)S(1)}, f32[16,256]{1,0:T(8,128)S(1)}, u32[]{:S(2)}, u32[]{:S(2)}) collective-permute-start(f32[16,256]{1,0:T(8,128)S(1)} %pad_maximum_fusion), channel_id=1, source_target_pairs={{0,48},{1,49},{2,50},{3,51},{4,52},{5,53},{6,54},{7,55},{8,56},{9,... | collective-permute-start | bytes 49160 | tf_op jit(solution)/shard_map/ppermute | solution.py:297
  20.9 7.8 %collective-permute-start.3 = (f32[16,33,128]{2,1,0:T(8,128)S(1)}, f32[16,33,128]{2,1,0:T(8,128)S(1)}, u32[]{:S(2)}, u32[]{:S(2)}) collective-permute-start(f32[16,33,128]{2,1,0:T(8,128)S(1)} %all-to-all-done.columns_ref), channel_id=1, source_target_pairs={{0,1},{1,0},{2,3},{3,2},{4,5},{5,4},{6,7},{7,6},{8,9},{9,8},{10,11... | collective-permute-start | bytes 811016 | tf_op jit(solution)/shard_map/ppermute | solution.py:302
  23.2 3.6 %collective-permute-start.2 = (f32[16,512]{1,0:T(8,128)S(1)}, f32[16,512]{1,0:T(8,128)S(1)}, u32[]{:S(2)}, u32[]{:S(2)}) collective-permute-start(f32[16,512]{1,0:T(8,128)S(1)} %constant_dynamic-update-slice_fusion.points_ref), channel_id=1, source_target_pairs={{0,8},{1,9},{2,10},{3,11},{4,12},{5,13},{6,14},{7,15},{8,0},{9,1},... | collective-permute-start | bytes 98312 | tf_op jit(solution)/shard_map/ppermute | solution.py:299
  30.6 3.0 %collective-permute-start.4 = (f32[17,512]{1,0:T(8,128)S(1)}, f32[17,512]{1,0:T(8,128)S(1)}, u32[]{:S(2)}, u32[]{:S(2)}) collective-permute-start(f32[17,512]{1,0:T(8,128)S(1)} %get-tuple-element.43), channel_id=1, source_target_pairs={{0,8},{1,9},{2,10},{3,11},{4,12},{5,13},{6,14},{7,15},{8,0},{9,1},... | collective-permute-start | bytes 104456 | tf_op jit(solution)/shard_map/ppermute | solution.py:313
  33.7 6.8 %collective-permute-start.7 = (f32[68,128]{1,0:T(8,128)S(1)}, f32[68,128]{1,0:T(8,128)S(1)}, u32[]{:S(2)}, u32[]{:S(2)}) collective-permute-start(f32[68,128]{1,0:T(8,128)S(1)} %stack.1.own_ref), channel_id=1, source_target_pairs={{0,32},{1,33},{2,34},{3,35},{4,36},{5,37},{6,38},{7,39},{8,40},{9,... | collective-permute-start | bytes 104456 | tf_op jit(solution)/shard_map/ppermute | solution.py:320
  38.0 4.9 %collective-permute-start.6 = (f32[68,128]{1,0:T(8,128)S(1)}, f32[68,128]{1,0:T(8,128)S(1)}, u32[]{:S(2)}, u32[]{:S(2)}) collective-permute-start(f32[68,128]{1,0:T(8,128)S(1)} %stack.1.own_ref), channel_id=1, source_target_pairs={{0,48},{1,49},{2,50},{3,51},{4,52},{5,53},{6,54},{7,55},{8,56},{9,... | collective-permute-start | bytes 104456 | tf_op jit(solution)/shard_map/ppermute | solution.py:320
  38.0 4.9 %collective-permute-start.5 = (f32[68,128]{1,0:T(8,128)S(1)}, f32[68,128]{1,0:T(8,128)S(1)}, u32[]{:S(2)}, u32[]{:S(2)}) collective-permute-start(f32[68,128]{1,0:T(8,128)S(1)} %stack.1.own_ref), channel_id=1, source_target_pairs={{0,16},{1,17},{2,18},{3,19},{4,20},{5,21},{6,22},{7,23},{8,24},{9,... | collective-permute-start | bytes 104456 | tf_op jit(solution)/shard_map/ppermute | solution.py:320
  43.0 3.3 %collective-permute-start.8 = (f32[17,512]{1,0:T(8,128)S(1)}, f32[17,512]{1,0:T(8,128)S(1)}, u32[]{:S(2)}, u32[]{:S(2)}) collective-permute-start(f32[17,512]{1,0:T(8,128)S(1)} %image.1.image_ref), channel_id=1, source_target_pairs={{0,8},{1,9},{2,10},{3,11},{4,12},{5,13},{6,14},{7,15},{8,0},{9,1},... | collective-permute-start | bytes 104456 | tf_op jit(solution)/shard_map/ppermute | solution.py:324
  47.1 5.9 %collective-permute-start.9 = (f32[16,17,128]{2,1,0:T(8,128)S(1)}, f32[16,17,128]{2,1,0:T(8,128)S(1)}, u32[]{:S(2)}, u32[]{:S(2)}) collective-permute-start(f32[16,17,128]{2,1,0:T(8,128)S(1)} %other_transposed.1), channel_id=1, source_target_pairs={{0,1},{1,0},{2,3},{3,2},{4,5},{5,4},{6,7},{7,6},{8,9},{9,8},{10,11... | collective-permute-start | bytes 417800 | tf_op jit(solution)/shard_map/ppermute | solution.py:333
  64.0 2.7 %collective-permute-start.10 = (f32[1,128]{1,0:T(1,128)S(1)}, f32[1,128]{1,0:T(1,128)S(1)}, u32[]{:S(2)}, u32[]{:S(2)}) collective-permute-start(f32[1,128]{1,0:T(1,128)S(1)} %get-tuple-element.55), channel_id=1, source_target_pairs={{0,1},{1,0},{2,3},{3,2},{4,5},{5,4},{6,7},{7,6},{8,9},{9,8},{10,11... | collective-permute-start | bytes 1544 | tf_op jit(solution)/shard_map/ppermute | solution.py:341

commit v7 on v6

--- a/solution.py
+++ b/solution.py
@@ -148,37 +148,40 @@
     left_ref, columns_ref, before_ref, high_ref, low_ref, out_ref, right_ref, vectors_ref
 ):
     make_right(columns_ref, right_ref, vectors_ref)
+    total = before_ref[...] + tile_rows(
+        left_ref, right_ref, vectors_ref, high_ref, low_ref
+    )
+    for k in range(4):
+        out_ref[17 * k : 17 * k + 17, :] = total[:, 128 * k : 128 * k + 128]
+
+
+def near_other_kernel(
+    left_ref, right_ref, vectors_ref, before_ref, high_ref, low_ref, out_ref
+):
     out_ref[...] = before_ref[...] + tile_rows(
         left_ref, right_ref, vectors_ref, high_ref, low_ref
     )
 
 
-def near_other_kernel(
-    left_ref, right_ref, vectors_ref, before_ref, high_ref, low_ref, out_ref
-):
-    out_ref[...] = before_ref[...] + tile_rows(
-        left_ref, right_ref, vectors_ref, high_ref, low_ref
-    )
-
-
 def stack_kernel(sum_ref, from_p_ref, out_ref):
-    total = sum_ref[...] + from_p_ref[...]
     for k in range(4):
-        out_ref[17 * k : 17 * k + 17, :] = total[:, 128 * k : 128 * k + 128]
-
-
-def image_kernel(own_ref, one_ref, two_ref, three_ref, out_ref):
+        at = slice(17 * k, 17 * k + 17)
+        out_ref[at, :] = sum_ref[:, 128 * k : 128 * k + 128] + from_p_ref[at, :]
+
+
+def image_kernel(own_ref, one_ref, two_ref, three_ref, out_ref, packed_ref):
     for k in range(4):
         total = own_ref[17 * k : 17 * k + 17, :]
         for distance, ref in ((1, one_ref), (2, two_ref), (3, three_ref)):
             at = 17 * (k ^ distance)
             total = total + ref[at : at + 17, :]
         out_ref[:, 128 * k : 128 * k + 128] = total
-
-
-def vector_parts(image_ref):
+        packed_ref[17 * k : 17 * k + 17, :] = total
+
+
+def vector_parts(image):
     return jnp.concatenate(
-        [pad_rows(part, 32) for part in split3(image_ref[...])], axis=0
+        [pad_rows(part, 32) for part in split3(image)], axis=0
     ).astype(BF16)
 
 
@@ -192,7 +195,7 @@
 def near_transposed_kernel(
     image_ref, other_high_ref, other_low_ref, own_high_ref, own_low_ref, other_ref, own_ref
 ):
-    left = vector_parts(image_ref)
+    left = vector_parts(image_ref[...])
     for high_ref, low_ref, out_ref in (
         (other_high_ref, other_low_ref, other_ref), (own_high_ref, own_low_ref, own_ref)
     ):
@@ -202,7 +205,9 @@
 
 
 def next_transposed_kernel(image_ref, high_ref, low_ref, before_ref, out_ref):
-    total = transposed_product(vector_parts(image_ref), high_ref, low_ref)
+    total = transposed_product(vector_parts(
+        jnp.concatenate([image_ref[17 * k : 17 * k + 17, :] for k in range(4)], axis=1)
+    ), high_ref, low_ref)
     for k in range(16):
         out_ref[k] = before_ref[k] + total[:, k * 128 : (k + 1) * 128]
 
@@ -308,7 +313,7 @@
         next_own_kernel, "next_own", [*tiles, shape(17, 512), left_shape]
     )(next_points, right, vectors)
     *next_other, next_sum, right, vectors = make(
-        next_other_kernel, "next_other", [*tiles, shape(17, 512), *right_shapes]
+        next_other_kernel, "next_other", [*tiles, shape(68, 128), *right_shapes]
     )(next_left, other, next_sum)
     from_p = permute(next_sum, perm=swap_p)
     *near_other, near_sum = make(
@@ -316,12 +321,12 @@
     )(near_left, right, vectors, near_sum)
 
     total = call(stack_kernel, "stack", shape(68, 128))(near_sum, from_p)
-    image = call(image_kernel, "image", shape(17, 512))(
+    image, packed = call(image_kernel, "image", [shape(17, 512), shape(68, 128)])(
         total, *(permute(total, perm=p) for p in (swap_v, swap_uv, swap("u")))
     )
 
     by_owner = shape(16, 17, 128)
-    next_image = permute(image, perm=swap_p)
+    next_image = permute(packed, perm=swap_p)
     other_part, own_part = call(
         near_transposed_kernel, "near_transposed", [by_owner, by_owner],
         flops=1024 * 2048 * 512,

time: 86.7 us -> 86.4 us (level)
  no operation moved by 1% of the time
where the time goes in v7:
time: 86.4 us; the launch traced here: 86.1 us
  starting transfers between devices  33.8 us (39%)
  blocking collectives  29.6 us (34%)
  Pallas kernels  13.2 us (15%)
  waiting for transfers between devices  8.66 us (10%)
    all_to_all x1, blocking collectives, per_device(): exchange(jnp.broadcast_to(dots[None], (128, 1, 128)), axis_index_groups=g...  18.7 us
    all_to_all x1, blocking collectives, per_device(): pieces = exchange(own_part + from_c, axis_index_groups=column_groups)  10.9 us
    all_to_all x1, starting transfers between devices, per_device(): own = exchange(copies, axis_index_groups=column_groups)  6.77 us
    ppermute x3, starting transfers between devices, per_device(): permute(total, perm=p)  5.74 us
    ppermute x1, starting transfers between devices, per_device(): from_c = permute(other_part, perm=swap_c)  4.73 us
    ppermute x1, starting transfers between devices, per_device(): near_points = jnp.concatenate([pair, permute(pair, perm=swap_uv)], axis=1)  4.29 us
    ppermute x1, starting transfers between devices, per_device(): by_v = permute(points, perm=swap_v)  3.91 us
    ppermute x3, waiting for transfers between devices, per_device(): permute(total, perm=p)  3.5 us
  transfers between devices with their start and end apart: 12, of which 8 were waited for; matrix products, arithmetic and copies ran while one was open for 0% of the time, Pallas kernels for 11%

profile of v7, /device:TPU:1, one launch (start us, length us, event | category | flops | bytes accessed | tf_op | source)
XLA Modules:
  0.0 86.1 jit_solution(15689897691812050635)
XLA Ops:
  0.6 3.9 %collective-permute-start = (f32[16,128]{1,0:T(8,128)}, f32[16,128]{1,0:T(8,128)S(1)}, u32[]{:S(2)}, u32[]{:S(2)}) collective-permute-start(f32[16,128]{1,0:T(8,128)} %points_hbm.1), channel_id=1, source_target_pairs={{0,16},{1,17},{2,18},{3,19},{4,20},{5,21},{6,22},{7,23},{8,24},{9,... | collective-permute-start | bytes 24584 | tf_op jit(solution)/shard_map/ppermute | solution.py:290
  4.5 1.5 %spread.1 = (f32[16,128]{1,0:T(8,128)S(1)}, f32[17,128]{1,0:T(8,128)S(1)}, f32[16,33,128]{2,1,0:T(8,128)}) custom-call(f32[16,128]{1,0:T(8,128)} %points_hbm.1, f32[17,128]{1,0:T(8,128)} %sides_hbm.1), custom_call_target="tpu_custom_call" | custom-call | tf_op jit(solution)/shard_map/spread/pallas_call | solution.py:291
  6.0 6.8 %all-to-all-start = ((f32[16,33,128]{2,1,0:T(8,128)}), f32[16,33,128]{2,1,0:T(8,128)S(1)}, u32[]{:S(2)}, u32[]{:S(2)}) async-start(f32[16,33,128]{2,1,0:T(8,128)} %get-tuple-element.32), calls=%async_computation | async-start | bytes 655360 | tf_op jit(solution)/shard_map/all_to_all | solution.py:303
  12.8 0.0 collective-permute-done
  12.9 4.3 %collective-permute-start.1 = (f32[16,256]{1,0:T(8,128)S(1)}, f32[16,256]{1,0:T(8,128)S(1)}, u32[]{:S(2)}, u32[]{:S(2)}) collective-permute-start(f32[16,256]{1,0:T(8,128)S(1)} %pad_maximum_fusion), channel_id=1, source_target_pairs={{0,48},{1,49},{2,50},{3,51},{4,52},{5,53},{6,54},{7,55},{8,56},{9,... | collective-permute-start | bytes 49160 | tf_op jit(solution)/shard_map/ppermute | solution.py:302
  17.1 1.1 %collective-permute-done.1 = f32[16,256]{1,0:T(8,128)S(1)} collective-permute-done((f32[16,256]{1,0:T(8,128)S(1)}, f32[16,256]{1,0:T(8,128)S(1)}, u32[]{:S(2)}, u32[]{:S(2)}) %collective-permute-start.1) | collective-permute-done | bytes 16416 | tf_op jit(solution)/shard_map/ppermute | solution.py:302
  18.3 2.7 %all-to-all-done.columns_ref = f32[16,33,128]{2,1,0:T(8,128)S(1)} async-done(((f32[16,33,128]{2,1,0:T(8,128)}), f32[16,33,128]{2,1,0:T(8,128)S(1)}, u32[]{:S(2)}, u32[]{:S(2)}) %all-to-all-start) | async-done | bytes 270368 | tf_op jit(solution)/shard_map/all_to_all | solution.py:303
  20.9 2.2 %collective-permute-start.3 = (f32[16,33,128]{2,1,0:T(8,128)S(1)}, f32[16,33,128]{2,1,0:T(8,128)S(1)}, u32[]{:S(2)}, u32[]{:S(2)}) collective-permute-start(f32[16,33,128]{2,1,0:T(8,128)S(1)} %all-to-all-done.columns_ref), channel_id=1, source_target_pairs={{0,1},{1,0},{2,3},{3,2},{4,5},{5,4},{6,7},{7,6},{8,9},{9,8},{10,11... | collective-permute-start | bytes 811016 | tf_op jit(solution)/shard_map/ppermute | solution.py:307
  23.2 1.6 %collective-permute-start.2 = (f32[16,512]{1,0:T(8,128)S(1)}, f32[16,512]{1,0:T(8,128)S(1)}, u32[]{:S(2)}, u32[]{:S(2)}) collective-permute-start(f32[16,512]{1,0:T(8,128)S(1)} %constant_dynamic-update-slice_fusion.points_ref), channel_id=1, source_target_pairs={{0,8},{1,9},{2,10},{3,11},{4,12},{5,13},{6,14},{7,15},{8,0},{9,1},... | collective-permute-start | bytes 98312 | tf_op jit(solution)/shard_map/ppermute | solution.py:304
  24.8 2.0 %near_own.1 = (bf16[512,2048]{1,0:T(8,128)(2,1)S(1)}, bf16[512,2048]{1,0:T(8,128)(2,1)S(1)}, f32[17,512]{1,0:T(8,128)S(1)}, bf16[512,128]{1,0:T(8,128)(2,1)S(1)}...) custom-call(f32[16,512]{1,0:T(8,128)S(1)} %constant_dynamic-update-slice_fusion.points_ref, ...), custom_call_target="tpu_custom_call" | custom-call | flops 805306368 | tf_op jit(solution)/shard_map/near_own/pallas_call | solution.py:308
  26.8 0.0 collective-permute-done.2.points_ref
  26.8 2.0 %next_own.1 = (bf16[512,2048]{1,0:T(8,128)(2,1)S(1)}, bf16[512,2048]{1,0:T(8,128)(2,1)S(1)}, f32[17,512]{1,0:T(8,128)S(1)}, bf16[512,128]{1,0:T(8,128)(2,1)S(1)}) custom-call(f32[16,512]{1,0:T(8,128)S(1)} %collective-permute-done.2.points_ref, bf16[128,2048]{1,0:T(8,128)(2,1)S(1)} %get-tuple-element.37.right_ref, ...), custom_call_target="tpu_custom_call" | custom-call | flops 805306368 | tf_op jit(solution)/shard_map/next_own/pallas_call | solution.py:312
  28.7 0.0 collective-permute-done.3.columns_ref
  28.7 1.9 %next_other.1 = (bf16[512,2048]{1,0:T(8,128)(2,1)S(1)}, bf16[512,2048]{1,0:T(8,128)(2,1)S(1)}, f32[68,128]{1,0:T(8,128)S(1)}, bf16[128,2048]{1,0:T(8,128)(2,1)S(1)}, bf16[96,2048]{1,0:T(8,128)(2,1)S(1)}) custom-call(bf16[512,128]{1,0:T(8,128)(2,1)S(1)} %get-tuple-element.39.left_ref, f32[16,33,128]{2,1,0:T(8,128)S(1)} %collective-permute-done.3.columns_ref, ...), custom_call_target="tpu_custom_call" | custom-call | flops 805306368 | tf_op jit(solution)/shard_map/next_other/pallas_call | solution.py:315
  30.7 0.8 collective-permute-start.4
  31.5 1.9 %near_other.1 = (bf16[512,2048]{1,0:T(8,128)(2,1)S(1)}, bf16[512,2048]{1,0:T(8,128)(2,1)S(1)}, f32[17,512]{1,0:T(8,128)S(1)}) custom-call(bf16[512,128]{1,0:T(8,128)(2,1)S(1)} %get-tuple-element.36.left_ref, bf16[128,2048]{1,0:T(8,128)(2,1)S(1)} %get-tuple-element.41.right_ref, bf16[96,2048]{1,0:T(8,128)(2,1)S(1)} %get-tuple-element.42.vectors_ref, ...), custom_call_target="tpu_custom_call" | custom-call | flops 805306368 | tf_op jit(solution)/shard_map/near_other/pallas_call | solution.py:319
  33.4 0.2 collective-permute-done.4.from_p_ref
  33.6 4.3 %collective-permute-start.7 = (f32[68,128]{1,0:T(8,128)S(1)}, f32[68,128]{1,0:T(8,128)S(1)}, u32[]{:S(2)}, u32[]{:S(2)}) collective-permute-start(f32[68,128]{1,0:T(8,128)S(1)} %stack.1.own_ref), channel_id=1, source_target_pairs={{0,32},{1,33},{2,34},{3,35},{4,36},{5,37},{6,38},{7,39},{8,40},{9,... | collective-permute-start | bytes 104456 | tf_op jit(solution)/shard_map/ppermute | solution.py:325
  37.9 0.0 collective-permute-start.6
  37.9 1.4 %collective-permute-start.5 = (f32[68,128]{1,0:T(8,128)S(1)}, f32[68,128]{1,0:T(8,128)S(1)}, u32[]{:S(2)}, u32[]{:S(2)}) collective-permute-start(f32[68,128]{1,0:T(8,128)S(1)} %stack.1.own_ref), channel_id=1, source_target_pairs={{0,16},{1,17},{2,18},{3,19},{4,20},{5,21},{6,22},{7,23},{8,24},{9,... | collective-permute-start | bytes 104456 | tf_op jit(solution)/shard_map/ppermute | solution.py:325
  39.3 1.1 %collective-permute-done.7.three_ref = f32[68,128]{1,0:T(8,128)S(1)} collective-permute-done((f32[68,128]{1,0:T(8,128)S(1)}, f32[68,128]{1,0:T(8,128)S(1)}, u32[]{:S(2)}, u32[]{:S(2)}) %collective-permute-start.7) | collective-permute-done | bytes 34848 | tf_op jit(solution)/shard_map/ppermute | solution.py:325
  40.4 2.4 %collective-permute-done.6.two_ref = f32[68,128]{1,0:T(8,128)S(1)} collective-permute-done((f32[68,128]{1,0:T(8,128)S(1)}, f32[68,128]{1,0:T(8,128)S(1)}, u32[]{:S(2)}, u32[]{:S(2)}) %collective-permute-start.6) | collective-permute-done | bytes 34848 | tf_op jit(solution)/shard_map/ppermute | solution.py:325
  42.8 0.0 collective-permute-done.5.one_ref
  42.8 1.8 %collective-permute-start.8 = (f32[68,128]{1,0:T(8,128)S(1)}, f32[68,128]{1,0:T(8,128)S(1)}, u32[]{:S(2)}, u32[]{:S(2)}) collective-permute-start(f32[68,128]{1,0:T(8,128)S(1)} %get-tuple-element.46), channel_id=1, source_target_pairs={{0,8},{1,9},{2,10},{3,11},{4,12},{5,13},{6,14},{7,15},{8,0},{9,1},... | collective-permute-start | bytes 104456 | tf_op jit(solution)/shard_map/ppermute | solution.py:329
  44.6 1.4 %near_transposed.1 = (f32[16,17,128]{2,1,0:T(8,128)S(1)}, f32[16,17,128]{2,1,0:T(8,128)S(1)}) custom-call(f32[17,512]{1,0:T(8,128)S(1)} %get-tuple-element.49.image_ref, bf16[512,2048]{1,0:T(8,128)(2,1)S(1)} %get-tuple-element.50.other_high_ref, bf16[512,2048]{1,0:T(8,128)(2,1)S(1)} %get-tuple-element.51.other_low_ref, ...), custom_call_target="tpu_custom_call" | custom-call | flops 1073741824 | tf_op jit(solution)/shard_map/near_transposed/pallas_call | solution.py:330
  46.0 0.1 collective-permute-done.8.image_ref
  46.2 0.8 other_transposed.1
  47.0 4.7 %collective-permute-start.9 = (f32[16,17,128]{2,1,0:T(8,128)S(1)}, f32[16,17,128]{2,1,0:T(8,128)S(1)}, u32[]{:S(2)}, u32[]{:S(2)}) collective-permute-start(f32[16,17,128]{2,1,0:T(8,128)S(1)} %other_transposed.1), channel_id=1, source_target_pairs={{0,1},{1,0},{2,3},{3,2},{4,5},{5,4},{6,7},{7,6},{8,9},{9,8},{10,11... | collective-permute-start | bytes 417800 | tf_op jit(solution)/shard_map/ppermute | solution.py:338
  51.7 0.8 own_transposed.1
  52.5 0.3 collective-permute-done.9
  52.8 10.9 %all_to_all.15.parts_ref = f32[16,17,128]{2,1,0:T(8,128)S(1)} all-to-all(f32[16,17,128]{2,1,0:T(8,128)S(1)} %add.6), channel_id=1, replica_groups={{0,2,4,6,64,66,68,70,128,130,132,134,192,194,196,198},{1,3,5,7,65,67,69..., dimensions={0} | all-to-all | bytes 278528 | tf_op jit(solution)/shard_map/all_to_all | solution.py:340
  63.7 0.1 dots.1
  63.8 1.9 %collective-permute-start.10 = (f32[1,128]{1,0:T(1,128)S(1)}, f32[1,128]{1,0:T(1,128)S(1)}, u32[]{:S(2)}, u32[]{:S(2)}) collective-permute-start(f32[1,128]{1,0:T(1,128)S(1)} %get-tuple-element.59), channel_id=1, source_target_pairs={{0,1},{1,0},{2,3},{3,2},{4,5},{5,4},{6,7},{7,6},{8,9},{9,8},{10,11... | collective-permute-start | bytes 1544 | tf_op jit(solution)/shard_map/ppermute | solution.py:346
  65.7 0.8 collective-permute-done.10
  66.5 18.7 %all_to_all.16.dots_ref = f32[128,1,128]{2,1,0:T(1,128)S(1)} all-to-all(f32[128,1,128]{2,1,0:T(1,128)S(1)} %broadcast_in_dim.9), channel_id=1, replica_groups={{0,2,4,6,8,10,12,14,16,18,20,22,24,26,28,30,32,34,36,38,40,42,44,46,48,..., dimensions={0} | all-to-all | bytes 131072 | tf_op jit(solution)/shard_map/all_to_all | solution.py:347
  85.3 0.8 finish.1
  (9 shorter events, 0.1 us)
Async XLA Ops:
  0.6 12.2 %collective-permute-start = (f32[16,128]{1,0:T(8,128)}, f32[16,128]{1,0:T(8,128)S(1)}, u32[]{:S(2)}, u32[]{:S(2)}) collective-permute-start(f32[16,128]{1,0:T(8,128)} %points_hbm.1), channel_id=1, source_target_pairs={{0,16},{1,17},{2,18},{3,19},{4,20},{5,21},{6,22},{7,23},{8,24},{9,... | collective-permute-start | bytes 24584 | tf_op jit(solution)/shard_map/ppermute | solution.py:290
  6.0 14.9 %all-to-all-start = ((f32[16,33,128]{2,1,0:T(8,128)}), f32[16,33,128]{2,1,0:T(8,128)S(1)}, u32[]{:S(2)}, u32[]{:S(2)}) async-start(f32[16,33,128]{2,1,0:T(8,128)} %get-tuple-element.32), calls=%async_computation | async-start | bytes 655360 | tf_op jit(solution)/shard_map/all_to_all | solution.py:303
  12.9 5.4 %collective-permute-start.1 = (f32[16,256]{1,0:T(8,128)S(1)}, f32[16,256]{1,0:T(8,128)S(1)}, u32[]{:S(2)}, u32[]{:S(2)}) collective-permute-start(f32[16,256]{1,0:T(8,128)S(1)} %pad_maximum_fusion), channel_id=1, source_target_pairs={{0,48},{1,49},{2,50},{3,51},{4,52},{5,53},{6,54},{7,55},{8,56},{9,... | collective-permute-start | bytes 49160 | tf_op jit(solution)/shard_map/ppermute | solution.py:302
  20.9 7.8 %collective-permute-start.3 = (f32[16,33,128]{2,1,0:T(8,128)S(1)}, f32[16,33,128]{2,1,0:T(8,128)S(1)}, u32[]{:S(2)}, u32[]{:S(2)}) collective-permute-start(f32[16,33,128]{2,1,0:T(8,128)S(1)} %all-to-all-done.columns_ref), channel_id=1, source_target_pairs={{0,1},{1,0},{2,3},{3,2},{4,5},{5,4},{6,7},{7,6},{8,9},{9,8},{10,11... | collective-permute-start | bytes 811016 | tf_op jit(solution)/shard_map/ppermute | solution.py:307
  23.2 3.6 %collective-permute-start.2 = (f32[16,512]{1,0:T(8,128)S(1)}, f32[16,512]{1,0:T(8,128)S(1)}, u32[]{:S(2)}, u32[]{:S(2)}) collective-permute-start(f32[16,512]{1,0:T(8,128)S(1)} %constant_dynamic-update-slice_fusion.points_ref), channel_id=1, source_target_pairs={{0,8},{1,9},{2,10},{3,11},{4,12},{5,13},{6,14},{7,15},{8,0},{9,1},... | collective-permute-start | bytes 98312 | tf_op jit(solution)/shard_map/ppermute | solution.py:304
  30.7 2.9 %collective-permute-start.4 = (f32[68,128]{1,0:T(8,128)S(1)}, f32[68,128]{1,0:T(8,128)S(1)}, u32[]{:S(2)}, u32[]{:S(2)}) collective-permute-start(f32[68,128]{1,0:T(8,128)S(1)} %get-tuple-element.45), channel_id=1, source_target_pairs={{0,8},{1,9},{2,10},{3,11},{4,12},{5,13},{6,14},{7,15},{8,0},{9,1},... | collective-permute-start | bytes 104456 | tf_op jit(solution)/shard_map/ppermute | solution.py:318
  33.6 6.8 %collective-permute-start.7 = (f32[68,128]{1,0:T(8,128)S(1)}, f32[68,128]{1,0:T(8,128)S(1)}, u32[]{:S(2)}, u32[]{:S(2)}) collective-permute-start(f32[68,128]{1,0:T(8,128)S(1)} %stack.1.own_ref), channel_id=1, source_target_pairs={{0,32},{1,33},{2,34},{3,35},{4,36},{5,37},{6,38},{7,39},{8,40},{9,... | collective-permute-start | bytes 104456 | tf_op jit(solution)/shard_map/ppermute | solution.py:325
  37.9 4.9 %collective-permute-start.6 = (f32[68,128]{1,0:T(8,128)S(1)}, f32[68,128]{1,0:T(8,128)S(1)}, u32[]{:S(2)}, u32[]{:S(2)}) collective-permute-start(f32[68,128]{1,0:T(8,128)S(1)} %stack.1.own_ref), channel_id=1, source_target_pairs={{0,48},{1,49},{2,50},{3,51},{4,52},{5,53},{6,54},{7,55},{8,56},{9,... | collective-permute-start | bytes 104456 | tf_op jit(solution)/shard_map/ppermute | solution.py:325
  37.9 4.9 %collective-permute-start.5 = (f32[68,128]{1,0:T(8,128)S(1)}, f32[68,128]{1,0:T(8,128)S(1)}, u32[]{:S(2)}, u32[]{:S(2)}) collective-permute-start(f32[68,128]{1,0:T(8,128)S(1)} %stack.1.own_ref), channel_id=1, source_target_pairs={{0,16},{1,17},{2,18},{3,19},{4,20},{5,21},{6,22},{7,23},{8,24},{9,... | collective-permute-start | bytes 104456 | tf_op jit(solution)/shard_map/ppermute | solution.py:325
  42.8 3.3 %collective-permute-start.8 = (f32[68,128]{1,0:T(8,128)S(1)}, f32[68,128]{1,0:T(8,128)S(1)}, u32[]{:S(2)}, u32[]{:S(2)}) collective-permute-start(f32[68,128]{1,0:T(8,128)S(1)} %get-tuple-element.46), channel_id=1, source_target_pairs={{0,8},{1,9},{2,10},{3,11},{4,12},{5,13},{6,14},{7,15},{8,0},{9,1},... | collective-permute-start | bytes 104456 | tf_op jit(solution)/shard_map/ppermute | solution.py:329
  47.0 5.8 %collective-permute-start.9 = (f32[16,17,128]{2,1,0:T(8,128)S(1)}, f32[16,17,128]{2,1,0:T(8,128)S(1)}, u32[]{:S(2)}, u32[]{:S(2)}) collective-permute-start(f32[16,17,128]{2,1,0:T(8,128)S(1)} %other_transposed.1), channel_id=1, source_target_pairs={{0,1},{1,0},{2,3},{3,2},{4,5},{5,4},{6,7},{7,6},{8,9},{9,8},{10,11... | collective-permute-start | bytes 417800 | tf_op jit(solution)/shard_map/ppermute | solution.py:338
  63.8 2.7 %collective-permute-start.10 = (f32[1,128]{1,0:T(1,128)S(1)}, f32[1,128]{1,0:T(1,128)S(1)}, u32[]{:S(2)}, u32[]{:S(2)}) collective-permute-start(f32[1,128]{1,0:T(1,128)S(1)} %get-tuple-element.59), channel_id=1, source_target_pairs={{0,1},{1,0},{2,3},{3,2},{4,5},{5,4},{6,7},{7,6},{8,9},{9,8},{10,11... | collective-permute-start | bytes 1544 | tf_op jit(solution)/shard_map/ppermute | solution.py:346

commit v8 on v7

--- a/solution.py
+++ b/solution.py
@@ -24,6 +24,10 @@
 def swap(*names):
     target = np.flip(IDS, [NAMES.index(n) for n in names])
     return list(zip(IDS.reshape(-1).tolist(), target.reshape(-1).tolist()))
+
+
+def by_core(even, odd):
+    return [(a if d % 2 == 0 else b) for d, (a, b) in enumerate(zip(even, odd))]
 
 
 def groups_over(*names):
@@ -274,6 +278,7 @@
     )
     column_groups = groups_over("y", "x")
     swap_c, swap_p, swap_v, swap_uv = swap("c"), swap("p"), swap("v"), swap("u", "v")
+    swap_v, swap_uv = by_core(swap_v, swap_uv), by_core(swap_uv, swap_v)
 
     def shape(*dims, dtype=F32):
         return jax.ShapeDtypeStruct(dims, dtype)

time: 86.4 us -> 86.4 us (level)
  starting transfers between devices: 33.8 us -> 29.6 us
  waiting for transfers between devices: 8.66 us -> 12.8 us
    ppermute x1, starting transfers between devices: 3.91 us -> 6.94 us  [per_device(): by_v = permute(points, perm=swap_v)]
    ppermute x1, starting transfers between devices: 4.29 us -> 1.26 us  [per_device(): near_points = jnp.concatenate([pair, permute(pair, perm=swap_uv)], axis=1)]
    ppermute x1, starting transfers between devices: 2.23 us -> 0.01 us  [per_device(): other = permute(own, perm=swap_c)]
    all_to_all x1, waiting for transfers between devices: 2.66 us -> 4.41 us  [per_device(): own = exchange(copies, axis_index_groups=column_groups)]
    ppermute x1, waiting for transfers between devices: 1.13 us -> 2.61 us  [per_device(): near_points = jnp.concatenate([pair, permute(pair, perm=swap_uv)], axis=1)]
    ppermute x1, starting transfers between devices: 4.73 us -> 3.45 us  [per_device(): from_c = permute(other_part, perm=swap_c)]
    ppermute x1, starting transfers between devices: 1.76 us -> 0.67 us  [per_device(): next_image = permute(packed, perm=swap_p)]
where the time goes in v8:
time: 86.4 us; the launch traced here: 86 us
  starting transfers between devices  29.6 us (34%)
  blocking collectives  29.6 us (34%)
  Pallas kernels  13.3 us (15%)
  waiting for transfers between devices  12.8 us (15%)
    all_to_all x1, blocking collectives, per_device(): exchange(jnp.broadcast_to(dots[None], (128, 1, 128)), axis_index_groups=g...  18.6 us
    all_to_all x1, blocking collectives, per_device(): pieces = exchange(own_part + from_c, axis_index_groups=column_groups)  11 us
    ppermute x1, starting transfers between devices, per_device(): by_v = permute(points, perm=swap_v)  6.94 us
    all_to_all x1, starting transfers between devices, per_device(): own = exchange(copies, axis_index_groups=column_groups)  6.77 us
    ppermute x3, starting transfers between devices, per_device(): permute(total, perm=p)  5.74 us
    all_to_all x1, waiting for transfers between devices, per_device(): own = exchange(copies, axis_index_groups=column_groups)  4.41 us
    ppermute x3, waiting for transfers between devices, per_device(): permute(total, perm=p)  3.58 us
    ppermute x1, starting transfers between devices, per_device(): from_c = permute(other_part, perm=swap_c)  3.45 us
  transfers between devices with their start and end apart: 12, of which 8 were waited for; matrix products, arithmetic and copies ran while one was open for 0% of the time, Pallas kernels for 11%

profile of v8, /device:TPU:1, one launch (start us, length us, event | category | flops | bytes accessed | tf_op | source)
XLA Modules:
  0.0 86.0 jit_solution(8152353678797073570)
XLA Ops:
  0.6 6.9 %collective-permute-start = (f32[16,128]{1,0:T(8,128)}, f32[16,128]{1,0:T(8,128)S(1)}, u32[]{:S(2)}, u32[]{:S(2)}) collective-permute-start(f32[16,128]{1,0:T(8,128)} %points_hbm.1), channel_id=1, source_target_pairs={{0,16},{1,49},{2,18},{3,51},{4,20},{5,53},{6,22},{7,55},{8,24},{9,... | collective-permute-start | bytes 24584 | tf_op jit(solution)/shard_map/ppermute | solution.py:295
  7.6 1.5 %spread.1 = (f32[16,128]{1,0:T(8,128)S(1)}, f32[17,128]{1,0:T(8,128)S(1)}, f32[16,33,128]{2,1,0:T(8,128)}) custom-call(f32[16,128]{1,0:T(8,128)} %points_hbm.1, f32[17,128]{1,0:T(8,128)} %sides_hbm.1), custom_call_target="tpu_custom_call" | custom-call | tf_op jit(solution)/shard_map/spread/pallas_call | solution.py:296
  9.1 6.8 %all-to-all-start = ((f32[16,33,128]{2,1,0:T(8,128)}), f32[16,33,128]{2,1,0:T(8,128)S(1)}, u32[]{:S(2)}, u32[]{:S(2)}) async-start(f32[16,33,128]{2,1,0:T(8,128)} %get-tuple-element.32), calls=%async_computation | async-start | bytes 655360 | tf_op jit(solution)/shard_map/all_to_all | solution.py:308
  15.9 0.0 collective-permute-done
  15.9 1.3 %collective-permute-start.1 = (f32[16,256]{1,0:T(8,128)S(1)}, f32[16,256]{1,0:T(8,128)S(1)}, u32[]{:S(2)}, u32[]{:S(2)}) collective-permute-start(f32[16,256]{1,0:T(8,128)S(1)} %pad_maximum_fusion), channel_id=1, source_target_pairs={{0,48},{1,17},{2,50},{3,19},{4,52},{5,21},{6,54},{7,23},{8,56},{9,... | collective-permute-start | bytes 49160 | tf_op jit(solution)/shard_map/ppermute | solution.py:307
  17.1 2.6 %collective-permute-done.1 = f32[16,256]{1,0:T(8,128)S(1)} collective-permute-done((f32[16,256]{1,0:T(8,128)S(1)}, f32[16,256]{1,0:T(8,128)S(1)}, u32[]{:S(2)}, u32[]{:S(2)}) %collective-permute-start.1) | collective-permute-done | bytes 16416 | tf_op jit(solution)/shard_map/ppermute | solution.py:307
  19.8 4.4 %all-to-all-done.columns_ref = f32[16,33,128]{2,1,0:T(8,128)S(1)} async-done(((f32[16,33,128]{2,1,0:T(8,128)}), f32[16,33,128]{2,1,0:T(8,128)S(1)}, u32[]{:S(2)}, u32[]{:S(2)}) %all-to-all-start) | async-done | bytes 270368 | tf_op jit(solution)/shard_map/all_to_all | solution.py:308
  24.2 0.0 collective-permute-start.3
  24.2 2.0 %collective-permute-start.2 = (f32[16,512]{1,0:T(8,128)S(1)}, f32[16,512]{1,0:T(8,128)S(1)}, u32[]{:S(2)}, u32[]{:S(2)}) collective-permute-start(f32[16,512]{1,0:T(8,128)S(1)} %constant_dynamic-update-slice_fusion.points_ref), channel_id=1, source_target_pairs={{0,8},{1,9},{2,10},{3,11},{4,12},{5,13},{6,14},{7,15},{8,0},{9,1},... | collective-permute-start | bytes 98312 | tf_op jit(solution)/shard_map/ppermute | solution.py:309
  26.2 2.0 %near_own.1 = (bf16[512,2048]{1,0:T(8,128)(2,1)S(1)}, bf16[512,2048]{1,0:T(8,128)(2,1)S(1)}, f32[17,512]{1,0:T(8,128)S(1)}, bf16[512,128]{1,0:T(8,128)(2,1)S(1)}...) custom-call(f32[16,512]{1,0:T(8,128)S(1)} %constant_dynamic-update-slice_fusion.points_ref, ...), custom_call_target="tpu_custom_call" | custom-call | flops 805306368 | tf_op jit(solution)/shard_map/near_own/pallas_call | solution.py:313
  28.1 0.0 collective-permute-done.2.points_ref
  28.1 2.0 %next_own.1 = (bf16[512,2048]{1,0:T(8,128)(2,1)S(1)}, bf16[512,2048]{1,0:T(8,128)(2,1)S(1)}, f32[17,512]{1,0:T(8,128)S(1)}, bf16[512,128]{1,0:T(8,128)(2,1)S(1)}) custom-call(f32[16,512]{1,0:T(8,128)S(1)} %collective-permute-done.2.points_ref, bf16[128,2048]{1,0:T(8,128)(2,1)S(1)} %get-tuple-element.37.right_ref, ...), custom_call_target="tpu_custom_call" | custom-call | flops 805306368 | tf_op jit(solution)/shard_map/next_own/pallas_call | solution.py:317
  30.1 0.0 collective-permute-done.3.columns_ref
  30.1 1.9 %next_other.1 = (bf16[512,2048]{1,0:T(8,128)(2,1)S(1)}, bf16[512,2048]{1,0:T(8,128)(2,1)S(1)}, f32[68,128]{1,0:T(8,128)S(1)}, bf16[128,2048]{1,0:T(8,128)(2,1)S(1)}, bf16[96,2048]{1,0:T(8,128)(2,1)S(1)}) custom-call(bf16[512,128]{1,0:T(8,128)(2,1)S(1)} %get-tuple-element.39.left_ref, f32[16,33,128]{2,1,0:T(8,128)S(1)} %collective-permute-done.3.columns_ref, ...), custom_call_target="tpu_custom_call" | custom-call | flops 805306368 | tf_op jit(solution)/shard_map/next_other/pallas_call | solution.py:320
  32.0 0.9 collective-permute-start.4
  32.9 1.9 %near_other.1 = (bf16[512,2048]{1,0:T(8,128)(2,1)S(1)}, bf16[512,2048]{1,0:T(8,128)(2,1)S(1)}, f32[17,512]{1,0:T(8,128)S(1)}) custom-call(bf16[512,128]{1,0:T(8,128)(2,1)S(1)} %get-tuple-element.36.left_ref, bf16[128,2048]{1,0:T(8,128)(2,1)S(1)} %get-tuple-element.41.right_ref, bf16[96,2048]{1,0:T(8,128)(2,1)S(1)} %get-tuple-element.42.vectors_ref, ...), custom_call_target="tpu_custom_call" | custom-call | flops 805306368 | tf_op jit(solution)/shard_map/near_other/pallas_call | solution.py:324
  34.8 0.2 collective-permute-done.4.from_p_ref
  35.0 2.9 %collective-permute-start.7 = (f32[68,128]{1,0:T(8,128)S(1)}, f32[68,128]{1,0:T(8,128)S(1)}, u32[]{:S(2)}, u32[]{:S(2)}) collective-permute-start(f32[68,128]{1,0:T(8,128)S(1)} %stack.1.own_ref), channel_id=1, source_target_pairs={{0,32},{1,33},{2,34},{3,35},{4,36},{5,37},{6,38},{7,39},{8,40},{9,... | collective-permute-start | bytes 104456 | tf_op jit(solution)/shard_map/ppermute | solution.py:330
  37.8 1.2 %collective-permute-start.6 = (f32[68,128]{1,0:T(8,128)S(1)}, f32[68,128]{1,0:T(8,128)S(1)}, u32[]{:S(2)}, u32[]{:S(2)}) collective-permute-start(f32[68,128]{1,0:T(8,128)S(1)} %stack.1.own_ref), channel_id=1, source_target_pairs={{0,48},{1,17},{2,50},{3,19},{4,52},{5,21},{6,54},{7,23},{8,56},{9,... | collective-permute-start | bytes 104456 | tf_op jit(solution)/shard_map/ppermute | solution.py:330
  39.0 1.7 %collective-permute-start.5 = (f32[68,128]{1,0:T(8,128)S(1)}, f32[68,128]{1,0:T(8,128)S(1)}, u32[]{:S(2)}, u32[]{:S(2)}) collective-permute-start(f32[68,128]{1,0:T(8,128)S(1)} %stack.1.own_ref), channel_id=1, source_target_pairs={{0,16},{1,49},{2,18},{3,51},{4,20},{5,53},{6,22},{7,55},{8,24},{9,... | collective-permute-start | bytes 104456 | tf_op jit(solution)/shard_map/ppermute | solution.py:330
  40.7 1.1 %collective-permute-done.7.three_ref = f32[68,128]{1,0:T(8,128)S(1)} collective-permute-done((f32[68,128]{1,0:T(8,128)S(1)}, f32[68,128]{1,0:T(8,128)S(1)}, u32[]{:S(2)}, u32[]{:S(2)}) %collective-permute-start.7) | collective-permute-done | bytes 34848 | tf_op jit(solution)/shard_map/ppermute | solution.py:330
  41.8 0.0 collective-permute-done.6.two_ref
  41.8 2.5 %collective-permute-done.5.one_ref = f32[68,128]{1,0:T(8,128)S(1)} collective-permute-done((f32[68,128]{1,0:T(8,128)S(1)}, f32[68,128]{1,0:T(8,128)S(1)}, u32[]{:S(2)}, u32[]{:S(2)}) %collective-permute-start.5) | collective-permute-done | bytes 34848 | tf_op jit(solution)/shard_map/ppermute | solution.py:330
  44.3 0.7 collective-permute-start.8
  45.0 1.5 %near_transposed.1 = (f32[16,17,128]{2,1,0:T(8,128)S(1)}, f32[16,17,128]{2,1,0:T(8,128)S(1)}) custom-call(f32[17,512]{1,0:T(8,128)S(1)} %get-tuple-element.49.image_ref, bf16[512,2048]{1,0:T(8,128)(2,1)S(1)} %get-tuple-element.50.other_high_ref, bf16[512,2048]{1,0:T(8,128)(2,1)S(1)} %get-tuple-element.51.other_low_ref, ...), custom_call_target="tpu_custom_call" | custom-call | flops 1073741824 | tf_op jit(solution)/shard_map/near_transposed/pallas_call | solution.py:335
  46.4 1.0 %collective-permute-done.8.image_ref = f32[68,128]{1,0:T(8,128)S(1)} collective-permute-done((f32[68,128]{1,0:T(8,128)S(1)}, f32[68,128]{1,0:T(8,128)S(1)}, u32[]{:S(2)}, u32[]{:S(2)}) %collective-permute-start.8) | collective-permute-done | bytes 34848 | tf_op jit(solution)/shard_map/ppermute | solution.py:334
  47.4 0.8 other_transposed.1
  48.2 3.5 %collective-permute-start.9 = (f32[16,17,128]{2,1,0:T(8,128)S(1)}, f32[16,17,128]{2,1,0:T(8,128)S(1)}, u32[]{:S(2)}, u32[]{:S(2)}) collective-permute-start(f32[16,17,128]{2,1,0:T(8,128)S(1)} %other_transposed.1), channel_id=1, source_target_pairs={{0,1},{1,0},{2,3},{3,2},{4,5},{5,4},{6,7},{7,6},{8,9},{9,8},{10,11... | collective-permute-start | bytes 417800 | tf_op jit(solution)/shard_map/ppermute | solution.py:343
  51.6 0.8 own_transposed.1
  52.4 0.3 collective-permute-done.9
  52.7 11.0 %all_to_all.15.parts_ref = f32[16,17,128]{2,1,0:T(8,128)S(1)} all-to-all(f32[16,17,128]{2,1,0:T(8,128)S(1)} %add.6), channel_id=1, replica_groups={{0,2,4,6,64,66,68,70,128,130,132,134,192,194,196,198},{1,3,5,7,65,67,69..., dimensions={0} | all-to-all | bytes 278528 | tf_op jit(solution)/shard_map/all_to_all | solution.py:345
  63.7 0.1 dots.1
  63.8 1.9 %collective-permute-start.10 = (f32[1,128]{1,0:T(1,128)S(1)}, f32[1,128]{1,0:T(1,128)S(1)}, u32[]{:S(2)}, u32[]{:S(2)}) collective-permute-start(f32[1,128]{1,0:T(1,128)S(1)} %get-tuple-element.59), channel_id=1, source_target_pairs={{0,1},{1,0},{2,3},{3,2},{4,5},{5,4},{6,7},{7,6},{8,9},{9,8},{10,11... | collective-permute-start | bytes 1544 | tf_op jit(solution)/shard_map/ppermute | solution.py:351
  65.7 0.8 collective-permute-done.10
  66.5 18.6 %all_to_all.16.dots_ref = f32[128,1,128]{2,1,0:T(1,128)S(1)} all-to-all(f32[128,1,128]{2,1,0:T(1,128)S(1)} %broadcast_in_dim.9), channel_id=1, replica_groups={{0,2,4,6,8,10,12,14,16,18,20,22,24,26,28,30,32,34,36,38,40,42,44,46,48,..., dimensions={0} | all-to-all | bytes 131072 | tf_op jit(solution)/shard_map/all_to_all | solution.py:352
  85.2 0.8 finish.1
  (9 shorter events, 0.1 us)
Async XLA Ops:
  0.6 15.2 %collective-permute-start = (f32[16,128]{1,0:T(8,128)}, f32[16,128]{1,0:T(8,128)S(1)}, u32[]{:S(2)}, u32[]{:S(2)}) collective-permute-start(f32[16,128]{1,0:T(8,128)} %points_hbm.1), channel_id=1, source_target_pairs={{0,16},{1,49},{2,18},{3,51},{4,20},{5,53},{6,22},{7,55},{8,24},{9,... | collective-permute-start | bytes 24584 | tf_op jit(solution)/shard_map/ppermute | solution.py:295
  9.1 15.1 %all-to-all-start = ((f32[16,33,128]{2,1,0:T(8,128)}), f32[16,33,128]{2,1,0:T(8,128)S(1)}, u32[]{:S(2)}, u32[]{:S(2)}) async-start(f32[16,33,128]{2,1,0:T(8,128)} %get-tuple-element.32), calls=%async_computation | async-start | bytes 655360 | tf_op jit(solution)/shard_map/all_to_all | solution.py:308
  15.9 3.9 %collective-permute-start.1 = (f32[16,256]{1,0:T(8,128)S(1)}, f32[16,256]{1,0:T(8,128)S(1)}, u32[]{:S(2)}, u32[]{:S(2)}) collective-permute-start(f32[16,256]{1,0:T(8,128)S(1)} %pad_maximum_fusion), channel_id=1, source_target_pairs={{0,48},{1,17},{2,50},{3,19},{4,52},{5,21},{6,54},{7,23},{8,56},{9,... | collective-permute-start | bytes 49160 | tf_op jit(solution)/shard_map/ppermute | solution.py:307
  24.2 5.9 %collective-permute-start.3 = (f32[16,33,128]{2,1,0:T(8,128)S(1)}, f32[16,33,128]{2,1,0:T(8,128)S(1)}, u32[]{:S(2)}, u32[]{:S(2)}) collective-permute-start(f32[16,33,128]{2,1,0:T(8,128)S(1)} %all-to-all-done.columns_ref), channel_id=1, source_target_pairs={{0,1},{1,0},{2,3},{3,2},{4,5},{5,4},{6,7},{7,6},{8,9},{9,8},{10,11... | collective-permute-start | bytes 811016 | tf_op jit(solution)/shard_map/ppermute | solution.py:312
  24.2 4.0 %collective-permute-start.2 = (f32[16,512]{1,0:T(8,128)S(1)}, f32[16,512]{1,0:T(8,128)S(1)}, u32[]{:S(2)}, u32[]{:S(2)}) collective-permute-start(f32[16,512]{1,0:T(8,128)S(1)} %constant_dynamic-update-slice_fusion.points_ref), channel_id=1, source_target_pairs={{0,8},{1,9},{2,10},{3,11},{4,12},{5,13},{6,14},{7,15},{8,0},{9,1},... | collective-permute-start | bytes 98312 | tf_op jit(solution)/shard_map/ppermute | solution.py:309
  32.0 2.9 %collective-permute-start.4 = (f32[68,128]{1,0:T(8,128)S(1)}, f32[68,128]{1,0:T(8,128)S(1)}, u32[]{:S(2)}, u32[]{:S(2)}) collective-permute-start(f32[68,128]{1,0:T(8,128)S(1)} %get-tuple-element.45), channel_id=1, source_target_pairs={{0,8},{1,9},{2,10},{3,11},{4,12},{5,13},{6,14},{7,15},{8,0},{9,1},... | collective-permute-start | bytes 104456 | tf_op jit(solution)/shard_map/ppermute | solution.py:323
  35.0 6.8 %collective-permute-start.7 = (f32[68,128]{1,0:T(8,128)S(1)}, f32[68,128]{1,0:T(8,128)S(1)}, u32[]{:S(2)}, u32[]{:S(2)}) collective-permute-start(f32[68,128]{1,0:T(8,128)S(1)} %stack.1.own_ref), channel_id=1, source_target_pairs={{0,32},{1,33},{2,34},{3,35},{4,36},{5,37},{6,38},{7,39},{8,40},{9,... | collective-permute-start | bytes 104456 | tf_op jit(solution)/shard_map/ppermute | solution.py:330
  37.8 3.9 %collective-permute-start.6 = (f32[68,128]{1,0:T(8,128)S(1)}, f32[68,128]{1,0:T(8,128)S(1)}, u32[]{:S(2)}, u32[]{:S(2)}) collective-permute-start(f32[68,128]{1,0:T(8,128)S(1)} %stack.1.own_ref), channel_id=1, source_target_pairs={{0,48},{1,17},{2,50},{3,19},{4,52},{5,21},{6,54},{7,23},{8,56},{9,... | collective-permute-start | bytes 104456 | tf_op jit(solution)/shard_map/ppermute | solution.py:330
  39.0 5.3 %collective-permute-start.5 = (f32[68,128]{1,0:T(8,128)S(1)}, f32[68,128]{1,0:T(8,128)S(1)}, u32[]{:S(2)}, u32[]{:S(2)}) collective-permute-start(f32[68,128]{1,0:T(8,128)S(1)} %stack.1.own_ref), channel_id=1, source_target_pairs={{0,16},{1,49},{2,18},{3,51},{4,20},{5,53},{6,22},{7,55},{8,24},{9,... | collective-permute-start | bytes 104456 | tf_op jit(solution)/shard_map/ppermute | solution.py:330
  44.3 3.1 %collective-permute-start.8 = (f32[68,128]{1,0:T(8,128)S(1)}, f32[68,128]{1,0:T(8,128)S(1)}, u32[]{:S(2)}, u32[]{:S(2)}) collective-permute-start(f32[68,128]{1,0:T(8,128)S(1)} %get-tuple-element.46), channel_id=1, source_target_pairs={{0,8},{1,9},{2,10},{3,11},{4,12},{5,13},{6,14},{7,15},{8,0},{9,1},... | collective-permute-start | bytes 104456 | tf_op jit(solution)/shard_map/ppermute | solution.py:334
  48.2 4.5 %collective-permute-start.9 = (f32[16,17,128]{2,1,0:T(8,128)S(1)}, f32[16,17,128]{2,1,0:T(8,128)S(1)}, u32[]{:S(2)}, u32[]{:S(2)}) collective-permute-start(f32[16,17,128]{2,1,0:T(8,128)S(1)} %other_transposed.1), channel_id=1, source_target_pairs={{0,1},{1,0},{2,3},{3,2},{4,5},{5,4},{6,7},{7,6},{8,9},{9,8},{10,11... | collective-permute-start | bytes 417800 | tf_op jit(solution)/shard_map/ppermute | solution.py:343
  63.8 2.7 %collective-permute-start.10 = (f32[1,128]{1,0:T(1,128)S(1)}, f32[1,128]{1,0:T(1,128)S(1)}, u32[]{:S(2)}, u32[]{:S(2)}) collective-permute-start(f32[1,128]{1,0:T(1,128)S(1)} %get-tuple-element.59), channel_id=1, source_target_pairs={{0,1},{1,0},{2,3},{3,2},{4,5},{5,4},{6,7},{7,6},{8,9},{9,8},{10,11... | collective-permute-start | bytes 1544 | tf_op jit(solution)/shard_map/ppermute | solution.py:351
